TPU v7x, 32 devices: a whole 2x2x4 slice. The times are simulated.
32 devices in a mesh: batch: 8 (over z, y), temp: 4 (over x, core).
Axes of the slice: x: 2, y: 2, z: 4, core: 2. Of those that a mesh axis runs over, the one named last changes fastest.
Arguments:
- embeddings: bfloat16 [2, 1024, 1152], P(None, 'batch'), may hold values from -40 to 40
- spread_code: int32 [1024], replicated, may hold values from 0 to 3
- level_index: int32 [4], P('temp'), may hold values from 0 to 5
Outputs:
- grad_student: float32 [1024, 1152], P(('batch', 'temp'))
- row_loss: float32 [1024], P(('batch', 'temp'))
Inputs may be any that keep to these rules, and one draw needn't show every extreme that they name: `spread_code`: spread codes. `level_index`: temperature codes.
All inputs are finite; a program needn't handle non-finite values.
Results may differ from a plain program's by a relative error of at most 0.0075.
Values may be sent and summed in bfloat16 or wider, within the bound.
No kernel may reach another device: no remote copies, remote signals or barrier semaphores. Data moves between devices by JAX's collectives and lax.ppermute only.
A program may use at most 192 MiB of HBM per device.

v0:
```python
import jax
import jax.numpy as jnp
from jax import lax
from jax.sharding import PartitionSpec as P

WEIGHT = 16.0
NEG = -1e30


def widths(codes, level, width):
    return jnp.exp2(0.5 * (codes.astype(jnp.float32) - level.astype(jnp.float32))) / jnp.sqrt(
        jnp.float32(width)
    )


def logsum(row_beta, gram, self_pair):
    logits = jnp.where(self_pair, NEG, row_beta[:, None] * gram)
    top = jnp.max(logits, axis=1)
    return top + jnp.log(jnp.sum(jnp.exp(logits - top[:, None]), axis=1))


def mixing(row_beta, col_beta, row_lt, row_ls, col_lt, col_ls, gt, gs, self_pair):
    pr = jnp.exp(jnp.where(self_pair, NEG, row_beta[:, None] * gt) - row_lt[:, None])
    qr = jnp.exp(jnp.where(self_pair, NEG, row_beta[:, None] * gs) - row_ls[:, None])
    pc = jnp.exp(jnp.where(self_pair, NEG, col_beta[None, :] * gt) - col_lt[None, :])
    qc = jnp.exp(jnp.where(self_pair, NEG, col_beta[None, :] * gs) - col_ls[None, :])
    return (WEIGHT * (row_beta[:, None] * (qr - pr) + col_beta[None, :] * (qc - pc))).astype(
        jnp.bfloat16
    )


def shards(embeddings, spread_code, level_index):
    rows = embeddings.shape[1]
    width = embeddings.shape[2]
    total = rows * lax.axis_size("batch")
    first_row = lax.axis_index("batch") * rows
    own = first_row + jnp.arange(rows, dtype=jnp.int32)

    def self_mask(count):
        return own[:, None] == jnp.arange(count, dtype=jnp.int32)[None, :]

    students = embeddings[1]
    gram = jnp.einsum(
        "kad,kjd->kaj",
        embeddings,
        lax.all_gather(embeddings, "batch", axis=1, tiled=True),
        preferred_element_type=jnp.float32,
    )
    betas = [widths(spread_code, level_index[0], width)]
    local_betas = [lax.dynamic_slice_in_dim(betas[0], first_row, rows)]
    whole_mask = self_mask(total)
    sums = jnp.stack(
        [
            jnp.stack(
                [
                    logsum(local_betas[0], gram[0], whole_mask),
                    logsum(local_betas[0], gram[1], whole_mask),
                ]
            )
        ]
    )
    k = 0
    pr = jnp.exp(
        jnp.where(whole_mask, NEG, local_betas[k][:, None] * gram[0]) - sums[k, 0][:, None]
    )
    loss = (
        jnp.sum(pr * (local_betas[k][:, None] * (gram[0] - gram[1])), axis=1)
        - sums[k, 0]
        + sums[k, 1]
    )
    stats = lax.all_gather(sums, "batch", axis=2, tiled=True)
    piece = lax.all_gather(students, "batch", axis=0, tiled=True)
    k = 0
    gt = gram[0]
    gs = gram[1]
    col_beta = betas[k]
    col_lt = stats[k, 0]
    col_ls = stats[k, 1]
    carry = jnp.dot(
        mixing(
            local_betas[k],
            col_beta,
            sums[k, 0],
            sums[k, 1],
            col_lt,
            col_ls,
            gt,
            gs,
            self_mask(piece.shape[0]),
        ),
        piece,
        preferred_element_type=jnp.float32,
    )
    grad_part, loss_part = (
        lax.psum_scatter(carry, "temp", scatter_dimension=0, tiled=True),
        lax.psum_scatter(loss, "temp", scatter_dimension=0, tiled=True),
    )
    return (grad_part, loss_part)


def solution(mesh):
    in_specs = (P(None, "batch", None), P(), P("temp"))
    out_specs = (P(("batch", "temp"), None), P(("batch", "temp")))
    return jax.shard_map(shards, mesh=mesh, in_specs=in_specs, out_specs=out_specs, check_vma=False)
```

profile of v0, /device:TPU:0, one launch (start us, length us, event | category | flops | bytes accessed | tf_op | source)
XLA Modules:
  0.0 176.1 jit_solution(5987837914974862042)
XLA Ops:
  7.2 0.0 all-gather.5.cloned.1.call-start
  7.2 0.7 all-gather.5.cloned.1.call-update
  7.9 0.0 all-gather.7.cloned.1.call-start
  7.9 1.7 slice.35
  9.7 0.0 all-gather.7.cloned.1.call-update
  9.7 0.0 reduce-scatter.2.cloned.1.call-start
  10.4 0.7 exponential_multiply_fusion
  11.1 0.1 dynamic_slice.3
  11.2 81.6 %all-gather.5.cloned.1.call-done = bf16[2,1024,1152]{2,1,0:T(8,128)(2,1)} async-done(((bf16[2,128,1152]{2,1,0:T(8,128)(2,1)}), bf16[2,1024,1152]{2,1,0:T(8,128)(2,1)}) %all-gather.5.cloned.1.call-update) | async-done | bytes 4718608 | tf_op jit(solution)/shard_map/all_gather | solution.py:46
  92.8 4.1 %fusion.17 = f32[2,128,1024]{2,1,0:T(8,128)S(1)} fusion(bf16[2,128,1152]{2,1,0:T(8,128)(2,1)} %param.3, bf16[2,1024,1152]{2,1,0:T(8,128)(2,1)} %all-gather.5.cloned.1.call-done), kind=kOutput, calls=%fused_computation.35 | convolution fusion | flops 603979776 | bytes 6356992 | tf_op jit(solution)/shard_map/kad,kjd->kaj/dot_general | solution.py:43
  97.0 0.0 copy-start
  97.0 0.3 fusion.3
  97.3 0.4 exponential_reduce_fusion.1
  97.7 17.7 %all-gather = f32[2,1024]{1,0:T(2,128)S(1)} all-gather(f32[2,128]{1,0:T(2,128)S(1)} %get-tuple-element.11), channel_id=2, replica_groups=mesh['batch'=8,'temp'=4] {'batch'}, dimensions={1}, use_global_device_ids=true | all-gather | bytes 9216 | tf_op jit(solution)/shard_map/all_gather | solution.py:71
  115.4 29.9 %all-gather.7.cloned.1.call-done = bf16[1,1024,1152]{2,1,0:T(8,128)(2,1)} async-done(((bf16[1,128,1152]{2,1,0:T(8,128)(2,1)}), bf16[1,1024,1152]{2,1,0:T(8,128)(2,1)}) %all-gather.7.cloned.1.call-update) | async-done | bytes 2359312 | tf_op jit(solution)/shard_map/all_gather | solution.py:72
  145.3 3.4 %fusion = f32[128,1152]{1,0:T(8,128)} fusion(bf16[1,1024,1152]{2,1,0:T(8,128)(2,1)} %all-gather.7.cloned.1.call-done, f32[2,128,1024]{2,1,0:T(8,128)S(1)} %fusion.17, f32[1024]{0:T(1024)S(1)} %bitcast.48, f32[1024]{0:T(1024)S(1)} %bitcast.47, f32[1024]{0:T(1024)S(1)} %exponential_multiply_fusion, f32[128]{0:T(128)S(1)} %get-tuple-element.9, ...), kind=kOutput, calls=%fused_computation | convolution fusion | flops 304611328 | bytes 4012032 | tf_op jit(solution)/shard_map/dot_general | solution.py:79
  148.7 0.0 reduce-scatter.2.cloned.1.call-update
  148.8 0.0 copy-done
  148.8 0.6 dynamic-slice
  150.0 0.3 multiply_reduce_fusion
  150.4 5.7 %all-reduce = f32[128]{0:T(128)S(1)} all-reduce(f32[128]{0:T(128)S(1)} %subtract_add_fusion), channel_id=5, replica_groups=mesh['batch'=8,'temp'=4] {'temp'}, use_global_device_ids=true, to_apply=%region_6.7.clone | all-reduce | flops 128 | bytes 1024
  156.0 0.6 dynamic-slice.1
  156.6 12.9 %reduce-scatter.2.cloned.1.call-done = f32[32,1152]{1,0:T(8,128)} async-done(((f32[128,1152]{1,0:T(8,128)}), f32[32,1152]{1,0:T(8,128)}) %reduce-scatter.2.cloned.1.call-update) | async-done | bytes 147472 | tf_op jit(solution)/shard_map/reduce_scatter | solution.py:95
  (6 shorter events, 0.0 us)
Async XLA Ops:
  7.2 85.6 %all-gather.5.cloned.1.call-start = ((), (), s32[]{:S(2)}) async-start(), calls=%async_computation.1 | async-start | bytes 5308416 | tf_op jit(solution)/shard_map/all_gather | solution.py:46
  7.9 137.4 %all-gather.7.cloned.1.call-start = ((), (), s32[]{:S(2)}) async-start(), calls=%async_computation.3 | async-start | bytes 2654208 | tf_op jit(solution)/shard_map/all_gather | solution.py:72
  9.7 159.8 %reduce-scatter.2.cloned.1.call-start = ((), (), s32[]{:S(2)}) async-start(), calls=%async_computation.2 | async-start | bytes 737280 | tf_op jit(solution)/shard_map/reduce_scatter | solution.py:95
  97.0 51.8 %copy-start = (u32[32]{0:T(128)S(1)}, u32[32]{0:T(128)}, u32[]{:S(2)}) copy-start(u32[32]{0:T(128)} %constant.30) | copy-start | bytes 388
Sparse Core Ops, SparseCore 0:
  10.2 82.5 all-gather.4
  95.0 50.2 all-gather.6
  148.9 20.6 reduce-scatter.1
where the time goes:
time: 176 us
  waiting for transfers between devices  125 us (71%)
  blocking collectives  23.4 us (13%)
  between operations  15.1 us (9%)
  matrix products  7.56 us (4%)
  local copies, waits for them, and re-layouts  2.99 us (2%)
    all_gather x1, waiting for transfers between devices, shards(): lax.all_gather(embeddings, 'batch', axis=1, tiled=True)  81.6 us
    all_gather x1, waiting for transfers between devices, shards(): piece = lax.all_gather(students, 'batch', axis=0, tiled=True)  29.9 us
    all_gather x1, blocking collectives, shards(): stats = lax.all_gather(sums, 'batch', axis=2, tiled=True)  17.7 us
    reduce_scatter x1, waiting for transfers between devices, shards(): lax.psum_scatter(carry, 'temp', scatter_dimension=0, tiled=True)  12.9 us
    unnamed x1, blocking collectives  5.67 us
    dot_general x1, matrix products, shards(): jnp.einsum('kad,kjd->kaj', embeddings, lax.all_gather(embeddings, 'batch'...  4.15 us
  transfers between devices with their start and end apart: 3, of which 3 were waited for; matrix products, arithmetic and copies ran while one was open for 5% of the time, Pallas kernels for 0%

commit v1 on v0

v1 whole, which is shorter than its diff:
```python
import functools

import jax
import jax.numpy as jnp
from jax import lax
from jax.experimental import pallas as pl
from jax.experimental.pallas import tpu as pltpu
from jax.sharding import PartitionSpec as P

WEIGHT = 16.0
NEG = -1e30
LOG2E = 1.4426950408889634
TILE = 256
CHUNK = 128
SPAN = 1024
ALL = ("batch", "temp")


def loop(count, body):
    if count <= 8:
        for i in range(count):
            body(i)
    else:
        lax.fori_loop(0, count, lambda i, c: (body(i), c)[1], 0)


def at(i, size):
    return pl.ds(i * size if isinstance(i, int) else pl.multiple_of(i * size, size), size)


def column_betas(codes, level, width):
    return jnp.exp2(0.5 * (codes.astype(jnp.float32) - level.astype(jnp.float32))) / jnp.sqrt(
        jnp.float32(width)
    )


def stats_kernel(count, rows, scalars, codes, *refs):
    pieces, refs = refs[:count], refs[count:]
    if count == 1:
        whole, (stats, strip, gram) = pieces[0], refs
    else:
        stats, strip, whole, gram = refs
        for p, piece in enumerate(pieces):
            start = pl.multiple_of(scalars[2 + p], 64)
            whole[pl.ds(start, piece.shape[0]), :] = piece[...]
    levels = scalars.shape[0] - 2 - count
    total, width = whole.shape

    def tile(j):
        cols = at(j, TILE)
        gram[...] = lax.dot_general(
            whole[...], whole[cols, :], (((1,), (1,)), ((), ())), preferred_element_type=jnp.float32
        )
        square = gram[cols, :]
        own = lax.broadcasted_iota(jnp.int32, square.shape, 0) == lax.broadcasted_iota(
            jnp.int32, square.shape, 1
        )
        gram[cols, :] = jnp.where(own, NEG, square)
        strip[:, cols] = gram[pl.ds(pl.multiple_of(scalars[0], rows), rows), :]
        code = codes[:, cols]
        scale = [
            column_betas(code, scalars[2 + count + k], width) * LOG2E for k in range(levels)
        ]
        steps = total // CHUNK

        def top(i, best):
            return jnp.maximum(best, jnp.max(gram[at(i, CHUNK), :], axis=0, keepdims=True))

        best = jnp.full((1, TILE), NEG, jnp.float32)
        if steps <= 8:
            for i in range(steps):
                best = top(i, best)
        else:
            best = lax.fori_loop(0, steps, top, best)

        def add(i, sums):
            d = gram[at(i, CHUNK), :] - best
            return tuple(
                s + jnp.sum(jnp.exp2(d * b), axis=0, keepdims=True) for s, b in zip(sums, scale)
            )

        sums = tuple(jnp.zeros((1, TILE), jnp.float32) for _ in range(levels))
        if steps <= 8:
            for i in range(steps):
                sums = add(i, sums)
        else:
            sums = lax.fori_loop(0, steps, add, sums)
        stats[0:1, cols] = best
        for k in range(levels):
            stats[1 + k : 2 + k, cols] = sums[k]
        stats[levels + 1 : levels + 2, cols] = code.astype(jnp.float32)
        if levels + 2 < stats.shape[0]:
            stats[levels + 2 :, cols] = jnp.zeros((stats.shape[0] - levels - 2, TILE), jnp.float32)

    loop(total // TILE, tile)


def mix_kernel(rows, block, scalars, s_stats, s_strip, t_stats, t_strip, student, out, turned):
    levels = scalars.shape[0] - 2
    total, width = student.shape
    half = rows // 2
    own = pl.ds(pl.multiple_of(scalars[1], block), block)
    turned[0] = s_stats[:, own].T
    turned[1] = t_stats[:, own].T
    mine = pl.ds(pl.multiple_of(scalars[0] - scalars[1], rows), rows)
    s_row, t_row = turned[0, mine, :], turned[1, mine, :]
    root = jnp.sqrt(jnp.float32(width))

    def beta(code, k):
        return jnp.exp2(0.5 * (code - scalars[2 + k].astype(jnp.float32))) / root

    row_beta = [beta(s_row[:, levels + 1 : levels + 2], k) for k in range(levels)]
    span = min(SPAN, total)
    loss = jnp.zeros((rows, 1), jnp.float32)
    grad = jnp.zeros((rows, width), jnp.float32)

    def piece(i, carry):
        loss, grad = carry
        cols = at(i, span)
        gs, gt = s_strip[:, cols], t_strip[:, cols]
        code = s_stats[levels + 1 : levels + 2, cols]
        s_from_row, t_from_row = gs - s_row[:, 0:1], gt - t_row[:, 0:1]
        s_from_col, t_from_col = gs - s_stats[0:1, cols], gt - t_stats[0:1, cols]
        gap = gt - gs
        mix = None
        for k in range(levels):
            a = row_beta[k]
            b = beta(code, k)
            a2, b2 = a * LOG2E, b * LOG2E
            pr = jnp.exp2(t_from_row * a2) * (a / t_row[:, 1 + k : 2 + k])
            qr = jnp.exp2(s_from_row * a2) * (a / s_row[:, 1 + k : 2 + k])
            pc = jnp.exp2(t_from_col * b2) * (b / t_stats[1 + k : 2 + k, cols])
            qc = jnp.exp2(s_from_col * b2) * (b / s_stats[1 + k : 2 + k, cols])
            loss = loss + jnp.sum(pr * gap, axis=1, keepdims=True)
            term = (qr - pr) + (qc - pc)
            mix = term if mix is None else mix + term
        grad = grad + jnp.dot(
            (WEIGHT * mix).astype(jnp.bfloat16),
            student[cols, :],
            preferred_element_type=jnp.float32,
        )
        return loss, grad

    if total == span:
        loss, grad = piece(0, (loss, grad))
    else:
        loss, grad = lax.fori_loop(0, total // span, piece, (loss, grad))
    for k in range(levels):
        loss = loss + (
            row_beta[k] * (s_row[:, 0:1] - t_row[:, 0:1])
            + jnp.log(s_row[:, 1 + k : 2 + k])
            - jnp.log(t_row[:, 1 + k : 2 + k])
        )
    line = jnp.broadcast_to(loss, (rows, 128)).T
    for h in range(2):
        out[h, 0:half, :] = grad[h * half : (h + 1) * half]
        out[h, half : half + 8, 0:half] = line[0:8, h * half : (h + 1) * half]


def gather(mesh, u):
    rows = u.shape[0]
    count, parts = mesh.shape["batch"], mesh.shape["temp"]
    me = lax.axis_index("batch")
    if count != 8 or parts != 4:
        return [(lax.all_gather(u, "batch", axis=0, tiled=True), 0 * me)]

    def send(a, to):
        pairs = []
        for b in range(count):
            for t in range(parts):
                z, y, x, c = b // 2, b % 2, t // 2, t % 2
                z, y, x, c = to(z, y, x, c)
                pairs.append((b * parts + t, (z * 2 + y) * parts + x * 2 + c))
        return lax.ppermute(a, ALL, pairs)

    far = lambda z, y, x, c: (z ^ (2 + x), y, x, c)
    near = lambda z, y, x, c: (z ^ 1, y, x, c)
    over_y = lambda z, y, x, c: (z, 1 - y, x, c)
    over_x = lambda z, y, x, c: (z, y, 1 - x, c)
    x = lax.axis_index("temp") // 2
    mine, other = 4 + 2 * x, 6 - 2 * x
    half = rows // 2
    a = send(u, far)
    n = send(u, near)
    y = send(u, over_y)
    ny = send(n, over_y)
    ay = send(a, over_y)
    ax = send(a, over_x)
    d1 = send(ay[:half], over_x)
    d2 = send(ax[half:], over_y)
    return [
        (u, me * rows),
        (n, (me ^ 2) * rows),
        (y, (me ^ 1) * rows),
        (ny, (me ^ 3) * rows),
        (a, (me ^ mine) * rows),
        (ay, (me ^ mine ^ 1) * rows),
        (ax, (me ^ other) * rows),
        (d1, (me ^ other ^ 1) * rows),
        (d2, (me ^ other ^ 1) * rows + half),
    ]


def shards(mesh, embeddings, spread_code, level_index):
    block, width = embeddings.shape[1:]
    parts = mesh.shape["temp"]
    total = block * mesh.shape["batch"]
    me, part = lax.axis_index("batch"), lax.axis_index("temp")
    core = part % 2
    rows = 2 * block // parts

    swap = [(t, t ^ 1) for t in range(parts)]
    theirs = lax.ppermute(level_index, "temp", swap)
    level = jnp.where(
        core == 0,
        jnp.concatenate([level_index, theirs]),
        jnp.concatenate([theirs, level_index]),
    )
    others = [
        lax.ppermute(level, "temp", [(t, (t + 2 * d) % parts) for t in range(parts)])
        for d in range(1, parts // 2)
    ]
    level = jnp.concatenate([level] + others)

    u = lax.dynamic_index_in_dim(embeddings, core, 0, keepdims=False)
    pieces = gather(mesh, u)
    first = me * block + part // 2 * rows
    places = [first, me * block]
    scalars = jnp.concatenate(
        [jnp.stack(places + [s for _, s in pieces]).astype(jnp.int32), level]
    )
    codes = spread_code[None, :]
    high = 8 * pl.cdiv(parts + 2, 8)
    limit = (24 << 20) if total <= 1024 else (56 << 20)
    params = pltpu.CompilerParams(vmem_limit_bytes=limit)
    smem, vmem = pl.BlockSpec(memory_space=pltpu.SMEM), pl.BlockSpec(memory_space=pltpu.VMEM)

    shapes = [
        jax.ShapeDtypeStruct((high, total), jnp.float32),
        jax.ShapeDtypeStruct((rows, total), jnp.float32),
    ]
    if len(pieces) > 1:
        shapes.append(jax.ShapeDtypeStruct((total, width), jnp.bfloat16))
    stats, strip, *whole = pl.pallas_call(
        functools.partial(stats_kernel, len(pieces), rows),
        out_shape=shapes,
        in_specs=[smem, vmem] + [vmem] * len(pieces),
        out_specs=[vmem] * len(shapes),
        scratch_shapes=[pltpu.VMEM((total, TILE), jnp.float32)],
        compiler_params=params,
    )(scalars, codes, *[a for a, _ in pieces])

    t_stats = lax.ppermute(stats, "temp", swap)
    t_strip = lax.ppermute(strip, "temp", swap)
    half = rows // 2
    out = pl.pallas_call(
        functools.partial(mix_kernel, rows, block),
        out_shape=jax.ShapeDtypeStruct((2, half + 8, width), jnp.float32),
        in_specs=[smem] + [vmem] * 5,
        out_specs=vmem,
        scratch_shapes=[pltpu.VMEM((2, block, high), jnp.float32)],
        compiler_params=params,
    )(
        jnp.concatenate([jnp.stack(places).astype(jnp.int32), level]),
        stats,
        strip,
        t_stats,
        t_strip,
        whole[0] if whole else pieces[0][0],
    )
    back = lax.ppermute(out[0], "temp", [(t + 1, t) for t in range(0, parts, 2)])
    mine = jnp.where(core == 0, back, out[1])
    return mine[:half], mine[half, :half]


def solution(mesh):
    in_specs = (P(None, "batch", None), P(), P("temp"))
    out_specs = (P(("batch", "temp"), None), P(("batch", "temp")))
    return jax.shard_map(
        functools.partial(shards, mesh),
        mesh=mesh,
        in_specs=in_specs,
        out_specs=out_specs,
        check_vma=False,
    )
```

time: 176 us -> 58.3 us (0.33)
  waiting for transfers between devices: 125 us -> 30.2 us
  blocking collectives: 23.4 us -> 0 us
  starting transfers between devices: 0.12 us -> 14.7 us
  between operations: 15.1 us -> 1.39 us
  Pallas kernels: 0 us -> 7.95 us
  matrix products: 7.56 us -> 0 us
    all_gather x2 -> x0, waiting for transfers between devices: 112 us -> none  [the longest x1 81.6 us: shards(): lax.all_gather(embeddings, 'batch', axis=1, tiled=True)]
    ppermute x0 -> x13, waiting for transfers between devices: none -> 30.2 us  [the longest x8 23.1 us: send(): return lax.ppermute(a, ALL, pairs)]
    all_gather x1 -> x0, blocking collectives: 17.7 us -> none  [shards(): stats = lax.all_gather(sums, 'batch', axis=2, tiled=True)]
    ppermute x0 -> x13, starting transfers between devices: none -> 14.7 us  [the longest x8 12.7 us: send(): return lax.ppermute(a, ALL, pairs)]
    reduce_scatter x1 -> x0, waiting for transfers between devices: 12.9 us -> none  [shards(): lax.psum_scatter(carry, 'temp', scatter_dimension=0, tiled=True)]
    pallas_call x0 -> x2, Pallas kernels: none -> 7.95 us  [the longest x1 5.95 us: shards(): pl.pallas_call(functools.partial(stats_kernel, len(pieces), rows), out_sh...]
    dot_general x2 -> x0, matrix products: 7.56 us -> none  [the longest x1 4.15 us: shards(): jnp.einsum('kad,kjd->kaj', embeddings, lax.all_gather(embeddings, 'batch'...]
    unnamed x1 -> x0, blocking collectives: 5.67 us -> none
  transfers between devices with their start and end apart: 3 -> 13, of which waited for: 3 -> 9; matrix products, arithmetic and copies ran while one was open for 5% -> 2% of each run, Pallas kernels for 0% -> 0%
where the time goes in v1:
time: 58.3 us; the launch traced here: 58.1 us
  waiting for transfers between devices  30.2 us (52%)
  starting transfers between devices  14.7 us (25%)
  Pallas kernels  7.95 us (14%)
  local copies, waits for them, and re-layouts  3.06 us (5%)
  between operations  1.39 us (2%)
  other arithmetic  0.8 us (1%)
    ppermute x8, waiting for transfers between devices, send(): return lax.ppermute(a, ALL, pairs)  23.1 us
    ppermute x8, starting transfers between devices, send(): return lax.ppermute(a, ALL, pairs)  12.7 us
    pallas_call x1, Pallas kernels, shards(): pl.pallas_call(functools.partial(stats_kernel, len(pieces), rows), out_sh...  5.95 us
    ppermute x1, waiting for transfers between devices, shards(): lax.ppermute(level, 'temp', [(t, (t + 2 * d) % parts) for t in range(part...  3.46 us
    ppermute x1, waiting for transfers between devices, shards(): lax.ppermute(out[0], 'temp', [(t + 1, t) for t in range(0, parts, 2)])  2.02 us
    pallas_call x1, Pallas kernels, shards(): pl.pallas_call(functools.partial(mix_kernel, rows, block), out_shape=jax....  1.99 us
    unnamed x4, local copies, waits for them, and re-layouts  1.73 us
    ppermute x1, starting transfers between devices, shards(): lax.ppermute(out[0], 'temp', [(t + 1, t) for t in range(0, parts, 2)])  1.29 us
  transfers between devices with their start and end apart: 13, of which 9 were waited for; matrix products, arithmetic and copies ran while one was open for 2% of the time, Pallas kernels for 0%

profile of v1, /device:TPU:0, one launch (start us, length us, event | category | flops | bytes accessed | tf_op | source)
XLA Modules:
  0.0 58.1 jit_solution(9803630212080968206)
XLA Ops:
  0.6 0.0 copy-start
  0.7 1.0 %copy-done = bf16[2,128,1152]{2,1,0:T(8,128)(2,1)S(1)} copy-done((bf16[2,128,1152]{2,1,0:T(8,128)(2,1)S(1)}, bf16[2,128,1152]{2,1,0:T(8,128)(2,1)}, u32[]{:S(2)}) %copy-start) | copy-done | bytes 589848
  1.7 4.1 %collective-permute-start.5 = (bf16[128,1152]{1,0:T(8,128)(2,1)S(1)}, bf16[128,1152]{1,0:T(8,128)(2,1)S(1)}, u32[]{:S(2)}, u32[]{:S(2)}) collective-permute-start(bf16[128,1152]{1,0:T(8,128)(2,1)S(1)} %dynamic-slice_bitcast_fusion.refs_0_), channel_id=1, source_target_pairs={{0,16},{1,17},{2,26},{3,27},{4,20},{5,21},{6,30},{7,31},{8,24},{9,... | collective-permute-start | bytes 884744 | tf_op jit(solution)/shard_map/ppermute | solution.py:174
  5.8 1.6 %collective-permute-start.2 = (bf16[128,1152]{1,0:T(8,128)(2,1)S(1)}, bf16[128,1152]{1,0:T(8,128)(2,1)S(1)}, u32[]{:S(2)}, u32[]{:S(2)}) collective-permute-start(bf16[128,1152]{1,0:T(8,128)(2,1)S(1)} %dynamic-slice_bitcast_fusion.refs_0_), channel_id=1, source_target_pairs={{0,8},{1,9},{2,10},{3,11},{4,12},{5,13},{6,14},{7,15},{8,0},{9,1},... | collective-permute-start | bytes 884744 | tf_op jit(solution)/shard_map/ppermute | solution.py:174
  7.4 11.9 %collective-permute-done.5.refs_4_ = bf16[128,1152]{1,0:T(8,128)(2,1)S(1)} collective-permute-done((bf16[128,1152]{1,0:T(8,128)(2,1)S(1)}, bf16[128,1152]{1,0:T(8,128)(2,1)S(1)}, u32[]{:S(2)}, u32[]{:S(2)}) %collective-permute-start.5) | collective-permute-done | bytes 294944 | tf_op jit(solution)/shard_map/ppermute | solution.py:174
  19.3 0.0 collective-permute-start.7
  19.3 1.6 %collective-permute-start.6 = (bf16[128,1152]{1,0:T(8,128)(2,1)S(1)}, bf16[128,1152]{1,0:T(8,128)(2,1)S(1)}, u32[]{:S(2)}, u32[]{:S(2)}) collective-permute-start(bf16[128,1152]{1,0:T(8,128)(2,1)S(1)} %collective-permute-done.5.refs_4_), channel_id=1, source_target_pairs={{0,4},{1,5},{2,6},{3,7},{4,0},{5,1},{6,2},{7,3},{8,12},{9,13},{10,... | collective-permute-start | bytes 884744 | tf_op jit(solution)/shard_map/ppermute | solution.py:174
  20.9 0.4 collective-permute-start.3
  21.3 0.0 collective-permute-done.2.refs_1_
  21.3 1.6 %collective-permute-start.4 = (bf16[128,1152]{1,0:T(8,128)(2,1)S(1)}, bf16[128,1152]{1,0:T(8,128)(2,1)S(1)}, u32[]{:S(2)}, u32[]{:S(2)}) collective-permute-start(bf16[128,1152]{1,0:T(8,128)(2,1)S(1)} %collective-permute-done.2.refs_1_), channel_id=1, source_target_pairs={{0,4},{1,5},{2,6},{3,7},{4,0},{5,1},{6,2},{7,3},{8,12},{9,13},{10,... | collective-permute-start | bytes 884744 | tf_op jit(solution)/shard_map/ppermute | solution.py:174
  22.9 4.5 %collective-permute-done.7.refs_6_ = bf16[128,1152]{1,0:T(8,128)(2,1)S(1)} collective-permute-done((bf16[128,1152]{1,0:T(8,128)(2,1)S(1)}, bf16[128,1152]{1,0:T(8,128)(2,1)S(1)}, u32[]{:S(2)}, u32[]{:S(2)}) %collective-permute-start.7) | collective-permute-done | bytes 294944 | tf_op jit(solution)/shard_map/ppermute | solution.py:174
  27.4 1.3 %collective-permute-start.9 = (bf16[64,1152]{1,0:T(8,128)(2,1)S(1)}, bf16[64,1152]{1,0:T(8,128)(2,1)S(1)}, u32[]{:S(2)}, u32[]{:S(2)}) collective-permute-start(bf16[64,1152]{1,0:T(8,128)(2,1)S(1)} %slice.25), channel_id=1, source_target_pairs={{0,4},{1,5},{2,6},{3,7},{4,0},{5,1},{6,2},{7,3},{8,12},{9,13},{10,... | collective-permute-start | bytes 442376 | tf_op jit(solution)/shard_map/ppermute | solution.py:174
  28.7 0.5 collective-permute-done.6.refs_5_
  29.2 2.1 %collective-permute-start.8 = (bf16[64,1152]{1,0:T(8,128)(2,1)S(1)}, bf16[64,1152]{1,0:T(8,128)(2,1)S(1)}, u32[]{:S(2)}, u32[]{:S(2)}) collective-permute-start(bf16[64,1152]{1,0:T(8,128)(2,1)S(1)} %slice.24), channel_id=1, source_target_pairs={{0,2},{1,3},{2,0},{3,1},{4,6},{5,7},{6,4},{7,5},{8,10},{9,11},{10,... | collective-permute-start | bytes 442376 | tf_op jit(solution)/shard_map/ppermute | solution.py:174
  31.3 0.0 collective-permute-start
  32.0 0.6 collective-permute-done
  32.6 0.7 %broadcast_select_fusion = s32[2]{0:T(128)S(1)} fusion(pred[]{:T(512)S(6)} %eq.6, s32[1]{0:T(128)} %collective-permute-done, s32[1]{0:T(128)S(6)} %copy.5), kind=kLoop, calls=%fused_computation.4 | loop fusion | flops 6 | bytes 17 | tf_op jit(solution)/shard_map/jit(_where)/select_n | solution.py:214
  33.2 0.1 collective-permute-start.1
  33.3 3.5 %collective-permute-done.1 = s32[2]{0:T(128)S(1)} collective-permute-done((s32[2]{0:T(128)S(1)}, s32[2]{0:T(128)S(1)}, u32[]{:S(2)}, u32[]{:S(2)}) %collective-permute-start.1) | collective-permute-done | bytes 40 | tf_op jit(solution)/shard_map/ppermute | solution.py:220
  36.8 0.1 concatenate.18.scalars
  36.9 0.0 collective-permute-done.3.refs_2_
  36.9 4.7 %collective-permute-done.4.refs_3_ = bf16[128,1152]{1,0:T(8,128)(2,1)S(1)} collective-permute-done((bf16[128,1152]{1,0:T(8,128)(2,1)S(1)}, bf16[128,1152]{1,0:T(8,128)(2,1)S(1)}, u32[]{:S(2)}, u32[]{:S(2)}) %collective-permute-start.4) | collective-permute-done | bytes 294944 | tf_op jit(solution)/shard_map/ppermute | solution.py:174
  41.6 1.6 %collective-permute-done.9.refs_8_ = bf16[64,1152]{1,0:T(8,128)(2,1)S(1)} collective-permute-done((bf16[64,1152]{1,0:T(8,128)(2,1)S(1)}, bf16[64,1152]{1,0:T(8,128)(2,1)S(1)}, u32[]{:S(2)}, u32[]{:S(2)}) %collective-permute-start.9) | collective-permute-done | bytes 147488 | tf_op jit(solution)/shard_map/ppermute | solution.py:174
  43.2 0.0 collective-permute-done.8.refs_7_
  43.2 0.0 copy-start.1
  43.2 0.7 %copy-done.1 = s32[1024]{0:T(1024)S(1)} copy-done((s32[1024]{0:T(1024)S(1)}, s32[1024]{0:T(1024)}, u32[]{:S(2)}) %copy-start.1) | copy-done | bytes 4120
  43.9 6.0 %shard_map.50 = (f32[8,1024]{1,0:T(8,128)S(1)}, f32[64,1024]{1,0:T(8,128)S(1)}, bf16[1024,1152]{1,0:T(8,128)(2,1)S(1)}) custom-call(s32[15]{0:T(128)S(1)} %concatenate.18.scalars, s32[1,1024]{1,0:T(1,128)S(1)} %bitcast.21, bf16[128,1152]{1,0:T(8,128)(2,1)S(1)} %dynamic-slice_bitcast_fusion.refs_0_, bf16[128,1152]{1,0:T(8,128)(2,1)S(1)} %collective-permute-done.2.refs_1_, ...), custom_call_target="tpu_custom_call" | custom-call | tf_op jit(solution)/shard_map/pallas_call | solution.py:244
  49.9 0.1 collective-permute-start.11
  49.9 0.5 collective-permute-start.10
  50.4 0.1 pad_add_fusion.scalars
  50.5 1.0 %collective-permute-done.10.t_stats = f32[8,1024]{1,0:T(8,128)S(1)} collective-permute-done((f32[8,1024]{1,0:T(8,128)S(1)}, f32[8,1024]{1,0:T(8,128)S(1)}, u32[]{:S(2)}, u32[]{:S(2)}) %collective-permute-start.10) | collective-permute-done | bytes 32800 | tf_op jit(solution)/shard_map/ppermute | solution.py:253
  51.5 0.0 collective-permute-done.11.t_strip
  51.5 2.0 %shard_map.51 = f32[2,40,1152]{2,1,0:T(8,128)S(1)} custom-call(s32[6]{0:T(128)S(1)} %pad_add_fusion.scalars, f32[8,1024]{1,0:T(8,128)S(1)} %get-tuple-element.5.s_stats, f32[64,1024]{1,0:T(8,128)S(1)} %get-tuple-element.6.s_strip, f32[8,1024]{1,0:T(8,128)S(1)} %collective-permute-done.10.t_stats, f32[64,1024]{1,0:T(8,128)S(1)} %collective-permute-done.11.t_strip, ...), custom_call_target="tpu_custom_call" | custom-call | tf_op jit(solution)/shard_map/pallas_call | solution.py:256
  53.5 1.3 %collective-permute-start.12 = (f32[40,1152]{1,0:T(8,128)S(1)}, f32[40,1152]{1,0:T(8,128)S(1)}, u32[]{:S(2)}, u32[]{:S(2)}) collective-permute-start(f32[40,1152]{1,0:T(8,128)S(1)} %slice_bitcast_fusion.1), channel_id=1, source_target_pairs={{1,0},{3,2},{5,4},{7,6},{9,8},{11,10},{13,12},{15,14},{17,16},{19,... | collective-permute-start | bytes 552968 | tf_op jit(solution)/shard_map/ppermute | solution.py:271
  54.8 2.0 %collective-permute-done.12 = f32[40,1152]{1,0:T(8,128)S(1)} collective-permute-done((f32[40,1152]{1,0:T(8,128)S(1)}, f32[40,1152]{1,0:T(8,128)S(1)}, u32[]{:S(2)}, u32[]{:S(2)}) %collective-permute-start.12) | collective-permute-done | bytes 184352 | tf_op jit(solution)/shard_map/ppermute | solution.py:271
  56.9 0.5 slice_bitcast_fusion.2
  57.4 0.7 %slice.28 = f32[32,1152]{1,0:T(8,128)} slice(f32[40,1152]{1,0:T(8,128)S(1)} %fusion), slice={[0:32], [0:1152]} | slice | bytes 294912 | tf_op jit(solution)/shard_map/slice | solution.py:273
  (5 shorter events, 0.1 us)
Async XLA Ops:
  0.6 1.1 %copy-start = (bf16[2,128,1152]{2,1,0:T(8,128)(2,1)S(1)}, bf16[2,128,1152]{2,1,0:T(8,128)(2,1)}, u32[]{:S(2)}) copy-start(bf16[2,128,1152]{2,1,0:T(8,128)(2,1)} %param.3) | copy-start | bytes 1769476
  1.7 17.5 %collective-permute-start.5 = (bf16[128,1152]{1,0:T(8,128)(2,1)S(1)}, bf16[128,1152]{1,0:T(8,128)(2,1)S(1)}, u32[]{:S(2)}, u32[]{:S(2)}) collective-permute-start(bf16[128,1152]{1,0:T(8,128)(2,1)S(1)} %dynamic-slice_bitcast_fusion.refs_0_), channel_id=1, source_target_pairs={{0,16},{1,17},{2,26},{3,27},{4,20},{5,21},{6,30},{7,31},{8,24},{9,... | collective-permute-start | bytes 884744 | tf_op jit(solution)/shard_map/ppermute | solution.py:174
  5.8 15.5 %collective-permute-start.2 = (bf16[128,1152]{1,0:T(8,128)(2,1)S(1)}, bf16[128,1152]{1,0:T(8,128)(2,1)S(1)}, u32[]{:S(2)}, u32[]{:S(2)}) collective-permute-start(bf16[128,1152]{1,0:T(8,128)(2,1)S(1)} %dynamic-slice_bitcast_fusion.refs_0_), channel_id=1, source_target_pairs={{0,8},{1,9},{2,10},{3,11},{4,12},{5,13},{6,14},{7,15},{8,0},{9,1},... | collective-permute-start | bytes 884744 | tf_op jit(solution)/shard_map/ppermute | solution.py:174
  19.3 8.1 %collective-permute-start.7 = (bf16[128,1152]{1,0:T(8,128)(2,1)S(1)}, bf16[128,1152]{1,0:T(8,128)(2,1)S(1)}, u32[]{:S(2)}, u32[]{:S(2)}) collective-permute-start(bf16[128,1152]{1,0:T(8,128)(2,1)S(1)} %collective-permute-done.5.refs_4_), channel_id=1, source_target_pairs={{0,2},{1,3},{2,0},{3,1},{4,6},{5,7},{6,4},{7,5},{8,10},{9,11},{10,... | collective-permute-start | bytes 884744 | tf_op jit(solution)/shard_map/ppermute | solution.py:174
  19.3 9.9 %collective-permute-start.6 = (bf16[128,1152]{1,0:T(8,128)(2,1)S(1)}, bf16[128,1152]{1,0:T(8,128)(2,1)S(1)}, u32[]{:S(2)}, u32[]{:S(2)}) collective-permute-start(bf16[128,1152]{1,0:T(8,128)(2,1)S(1)} %collective-permute-done.5.refs_4_), channel_id=1, source_target_pairs={{0,4},{1,5},{2,6},{3,7},{4,0},{5,1},{6,2},{7,3},{8,12},{9,13},{10,... | collective-permute-start | bytes 884744 | tf_op jit(solution)/shard_map/ppermute | solution.py:174
  20.9 16.0 %collective-permute-start.3 = (bf16[128,1152]{1,0:T(8,128)(2,1)S(1)}, bf16[128,1152]{1,0:T(8,128)(2,1)S(1)}, u32[]{:S(2)}, u32[]{:S(2)}) collective-permute-start(bf16[128,1152]{1,0:T(8,128)(2,1)S(1)} %dynamic-slice_bitcast_fusion.refs_0_), channel_id=1, source_target_pairs={{0,4},{1,5},{2,6},{3,7},{4,0},{5,1},{6,2},{7,3},{8,12},{9,13},{10,... | collective-permute-start | bytes 884744 | tf_op jit(solution)/shard_map/ppermute | solution.py:174
  21.3 20.3 %collective-permute-start.4 = (bf16[128,1152]{1,0:T(8,128)(2,1)S(1)}, bf16[128,1152]{1,0:T(8,128)(2,1)S(1)}, u32[]{:S(2)}, u32[]{:S(2)}) collective-permute-start(bf16[128,1152]{1,0:T(8,128)(2,1)S(1)} %collective-permute-done.2.refs_1_), channel_id=1, source_target_pairs={{0,4},{1,5},{2,6},{3,7},{4,0},{5,1},{6,2},{7,3},{8,12},{9,13},{10,... | collective-permute-start | bytes 884744 | tf_op jit(solution)/shard_map/ppermute | solution.py:174
  27.4 15.8 %collective-permute-start.9 = (bf16[64,1152]{1,0:T(8,128)(2,1)S(1)}, bf16[64,1152]{1,0:T(8,128)(2,1)S(1)}, u32[]{:S(2)}, u32[]{:S(2)}) collective-permute-start(bf16[64,1152]{1,0:T(8,128)(2,1)S(1)} %slice.25), channel_id=1, source_target_pairs={{0,4},{1,5},{2,6},{3,7},{4,0},{5,1},{6,2},{7,3},{8,12},{9,13},{10,... | collective-permute-start | bytes 442376 | tf_op jit(solution)/shard_map/ppermute | solution.py:174
  29.2 14.0 %collective-permute-start.8 = (bf16[64,1152]{1,0:T(8,128)(2,1)S(1)}, bf16[64,1152]{1,0:T(8,128)(2,1)S(1)}, u32[]{:S(2)}, u32[]{:S(2)}) collective-permute-start(bf16[64,1152]{1,0:T(8,128)(2,1)S(1)} %slice.24), channel_id=1, source_target_pairs={{0,2},{1,3},{2,0},{3,1},{4,6},{5,7},{6,4},{7,5},{8,10},{9,11},{10,... | collective-permute-start | bytes 442376 | tf_op jit(solution)/shard_map/ppermute | solution.py:174
  31.3 1.2 %collective-permute-start = (s32[1]{0:T(128)}, s32[1]{0:T(128)}, u32[]{:S(2)}, u32[]{:S(2)}) collective-permute-start(s32[1]{0:T(128)} %param.5), channel_id=1, source_target_pairs={{0,1},{1,0},{2,3},{3,2},{4,5},{5,4},{6,7},{7,6},{8,9},{9,8},{10,11... | collective-permute-start | bytes 20 | tf_op jit(solution)/shard_map/ppermute | solution.py:213
  33.2 3.5 %collective-permute-start.1 = (s32[2]{0:T(128)S(1)}, s32[2]{0:T(128)S(1)}, u32[]{:S(2)}, u32[]{:S(2)}) collective-permute-start(s32[2]{0:T(128)S(1)} %broadcast_select_fusion), channel_id=1, source_target_pairs={{0,2},{1,3},{2,0},{3,1},{4,6},{5,7},{6,4},{7,5},{8,10},{9,11},{10,... | collective-permute-start | bytes 32 | tf_op jit(solution)/shard_map/ppermute | solution.py:220
  43.2 0.7 %copy-start.1 = (s32[1024]{0:T(1024)S(1)}, s32[1024]{0:T(1024)}, u32[]{:S(2)}) copy-start(s32[1024]{0:T(1024)} %param.4) | copy-start | bytes 12292
  49.9 1.7 %collective-permute-start.11 = (f32[64,1024]{1,0:T(8,128)S(1)}, f32[64,1024]{1,0:T(8,128)S(1)}, u32[]{:S(2)}, u32[]{:S(2)}) collective-permute-start(f32[64,1024]{1,0:T(8,128)S(1)} %get-tuple-element.6.s_strip), channel_id=1, source_target_pairs={{0,1},{1,0},{2,3},{3,2},{4,5},{5,4},{6,7},{7,6},{8,9},{9,8},{10,11... | collective-permute-start | bytes 786440 | tf_op jit(solution)/shard_map/ppermute | solution.py:254
  49.9 1.6 %collective-permute-start.10 = (f32[8,1024]{1,0:T(8,128)S(1)}, f32[8,1024]{1,0:T(8,128)S(1)}, u32[]{:S(2)}, u32[]{:S(2)}) collective-permute-start(f32[8,1024]{1,0:T(8,128)S(1)} %get-tuple-element.5.s_stats), channel_id=1, source_target_pairs={{0,1},{1,0},{2,3},{3,2},{4,5},{5,4},{6,7},{7,6},{8,9},{9,8},{10,11... | collective-permute-start | bytes 98312 | tf_op jit(solution)/shard_map/ppermute | solution.py:253
  53.5 3.3 %collective-permute-start.12 = (f32[40,1152]{1,0:T(8,128)S(1)}, f32[40,1152]{1,0:T(8,128)S(1)}, u32[]{:S(2)}, u32[]{:S(2)}) collective-permute-start(f32[40,1152]{1,0:T(8,128)S(1)} %slice_bitcast_fusion.1), channel_id=1, source_target_pairs={{1,0},{3,2},{5,4},{7,6},{9,8},{11,10},{13,12},{15,14},{17,16},{19,... | collective-permute-start | bytes 552968 | tf_op jit(solution)/shard_map/ppermute | solution.py:271

commit v2 on v0

v2 whole, which is shorter than its diff:
```python
import functools

import jax
import jax.numpy as jnp
from jax import lax
from jax.experimental import pallas as pl
from jax.experimental.pallas import tpu as pltpu
from jax.sharding import PartitionSpec as P

WEIGHT = 16.0
NEG = -1e30
LOG2E = 1.4426950408889634
CODES = 6
TILE = 256
CHUNK = 128
SPAN = 1024
ALL = ("batch", "temp")
SMEM = pl.BlockSpec(memory_space=pltpu.SMEM)
VMEM = pl.BlockSpec(memory_space=pltpu.VMEM)


def carried(count, body, carry):
    if count <= 8:
        for i in range(count):
            carry = body(i, carry)
        return carry
    return lax.fori_loop(0, count, body, carry)


def at(i, size):
    return pl.ds(i * size if isinstance(i, int) else pl.multiple_of(i * size, size), size)


def widths(code, width):
    root = jnp.sqrt(jnp.float32(width))
    return [jnp.exp2(0.5 * (code - jnp.float32(level))) / root for level in range(CODES)]


def powers(d, widest, wide):
    e = [None] * CODES
    e[5], e[4] = jnp.exp2(d * widest), jnp.exp2(d * wide)
    for level in (3, 2, 1, 0):
        e[level] = e[level + 2] * e[level + 2]
    return e


def columns(gram, count, bases):
    size = min(CHUNK, count)
    steps = count // size
    tile = gram.shape[1]
    best = carried(
        steps,
        lambda i, best: jnp.maximum(best, jnp.max(gram[at(i, size), :], axis=0, keepdims=True)),
        jnp.full((1, tile), NEG, jnp.float32),
    )

    def add(i, sums):
        e = powers(gram[at(i, size), :] - best, *bases)
        return tuple(s + jnp.sum(v, axis=0, keepdims=True) for s, v in zip(sums, e))

    return best, carried(steps, add, (jnp.zeros((1, tile), jnp.float32),) * CODES)


def times(a, b):
    return lax.dot_general(a, b, (((1,), (1,)), ((), ())), preferred_element_type=jnp.float32)


def hide_diagonal(gram, rows):
    square = gram[rows, :]
    own = lax.broadcasted_iota(jnp.int32, square.shape, 0) == lax.broadcasted_iota(
        jnp.int32, square.shape, 1
    )
    gram[rows, :] = jnp.where(own, NEG, square)


def bases_of(code, width):
    beta = widths(code.astype(jnp.float32), width)
    return beta[5] * LOG2E, beta[4] * LOG2E


def tiles(total):
    return [(i, min(TILE, total - i)) for i in range(0, total, TILE)]


def first_kernel(place, rows, scalars, codes, *refs):
    *pieces, stats, strip, whole, gram = refs if place else (*refs[:-1], refs[0], refs[-1])
    if place:
        place(scalars, pieces, whole)
    total, width = whole.shape
    mine = pl.ds(pl.multiple_of(scalars[0], rows), rows)

    def tile(cols, size):
        part = gram.at[:, 0:size]
        part[...] = times(whole[...], whole[cols, :])
        hide_diagonal(part, cols)
        strip[:, cols] = part[mine, :]
        best, sums = columns(part, total, bases_of(codes[:, cols], width))
        stats[0:1, cols] = best
        for level in range(CODES):
            stats[1 + level : 2 + level, cols] = sums[level]
        stats[1 + CODES :, cols] = jnp.zeros((stats.shape[0] - 1 - CODES, size), jnp.float32)

    if total <= 4 * TILE:
        for start, size in tiles(total):
            tile(pl.ds(start, size), size)
    else:

        @pl.loop(0, total // TILE)
        def _(i):
            tile(at(i, TILE), TILE)


def place_first(scalars, pieces, whole):
    u, p, q, f, a = pieces
    block, half = u.shape[0], f.shape[0]
    core = scalars[1]
    whole[0:block, :] = u[...]
    whole[pl.ds(pl.multiple_of((2 - core) * block, block), block), :] = p[...]
    whole[pl.ds(pl.multiple_of((1 + core) * block, block), block), :] = q[0:block, :]
    whole[3 * block : 4 * block, :] = q[block : 2 * block, :]
    whole[4 * block : 4 * block + half, :] = f[...]
    whole[4 * block + half : 5 * block, :] = a[...]


def place_second(core, n, a, b, c, whole):
    half = n.shape[0]
    whole[0 : 2 * half, :] = b[0 : 2 * half, :]
    whole[2 * half : 3 * half, :] = n[...]
    spot = lambda i: pl.ds(pl.multiple_of(i * half, half), half)
    whole[spot(3 + core), :] = a[...]
    whole[spot(4 - core), :] = c[0:half, :]
    whole[5 * half : 6 * half, :] = c[half : 2 * half, :]


def second_kernel(
    rows, scalars, codes, early, e_stats, e_strip, b, n, a, c, keep, send, stats, strip, late, gram
):
    core = scalars[1]
    place_second(core, n, a, b, c, late)
    head, width = early.shape
    tail = late.shape[0]
    mine = pl.ds(pl.multiple_of(scalars[0], rows), rows)
    strip[:, 0:head] = e_strip[...]
    for start, size in tiles(tail):
        cols = pl.ds(start, size)
        part = gram.at[:, 0:size]
        part[0:head, :] = times(early[...], late[cols, :])
        part[head : head + tail, :] = times(late[...], late[cols, :])
        hide_diagonal(part, pl.ds(head + start, size))
        strip[:, head + start : head + start + size] = part[mine, :]
        best, sums = columns(
            part, head + tail, bases_of(codes[:, head + start : head + start + size], width)
        )
        stats[0:1, head + start : head + start + size] = best
        for level in range(CODES):
            stats[1 + level : 2 + level, head + start : head + start + size] = sums[level]
    for start, size in tiles(head):
        cols = pl.ds(start, size)
        part = gram.at[0:tail, 0:size]
        part[...] = times(late[...], early[cols, :])
        bases = bases_of(codes[:, cols], width)
        best, sums = columns(part, tail, bases)
        before = e_stats[0:1, cols]
        top = jnp.maximum(best, before)
        was, now = powers(before - top, *bases), powers(best - top, *bases)
        stats[0:1, cols] = top
        for level in range(CODES):
            stats[1 + level : 2 + level, cols] = (
                e_stats[1 + level : 2 + level, cols] * was[level] + sums[level] * now[level]
            )
    line = jnp.zeros((1, head + tail), jnp.float32)
    lane = lax.broadcasted_iota(jnp.int32, line.shape, 1)
    level = scalars[2].astype(jnp.float32)
    theirs = b[2 * n.shape[0] : 2 * n.shape[0] + 1, 0:1].astype(jnp.float32)
    stats[1 + CODES :, :] = jnp.where(lane < 128, level, theirs)
    half = rows // 2
    keep[0:half, :] = strip[pl.ds(pl.multiple_of(core * half, half), half), :]
    send[0:half, :] = strip[pl.ds(pl.multiple_of((1 - core) * half, half), half), :]
    keep[half:, :] = stats[...]
    send[half:, :] = stats[...]


class Mixer:
    def __init__(self, scalars, block, width, codes, keep, recv, turned):
        self.codes, self.width, self.block = codes, width, block
        self.rows = keep.shape[0] - 8
        self.student = scalars[1] == 1
        self.keep, self.recv = keep, recv
        rows, own = self.rows, pl.ds(pl.multiple_of(scalars[3], block), block)
        code = codes[:, own].astype(jnp.float32)
        turned[0] = self.pick(rows, rows + 8, own, True).T
        turned[1] = self.pick(rows, rows + 8, own, False).T
        turned[2] = jnp.broadcast_to(code, (8, block)).T
        mine = pl.ds(pl.multiple_of(scalars[4], rows), rows)
        s, t = turned[0, mine, :], turned[1, mine, :]
        self.beta = widths(turned[2, mine, 0:1], width)
        found = [
            ref[rows + 1 + CODES : rows + 2 + CODES, lane : lane + 1]
            for ref in (keep, recv)
            for lane in (0, 128)
        ]
        self.count = [sum(jnp.where(v == jnp.float32(c), 1.0, 0.0) for v in found) for c in range(CODES)]
        self.s_top, self.t_top = s[:, 0:1], t[:, 0:1]
        self.s_sum = [s[:, 1 + c : 2 + c] for c in range(CODES)]
        self.t_sum = [t[:, 1 + c : 2 + c] for c in range(CODES)]

    def pick(self, low, high, cols, student):
        here, there = self.keep[low:high, cols], self.recv[low:high, cols]
        return jnp.where(self.student == student, here, there)

    def weighted(self, d, beta, sums):
        e = powers(d, beta[5] * LOG2E, beta[4] * LOG2E)
        return sum(v * (n * b / s) for v, n, b, s in zip(e, self.count, beta, sums))

    def part(self, cols):
        rows = self.rows
        gs, gt = self.pick(0, rows, cols, True), self.pick(0, rows, cols, False)
        s, t = self.pick(rows, rows + 8, cols, True), self.pick(rows, rows + 8, cols, False)
        beta = widths(self.codes[:, cols].astype(jnp.float32), self.width)
        lines = lambda a: [a[1 + c : 2 + c] for c in range(CODES)]
        p_row = self.weighted(gt - self.t_top, self.beta, self.t_sum)
        q_row = self.weighted(gs - self.s_top, self.beta, self.s_sum)
        p_col = self.weighted(gt - t[0:1], beta, lines(t))
        q_col = self.weighted(gs - s[0:1], beta, lines(s))
        mix = WEIGHT * ((q_row - p_row) + (q_col - p_col))
        return mix.astype(jnp.bfloat16), jnp.sum(p_row * (gt - gs), axis=1, keepdims=True)

    def store_loss(self, loss, out):
        for c in range(CODES):
            loss = loss + self.count[c] * (
                self.beta[c] * (self.s_top - self.t_top)
                + (jnp.log(self.s_sum[c]) - jnp.log(self.t_sum[c]))
            )
        out[...] = jnp.broadcast_to(loss, (self.rows, 128)).T[0:1, :]


def product(a, b):
    return jnp.dot(a, b, preferred_element_type=jnp.float32)


def mix_kernel(
    scalars, codes, keep, recv, early, their_early, b, n, a, c, their_bc, their_na, out, loss, late, turned
):
    block, half = 2 * n.shape[0], n.shape[0]
    mixer = Mixer(scalars, block, out.shape[1], codes, keep, recv, turned)
    head, tail = early.shape[0], late.shape[0]
    mix_head, loss_head = mixer.part(pl.ds(0, head))
    mix_tail, loss_tail = mixer.part(pl.ds(head, tail))
    mixer.store_loss(loss_head + loss_tail, loss)

    @pl.when(scalars[1] == 1)
    def _():
        place_second(1, n, a, b, c, late)
        out[...] = product(mix_head, early[...]) + product(mix_tail, late[...])

    @pl.when(scalars[1] == 0)
    def _():
        tail_b, tail_c = their_bc.at[0:block, :], their_bc.at[block : 2 * block, :]
        place_second(1, their_na.at[0:half, :], their_na.at[half:block, :], tail_b, tail_c, late)
        out[...] = product(mix_head, their_early[...]) + product(mix_tail, late[...])


def wide_mix_kernel(block, scalars, codes, keep, recv, student, out, loss, turned):
    total, width = student.shape
    mixer = Mixer(scalars, block, width, codes, keep, recv, turned)
    span = min(SPAN, total)

    def step(i, carry):
        mix, gap = mixer.part(at(i, span))
        return carry[0] + product(mix, student[at(i, span), :]), carry[1] + gap

    zero = jnp.zeros((mixer.rows, width), jnp.float32), jnp.zeros((mixer.rows, 1), jnp.float32)
    out[...], gap = lax.fori_loop(0, total // span, step, zero)
    mixer.store_loss(gap, loss)


def call(kernel, shapes, scratch, limit, *args):
    return pl.pallas_call(
        kernel,
        out_shape=shapes,
        in_specs=[SMEM] + [VMEM] * (len(args) - 1),
        out_specs=[VMEM] * len(shapes),
        scratch_shapes=scratch,
        compiler_params=pltpu.CompilerParams(vmem_limit_bytes=limit << 20),
    )(*args)


def shape(*dims, dtype=jnp.float32):
    return jax.ShapeDtypeStruct(dims, dtype)


def shards(mesh, embeddings, spread_code, level_index):
    block, width = embeddings.shape[1:]
    batches, parts = mesh.shape["batch"], mesh.shape["temp"]
    total = block * batches
    me, part = lax.axis_index("batch"), lax.axis_index("temp")
    x, core = part // 2, part % 2
    rows, half = block // 2, block // 4

    def send(a, to):
        pairs = []
        for b in range(batches):
            for t in range(parts):
                there = to(b, t // 2, t % 2)
                pairs.append((b * parts + t, there[0] * parts + there[1] * 2 + there[2]))
        return lax.ppermute(a, ALL, pairs)

    over_core = lambda b, x, c: (b, x, 1 - c)
    over_x = lambda b, x, c: (b, 1 - x, c)
    u = lax.dynamic_index_in_dim(embeddings, core, 0, keepdims=False)
    out_shapes = [shape(half, width), shape(1, half)]

    if batches != 8 or parts != 4:
        whole = lax.all_gather(u, "batch", axis=0, tiled=True)
        theirs = send(level_index, over_x)
        codes = spread_code[None, :]
        scalars = jnp.stack(
            [me * block + x * rows, core, level_index[0], me * block, x * rows + core * half]
        ).astype(jnp.int32)
        stats, strip = call(
            functools.partial(first_kernel, None, rows),
            [shape(8, total), shape(rows, total)],
            [pltpu.VMEM((total, TILE), jnp.float32)],
            56,
            scalars,
            codes,
            whole,
        )
        lane = jnp.arange(total)[None, :]
        line = jnp.where(lane < 128, level_index[0], theirs[0]).astype(jnp.float32)
        stats = jnp.concatenate([stats[: 1 + CODES], line])
        share = lambda c: lax.dynamic_slice_in_dim(strip, c * half, half)
        keep = jnp.concatenate([share(core), stats])
        recv = send(jnp.concatenate([share(1 - core), stats]), over_core)
        student = jnp.where(core == 1, whole, send(whole, over_core))
        out, loss = call(
            functools.partial(wide_mix_kernel, block),
            out_shapes,
            [pltpu.VMEM((3, block, 8), jnp.float32)],
            56,
            scalars,
            codes,
            keep,
            recv,
            student,
        )
        return out, loss[0]

    near = lambda b, x, c: (b ^ 2, x, c)
    far = lambda b, x, c: (b ^ 4, x, c)
    over_y = lambda b, x, c: (b ^ 1, x, c)
    either = lambda even, odd: lambda b, x, c: (odd if c else even)(b, x, c)
    row = lambda a: lax.dynamic_slice_in_dim(a, x * rows, rows, 0)
    f = send(row(u), far)
    p = send(u, either(near, over_y))
    n = send(f, near)
    q = send(jnp.concatenate([u, p]), either(over_y, near))
    fa = send(f, over_y)
    level = jnp.broadcast_to(level_index.astype(jnp.bfloat16), (16, width))
    b = send(jnp.concatenate([f, fa, level]), over_x)
    a = send(n, either(over_x, over_y))
    c = send(jnp.concatenate([n, a]), either(over_y, over_x))

    block_codes = [
        lax.dynamic_slice_in_dim(spread_code, (me ^ m) * block, block) for m in range(batches)
    ]
    first = lambda m: lax.dynamic_slice_in_dim(block_codes[m], x * rows, rows)
    second = lambda m: lax.dynamic_slice_in_dim(block_codes[m], (1 - x) * rows, rows)
    codes = jnp.concatenate(
        block_codes[:4]
        + [first(4), first(5), second(4), second(5), first(6), second(6), first(7), second(7)]
    )[None, :]
    scalars = jnp.stack(
        [x * rows, core, level_index[0], 0 * core, x * rows + core * half]
    ).astype(jnp.int32)
    head = 5 * block
    e_stats, e_strip, early = call(
        functools.partial(first_kernel, place_first, rows),
        [shape(8, head), shape(rows, head), shape(head, width, dtype=jnp.bfloat16)],
        [pltpu.VMEM((head, TILE), jnp.float32)],
        16,
        scalars,
        codes,
        u,
        p,
        q,
        f,
        fa,
    )
    their_early = send(early, over_core)
    their_na = send(jnp.concatenate([n, a]), over_core)
    their_bc = send(jnp.concatenate([b[:block], c]), over_core)
    tail = total - head
    keep, mail = call(
        functools.partial(second_kernel, rows),
        [shape(half + 8, total), shape(half + 8, total)],
        [
            pltpu.VMEM((8, total), jnp.float32),
            pltpu.VMEM((rows, total), jnp.float32),
            pltpu.VMEM((tail, width), jnp.bfloat16),
            pltpu.VMEM((total, TILE), jnp.float32),
        ],
        16,
        scalars,
        codes,
        early,
        e_stats,
        e_strip,
        b,
        n,
        a,
        c,
    )
    recv = send(mail, over_core)
    out, loss = call(
        mix_kernel,
        out_shapes,
        [pltpu.VMEM((tail, width), jnp.bfloat16), pltpu.VMEM((3, block, 8), jnp.float32)],
        16,
        scalars,
        codes,
        keep,
        recv,
        early,
        their_early,
        b,
        n,
        a,
        c,
        their_bc,
        their_na,
    )
    return out, loss[0]


def solution(mesh):
    in_specs = (P(None, "batch", None), P(), P("temp"))
    out_specs = (P(("batch", "temp"), None), P(("batch", "temp")))
    return jax.shard_map(
        functools.partial(shards, mesh),
        mesh=mesh,
        in_specs=in_specs,
        out_specs=out_specs,
        check_vma=False,
    )
```

time: 176 us -> 45.8 us (0.26)
  waiting for transfers between devices: 125 us -> 16 us
  blocking collectives: 23.4 us -> 0 us
  starting transfers between devices: 0.12 us -> 16.9 us
  between operations: 15.1 us -> 1.41 us
  Pallas kernels: 0 us -> 9.67 us
  matrix products: 7.56 us -> 0 us
    all_gather x2 -> x0, waiting for transfers between devices: 112 us -> none  [the longest x1 81.6 us: shards(): lax.all_gather(embeddings, 'batch', axis=1, tiled=True)]
    all_gather x1 -> x0, blocking collectives: 17.7 us -> none  [shards(): stats = lax.all_gather(sums, 'batch', axis=2, tiled=True)]
    ppermute x0 -> x12, starting transfers between devices: none -> 16.9 us  [send(): return lax.ppermute(a, ALL, pairs)]
    ppermute x0 -> x12, waiting for transfers between devices: none -> 16 us  [send(): return lax.ppermute(a, ALL, pairs)]
    reduce_scatter x1 -> x0, waiting for transfers between devices: 12.9 us -> none  [shards(): lax.psum_scatter(carry, 'temp', scatter_dimension=0, tiled=True)]
    pallas_call x0 -> x3, Pallas kernels: none -> 9.67 us  [call(): pl.pallas_call(kernel, out_shape=shapes, in_specs=[SMEM] + [VMEM] * (len(...]
    dot_general x2 -> x0, matrix products: 7.56 us -> none  [the longest x1 4.15 us: shards(): jnp.einsum('kad,kjd->kaj', embeddings, lax.all_gather(embeddings, 'batch'...]
    unnamed x1 -> x0, blocking collectives: 5.67 us -> none
  transfers between devices with their start and end apart: 3 -> 12, of which waited for: 3 -> 4; matrix products, arithmetic and copies ran while one was open for 5% -> 1% of each run, Pallas kernels for 0% -> 16%
where the time goes in v2:
time: 45.8 us; the launch traced here: 45.6 us
  starting transfers between devices  16.9 us (37%)
  waiting for transfers between devices  16 us (35%)
  Pallas kernels  9.67 us (21%)
  local copies, waits for them, and re-layouts  1.5 us (3%)
  between operations  1.41 us (3%)
    ppermute x12, starting transfers between devices, send(): return lax.ppermute(a, ALL, pairs)  16.9 us
    ppermute x12, waiting for transfers between devices, send(): return lax.ppermute(a, ALL, pairs)  16 us
    pallas_call x3, Pallas kernels, call(): pl.pallas_call(kernel, out_shape=shapes, in_specs=[SMEM] + [VMEM] * (len(...  9.67 us
    unnamed x5, local copies, waits for them, and re-layouts  1.05 us
  transfers between devices with their start and end apart: 12, of which 4 were waited for; matrix products, arithmetic and copies ran while one was open for 1% of the time, Pallas kernels for 16%

profile of v2, /device:TPU:0, one launch (start us, length us, event | category | flops | bytes accessed | tf_op | source)
XLA Modules:
  0.0 45.6 jit_solution(18298649747140977906)
XLA Ops:
  0.6 0.0 copy-start
  0.6 0.0 copy-start.1
  0.7 1.0 %copy-done = bf16[2,128,1152]{2,1,0:T(8,128)(2,1)S(1)} copy-done((bf16[2,128,1152]{2,1,0:T(8,128)(2,1)S(1)}, bf16[2,128,1152]{2,1,0:T(8,128)(2,1)}, u32[]{:S(2)}) %copy-start) | copy-done | bytes 589848
  1.7 3.1 %collective-permute-start = (bf16[128,1152]{1,0:T(8,128)(2,1)S(1)}, bf16[128,1152]{1,0:T(8,128)(2,1)S(1)}, u32[]{:S(2)}, u32[]{:S(2)}) collective-permute-start(bf16[128,1152]{1,0:T(8,128)(2,1)S(1)} %dynamic-slice_bitcast_fusion.refs_0_), channel_id=1, source_target_pairs={{0,8},{1,5},{2,10},{3,7},{4,12},{5,1},{6,14},{7,3},{8,0},{9,13},{1... | collective-permute-start | bytes 884744 | tf_op jit(solution)/shard_map/ppermute | solution.py:306
  4.9 2.7 %collective-permute-start.2 = (bf16[64,1152]{1,0:T(8,128)(2,1)S(1)}, bf16[64,1152]{1,0:T(8,128)(2,1)S(1)}, u32[]{:S(2)}, u32[]{:S(2)}) collective-permute-start(bf16[64,1152]{1,0:T(8,128)(2,1)S(1)} %dynamic-slice_bitcast_fusion.1), channel_id=1, source_target_pairs={{0,16},{1,17},{2,18},{3,19},{4,20},{5,21},{6,22},{7,23},{8,24},{9,... | collective-permute-start | bytes 442376 | tf_op jit(solution)/shard_map/ppermute | solution.py:306
  7.5 5.2 %collective-permute-done.2.refs_3_ = bf16[64,1152]{1,0:T(8,128)(2,1)S(1)} collective-permute-done((bf16[64,1152]{1,0:T(8,128)(2,1)S(1)}, bf16[64,1152]{1,0:T(8,128)(2,1)S(1)}, u32[]{:S(2)}, u32[]{:S(2)}) %collective-permute-start.2) | collective-permute-done | bytes 147488 | tf_op jit(solution)/shard_map/ppermute | solution.py:306
  12.7 1.1 %collective-permute-start.3 = (bf16[64,1152]{1,0:T(8,128)(2,1)S(1)}, bf16[64,1152]{1,0:T(8,128)(2,1)S(1)}, u32[]{:S(2)}, u32[]{:S(2)}) collective-permute-start(bf16[64,1152]{1,0:T(8,128)(2,1)S(1)} %collective-permute-done.2.refs_3_), channel_id=1, source_target_pairs={{0,4},{1,5},{2,6},{3,7},{4,0},{5,1},{6,2},{7,3},{8,12},{9,13},{10,... | collective-permute-start | bytes 442376 | tf_op jit(solution)/shard_map/ppermute | solution.py:306
  13.8 0.0 collective-permute-done.refs_1_
  13.8 1.0 %collective-permute-start.1 = (bf16[256,1152]{1,0:T(8,128)(2,1)S(1)}, bf16[256,1152]{1,0:T(8,128)(2,1)S(1)}, u32[]{:S(2)}, u32[]{:S(2)}) collective-permute-start(bf16[256,1152]{1,0:T(8,128)(2,1)S(1)} %pad_maximum_fusion), channel_id=1, source_target_pairs={{0,4},{1,9},{2,6},{3,11},{4,0},{5,13},{6,2},{7,15},{8,12},{9,1},{1... | collective-permute-start | bytes 1769480 | tf_op jit(solution)/shard_map/ppermute | solution.py:306
  14.8 0.0 copy-done.1
  14.8 0.1 fusion.1
  15.6 0.1 stack.15.scalars
  15.7 0.1 fusion
  15.8 0.1 concatenate.16
  15.9 3.0 %collective-permute-start.5 = (bf16[64,1152]{1,0:T(8,128)(2,1)S(1)}, bf16[64,1152]{1,0:T(8,128)(2,1)S(1)}, u32[]{:S(2)}, u32[]{:S(2)}) collective-permute-start(bf16[64,1152]{1,0:T(8,128)(2,1)S(1)} %collective-permute-done.2.refs_3_), channel_id=1, source_target_pairs={{0,8},{1,9},{2,10},{3,11},{4,12},{5,13},{6,14},{7,15},{8,0},{9,1},... | collective-permute-start | bytes 442376 | tf_op jit(solution)/shard_map/ppermute | solution.py:306
  18.9 0.0 collective-permute-done.3.refs_4_
  18.9 0.1 maximum_maximum_fusion
  19.0 1.6 %collective-permute-start.4 = (bf16[144,1152]{1,0:T(8,128)(2,1)S(1)}, bf16[144,1152]{1,0:T(8,128)(2,1)S(1)}, u32[]{:S(2)}, u32[]{:S(2)}) collective-permute-start(bf16[144,1152]{1,0:T(8,128)(2,1)S(1)} %maximum_maximum_fusion), channel_id=1, source_target_pairs={{0,2},{1,3},{2,0},{3,1},{4,6},{5,7},{6,4},{7,5},{8,10},{9,11},{10,... | collective-permute-start | bytes 995336 | tf_op jit(solution)/shard_map/ppermute | solution.py:306
  20.6 3.1 %collective-permute-done.5.n = bf16[64,1152]{1,0:T(8,128)(2,1)S(1)} collective-permute-done((bf16[64,1152]{1,0:T(8,128)(2,1)S(1)}, bf16[64,1152]{1,0:T(8,128)(2,1)S(1)}, u32[]{:S(2)}, u32[]{:S(2)}) %collective-permute-start.5) | collective-permute-done | bytes 147488 | tf_op jit(solution)/shard_map/ppermute | solution.py:306
  23.6 1.5 %collective-permute-start.6 = (bf16[64,1152]{1,0:T(8,128)(2,1)S(1)}, bf16[64,1152]{1,0:T(8,128)(2,1)S(1)}, u32[]{:S(2)}, u32[]{:S(2)}) collective-permute-start(bf16[64,1152]{1,0:T(8,128)(2,1)S(1)} %collective-permute-done.5.n), channel_id=1, source_target_pairs={{0,2},{1,5},{2,0},{3,7},{4,6},{5,1},{6,4},{7,3},{8,10},{9,13},{10,... | collective-permute-start | bytes 442376 | tf_op jit(solution)/shard_map/ppermute | solution.py:306
  25.1 0.0 collective-permute-done.1.refs_2_
  25.1 2.9 %shard_map.50 = (f32[8,640]{1,0:T(8,128)S(1)}, f32[64,640]{1,0:T(8,128)S(1)}, bf16[640,1152]{1,0:T(8,128)(2,1)S(1)}) custom-call(s32[5]{0:T(128)S(1)} %stack.15.scalars, s32[1,1024]{1,0:T(1,128)S(1)} %bitcast.10, bf16[128,1152]{1,0:T(8,128)(2,1)S(1)} %dynamic-slice_bitcast_fusion.refs_0_, bf16[128,1152]{1,0:T(8,128)(2,1)S(1)} %collective-permute-done.refs_1_, ...), custom_call_target="tpu_custom_call" | custom-call | tf_op jit(solution)/shard_map/pallas_call | solution.py:278
  28.1 1.9 %collective-permute-start.9 = (bf16[640,1152]{1,0:T(8,128)(2,1)S(1)}, bf16[640,1152]{1,0:T(8,128)(2,1)S(1)}, u32[]{:S(2)}, u32[]{:S(2)}) collective-permute-start(bf16[640,1152]{1,0:T(8,128)(2,1)S(1)} %get-tuple-element.9.early), channel_id=1, source_target_pairs={{0,1},{1,0},{2,3},{3,2},{4,5},{5,4},{6,7},{7,6},{8,9},{9,8},{10,11... | collective-permute-start | bytes 4423688 | tf_op jit(solution)/shard_map/ppermute | solution.py:306
  30.0 0.0 collective-permute-done.6.a
  30.0 0.4 collective-permute-start.7
  30.4 0.0 collective-permute-done.4.b
  30.4 6.4 %collective-permute-done.7.c = bf16[128,1152]{1,0:T(8,128)(2,1)S(1)} collective-permute-done((bf16[128,1152]{1,0:T(8,128)(2,1)S(1)}, bf16[128,1152]{1,0:T(8,128)(2,1)S(1)}, u32[]{:S(2)}, u32[]{:S(2)}) %collective-permute-start.7) | collective-permute-done | bytes 294944 | tf_op jit(solution)/shard_map/ppermute | solution.py:306
  36.8 0.1 collective-permute-start.10
  36.9 0.5 %collective-permute-start.11 = (bf16[128,1152]{1,0:T(8,128)(2,1)S(1)}, bf16[128,1152]{1,0:T(8,128)(2,1)S(1)}, u32[]{:S(2)}, u32[]{:S(2)}) collective-permute-start(bf16[128,1152]{1,0:T(8,128)(2,1)S(1)} %constant_dynamic-update-slice_fusion), channel_id=1, source_target_pairs={{0,1},{1,0},{2,3},{3,2},{4,5},{5,4},{6,7},{7,6},{8,9},{9,8},{10,11... | collective-permute-start | bytes 884744 | tf_op jit(solution)/shard_map/ppermute | solution.py:306
  37.4 4.2 %shard_map.51 = (f32[40,1024]{1,0:T(8,128)S(1)}, f32[40,1024]{1,0:T(8,128)S(1)}) custom-call(s32[5]{0:T(128)S(1)} %stack.15.scalars, s32[1,1024]{1,0:T(1,128)S(1)} %bitcast.11, bf16[640,1152]{1,0:T(8,128)(2,1)S(1)} %get-tuple-element.9.early, f32[8,640]{1,0:T(8,128)S(1)} %get-tuple-element.10.e_stats, f32[64,640]{1,0:T(8,128)S(1)} %get-tuple-element.11.e_strip, ...), custom_call_target="tpu_custom_call" | custom-call | tf_op jit(solution)/shard_map/pallas_call | solution.py:278
  41.6 0.2 collective-permute-start.8
  41.7 0.0 collective-permute-done.11.their_na
  41.7 1.3 %collective-permute-done.8.recv = f32[40,1024]{1,0:T(8,128)S(1)} collective-permute-done((f32[40,1024]{1,0:T(8,128)S(1)}, f32[40,1024]{1,0:T(8,128)S(1)}, u32[]{:S(2)}, u32[]{:S(2)}) %collective-permute-start.8) | collective-permute-done | bytes 163872 | tf_op jit(solution)/shard_map/ppermute | solution.py:306
  43.0 0.0 collective-permute-done.10.their_bc
  43.0 0.0 collective-permute-done.9.their_early
  43.0 2.6 %shard_map.52 = (f32[32,1152]{1,0:T(8,128)}, f32[1,32]{1,0:T(1,128)}) custom-call(s32[5]{0:T(128)S(1)} %stack.15.scalars, s32[1,1024]{1,0:T(1,128)S(1)} %bitcast.12, f32[40,1024]{1,0:T(8,128)S(1)} %get-tuple-element.12.keep, f32[40,1024]{1,0:T(8,128)S(1)} %collective-permute-done.8.recv, bf16[640,1152]{1,0:T(8,128)(2,1)S(1)} %get-tuple-element.9.early, ...), custom_call_target="tpu_custom_call" | custom-call | tf_op jit(solution)/shard_map/pallas_call | solution.py:278
  (9 shorter events, 0.2 us)
Async XLA Ops:
  0.6 1.1 %copy-start = (bf16[2,128,1152]{2,1,0:T(8,128)(2,1)S(1)}, bf16[2,128,1152]{2,1,0:T(8,128)(2,1)}, u32[]{:S(2)}) copy-start(bf16[2,128,1152]{2,1,0:T(8,128)(2,1)} %param.3) | copy-start | bytes 1769476
  0.6 14.2 %copy-start.1 = (s32[1024]{0:T(1024)S(1)}, s32[1024]{0:T(1024)}, u32[]{:S(2)}) copy-start(s32[1024]{0:T(1024)} %param.4) | copy-start | bytes 12292
  1.7 12.1 %collective-permute-start = (bf16[128,1152]{1,0:T(8,128)(2,1)S(1)}, bf16[128,1152]{1,0:T(8,128)(2,1)S(1)}, u32[]{:S(2)}, u32[]{:S(2)}) collective-permute-start(bf16[128,1152]{1,0:T(8,128)(2,1)S(1)} %dynamic-slice_bitcast_fusion.refs_0_), channel_id=1, source_target_pairs={{0,8},{1,5},{2,10},{3,7},{4,12},{5,1},{6,14},{7,3},{8,0},{9,13},{1... | collective-permute-start | bytes 884744 | tf_op jit(solution)/shard_map/ppermute | solution.py:306
  4.9 7.8 %collective-permute-start.2 = (bf16[64,1152]{1,0:T(8,128)(2,1)S(1)}, bf16[64,1152]{1,0:T(8,128)(2,1)S(1)}, u32[]{:S(2)}, u32[]{:S(2)}) collective-permute-start(bf16[64,1152]{1,0:T(8,128)(2,1)S(1)} %dynamic-slice_bitcast_fusion.1), channel_id=1, source_target_pairs={{0,16},{1,17},{2,18},{3,19},{4,20},{5,21},{6,22},{7,23},{8,24},{9,... | collective-permute-start | bytes 442376 | tf_op jit(solution)/shard_map/ppermute | solution.py:306
  12.7 6.2 %collective-permute-start.3 = (bf16[64,1152]{1,0:T(8,128)(2,1)S(1)}, bf16[64,1152]{1,0:T(8,128)(2,1)S(1)}, u32[]{:S(2)}, u32[]{:S(2)}) collective-permute-start(bf16[64,1152]{1,0:T(8,128)(2,1)S(1)} %collective-permute-done.2.refs_3_), channel_id=1, source_target_pairs={{0,4},{1,5},{2,6},{3,7},{4,0},{5,1},{6,2},{7,3},{8,12},{9,13},{10,... | collective-permute-start | bytes 442376 | tf_op jit(solution)/shard_map/ppermute | solution.py:306
  13.8 11.3 %collective-permute-start.1 = (bf16[256,1152]{1,0:T(8,128)(2,1)S(1)}, bf16[256,1152]{1,0:T(8,128)(2,1)S(1)}, u32[]{:S(2)}, u32[]{:S(2)}) collective-permute-start(bf16[256,1152]{1,0:T(8,128)(2,1)S(1)} %pad_maximum_fusion), channel_id=1, source_target_pairs={{0,4},{1,9},{2,6},{3,11},{4,0},{5,13},{6,2},{7,15},{8,12},{9,1},{1... | collective-permute-start | bytes 1769480 | tf_op jit(solution)/shard_map/ppermute | solution.py:306
  15.9 7.8 %collective-permute-start.5 = (bf16[64,1152]{1,0:T(8,128)(2,1)S(1)}, bf16[64,1152]{1,0:T(8,128)(2,1)S(1)}, u32[]{:S(2)}, u32[]{:S(2)}) collective-permute-start(bf16[64,1152]{1,0:T(8,128)(2,1)S(1)} %collective-permute-done.2.refs_3_), channel_id=1, source_target_pairs={{0,8},{1,9},{2,10},{3,11},{4,12},{5,13},{6,14},{7,15},{8,0},{9,1},... | collective-permute-start | bytes 442376 | tf_op jit(solution)/shard_map/ppermute | solution.py:306
  19.0 11.4 %collective-permute-start.4 = (bf16[144,1152]{1,0:T(8,128)(2,1)S(1)}, bf16[144,1152]{1,0:T(8,128)(2,1)S(1)}, u32[]{:S(2)}, u32[]{:S(2)}) collective-permute-start(bf16[144,1152]{1,0:T(8,128)(2,1)S(1)} %maximum_maximum_fusion), channel_id=1, source_target_pairs={{0,2},{1,3},{2,0},{3,1},{4,6},{5,7},{6,4},{7,5},{8,10},{9,11},{10,... | collective-permute-start | bytes 995336 | tf_op jit(solution)/shard_map/ppermute | solution.py:306
  23.6 6.3 %collective-permute-start.6 = (bf16[64,1152]{1,0:T(8,128)(2,1)S(1)}, bf16[64,1152]{1,0:T(8,128)(2,1)S(1)}, u32[]{:S(2)}, u32[]{:S(2)}) collective-permute-start(bf16[64,1152]{1,0:T(8,128)(2,1)S(1)} %collective-permute-done.5.n), channel_id=1, source_target_pairs={{0,2},{1,5},{2,0},{3,7},{4,6},{5,1},{6,4},{7,3},{8,10},{9,13},{10,... | collective-permute-start | bytes 442376 | tf_op jit(solution)/shard_map/ppermute | solution.py:306
  28.1 15.0 %collective-permute-start.9 = (bf16[640,1152]{1,0:T(8,128)(2,1)S(1)}, bf16[640,1152]{1,0:T(8,128)(2,1)S(1)}, u32[]{:S(2)}, u32[]{:S(2)}) collective-permute-start(bf16[640,1152]{1,0:T(8,128)(2,1)S(1)} %get-tuple-element.9.early), channel_id=1, source_target_pairs={{0,1},{1,0},{2,3},{3,2},{4,5},{5,4},{6,7},{7,6},{8,9},{9,8},{10,11... | collective-permute-start | bytes 4423688 | tf_op jit(solution)/shard_map/ppermute | solution.py:306
  30.0 6.8 %collective-permute-start.7 = (bf16[128,1152]{1,0:T(8,128)(2,1)S(1)}, bf16[128,1152]{1,0:T(8,128)(2,1)S(1)}, u32[]{:S(2)}, u32[]{:S(2)}) collective-permute-start(bf16[128,1152]{1,0:T(8,128)(2,1)S(1)} %constant_dynamic-update-slice_fusion), channel_id=1, source_target_pairs={{0,4},{1,3},{2,6},{3,1},{4,0},{5,7},{6,2},{7,5},{8,12},{9,11},{10,... | collective-permute-start | bytes 884744 | tf_op jit(solution)/shard_map/ppermute | solution.py:306
  36.8 6.2 %collective-permute-start.10 = (bf16[256,1152]{1,0:T(8,128)(2,1)S(1)}, bf16[256,1152]{1,0:T(8,128)(2,1)S(1)}, u32[]{:S(2)}, u32[]{:S(2)}) collective-permute-start(bf16[256,1152]{1,0:T(8,128)(2,1)S(1)} %pad_maximum_fusion.1), channel_id=1, source_target_pairs={{0,1},{1,0},{2,3},{3,2},{4,5},{5,4},{6,7},{7,6},{8,9},{9,8},{10,11... | collective-permute-start | bytes 1769480 | tf_op jit(solution)/shard_map/ppermute | solution.py:306
  36.9 4.8 %collective-permute-start.11 = (bf16[128,1152]{1,0:T(8,128)(2,1)S(1)}, bf16[128,1152]{1,0:T(8,128)(2,1)S(1)}, u32[]{:S(2)}, u32[]{:S(2)}) collective-permute-start(bf16[128,1152]{1,0:T(8,128)(2,1)S(1)} %constant_dynamic-update-slice_fusion), channel_id=1, source_target_pairs={{0,1},{1,0},{2,3},{3,2},{4,5},{5,4},{6,7},{7,6},{8,9},{9,8},{10,11... | collective-permute-start | bytes 884744 | tf_op jit(solution)/shard_map/ppermute | solution.py:306
  41.6 1.5 %collective-permute-start.8 = (f32[40,1024]{1,0:T(8,128)S(1)}, f32[40,1024]{1,0:T(8,128)S(1)}, u32[]{:S(2)}, u32[]{:S(2)}) collective-permute-start(f32[40,1024]{1,0:T(8,128)S(1)} %get-tuple-element.13), channel_id=1, source_target_pairs={{0,1},{1,0},{2,3},{3,2},{4,5},{5,4},{6,7},{7,6},{8,9},{9,8},{10,11... | collective-permute-start | bytes 491528 | tf_op jit(solution)/shard_map/ppermute | solution.py:306

commit v3 on v2

v3 whole, which is shorter than its diff:
```python
import functools

import jax
import jax.numpy as jnp
from jax import lax
from jax.experimental import pallas as pl
from jax.experimental.pallas import tpu as pltpu
from jax.sharding import PartitionSpec as P

WEIGHT = 16.0
NEG = -1e30
LOG2E = 1.4426950408889634
CODES = 6
TILE = 256
CHUNK = 128
SPAN = 1024
ALL = ("batch", "temp")
SMEM = pl.BlockSpec(memory_space=pltpu.SMEM)
VMEM = pl.BlockSpec(memory_space=pltpu.VMEM)


def carried(count, body, carry):
    if count <= 8:
        for i in range(count):
            carry = body(i, carry)
        return carry
    return lax.fori_loop(0, count, body, carry)


def at(i, size):
    return pl.ds(i * size if isinstance(i, int) else pl.multiple_of(i * size, size), size)


def widths(code, width):
    root = jnp.sqrt(jnp.float32(width))
    return [jnp.exp2(0.5 * (code - jnp.float32(level))) / root for level in range(CODES)]


def powers(d, widest, wide):
    e = [None] * CODES
    e[5], e[4] = jnp.exp2(d * widest), jnp.exp2(d * wide)
    for level in (3, 2, 1, 0):
        e[level] = e[level + 2] * e[level + 2]
    return e


def columns(gram, count, bases):
    size = min(CHUNK, count)
    steps = count // size
    tile = gram.shape[1]
    best = carried(
        steps,
        lambda i, best: jnp.maximum(best, jnp.max(gram[at(i, size), :], axis=0, keepdims=True)),
        jnp.full((1, tile), NEG, jnp.float32),
    )

    def add(i, sums):
        e = powers(gram[at(i, size), :] - best, *bases)
        return tuple(s + jnp.sum(v, axis=0, keepdims=True) for s, v in zip(sums, e))

    return best, carried(steps, add, (jnp.zeros((1, tile), jnp.float32),) * CODES)


def times(a, b):
    return lax.dot_general(a, b, (((1,), (1,)), ((), ())), preferred_element_type=jnp.float32)


def hide_diagonal(gram, rows):
    square = gram[rows, :]
    own = lax.broadcasted_iota(jnp.int32, square.shape, 0) == lax.broadcasted_iota(
        jnp.int32, square.shape, 1
    )
    gram[rows, :] = jnp.where(own, NEG, square)


def bases_of(code, width):
    beta = widths(code.astype(jnp.float32), width)
    return beta[5] * LOG2E, beta[4] * LOG2E


def tiles(total):
    return [(i, min(TILE, total - i)) for i in range(0, total, TILE)]


def position():
    part = lax.axis_index("temp")
    return lax.axis_index("batch"), part // 2, part % 2


def spot(i, size):
    return pl.ds(pl.multiple_of(i * size, size), size)


def order_codes(spread, line, block):
    me, x, core = position()
    half = block // 2
    cut = [spread[:, spot(me ^ m, block)] for m in range(8)]
    cut[4:] = [jnp.where(x == 0, v, pltpu.roll(v, half, 1)) for v in cut[4:]]
    left = lax.broadcasted_iota(jnp.int32, cut[0].shape, 1) < half
    other = [None] * 4 + [pltpu.roll(v, half, 1) for v in cut[4:]]
    even = core == 0
    order = cut[:3] + [
        jnp.where(left, cut[4], other[6]),
        cut[3],
        jnp.where(left, other[4], other[5]),
        jnp.where(left, other[5], jnp.where(even, cut[6], other[7])),
        jnp.where(left, jnp.where(even, cut[7], other[6]), cut[7]),
    ]
    for m, v in enumerate(order):
        line[:, m * block : (m + 1) * block] = v


def first_kernel(staged, spread, *refs):
    me, x, core = position()
    if staged:
        *pieces, codes, stats, strip, whole, gram = refs
        block = pieces[0].shape[0]
        order_codes(spread, codes, block)
        row = 0
        for piece in pieces:
            whole[row : row + piece.shape[0], :] = piece[...]
            row += piece.shape[0]
        first_row = x * (block // 2)
    else:
        whole, stats, strip, gram = refs
        codes, block = spread, strip.shape[0] * 2
        first_row = me * block + x * (block // 2)
    total, width = whole.shape
    mine = pl.ds(pl.multiple_of(first_row, block // 2), block // 2)

    def tile(cols, size):
        part = gram.at[:, 0:size]
        part[...] = times(whole[...], whole[cols, :])
        hide_diagonal(part, cols)
        strip[:, cols] = part[mine, :]
        best, sums = columns(part, total, bases_of(codes[:, cols], width))
        stats[0:1, cols] = best
        for level in range(CODES):
            stats[1 + level : 2 + level, cols] = sums[level]
        stats[1 + CODES :, cols] = jnp.zeros((stats.shape[0] - 1 - CODES, size), jnp.float32)

    if total <= 4 * TILE:
        for start, size in tiles(total):
            tile(pl.ds(start, size), size)
    else:

        @pl.loop(0, total // TILE)
        def _(i):
            tile(at(i, TILE), TILE)


def swapped(a, block):
    left, right = a[:, -2 * block : -block], a[:, -block:]
    half = block // 2
    low = lax.broadcasted_iota(jnp.int32, left.shape, 1) < half
    return jnp.where(low, left, pltpu.roll(right, half, 1)), jnp.where(
        low, pltpu.roll(left, half, 1), right
    )


def add_rows(x, codes, early, late, before, stats, strip, gram):
    head, width = early.shape
    tail = late.shape[0]
    for start, size in tiles(tail):
        cols, lines = pl.ds(start, size), slice(head + start, head + start + size)
        part = gram.at[0 : head + tail, 0:size]
        part[0:head, :] = times(early[...], late[cols, :])
        part[head : head + tail, :] = times(late[...], late[cols, :])
        hide_diagonal(part, pl.ds(head + start, size))
        strip[:, lines] = part[spot(x, strip.shape[0]), :]
        best, sums = columns(part, head + tail, bases_of(codes[:, lines], width))
        stats[0:1, lines] = best
        for level in range(CODES):
            stats[1 + level : 2 + level, lines] = sums[level]
    for start, size in tiles(head):
        cols = pl.ds(start, size)
        part = gram.at[0:tail, 0:size]
        part[...] = times(late[...], early[cols, :])
        bases = bases_of(codes[:, cols], width)
        best, sums = columns(part, tail, bases)
        top = jnp.maximum(best, before[0:1, cols])
        was, now = powers(before[0:1, cols] - top, *bases), powers(best - top, *bases)
        stats[0:1, cols] = top
        for level in range(CODES):
            stats[1 + level : 2 + level, cols] = (
                before[1 + level : 2 + level, cols] * was[level] + sums[level] * now[level]
            )


def second_kernel(codes, early, before, part_strip, ny, fa, fb, ga, stats, strip, whole, gram):
    _, x, core = position()
    head, block = early.shape[0], ny.shape[0]
    half = block // 2
    late = whole.at[head:, :]
    late[0:block, :] = ny[...]
    late[spot(2 + core, half), :] = fa[0:half, :]
    late[spot(3 - core, half), :] = fb[0:half, :]
    late[4 * half : 5 * half, :] = fb[half : 2 * half, :]
    late[5 * half : 6 * half, :] = ga[...]
    whole[0:head, :] = early[...]
    strip[:, 0:head] = part_strip[...]
    add_rows(x, codes, early, late, before, stats, strip, gram)
    stats[1 + CODES :, :] = jnp.zeros((stats.shape[0] - 1 - CODES, stats.shape[1]), jnp.float32)


def third_kernel(
    codes, early, before, part_strip, level_index, fa, fb, late, keep, send, stats, strip, gram
):
    _, x, core = position()
    head, block = early.shape[0], late.shape[0]
    half = block // 4
    strip[:, 0:head] = part_strip[...]
    add_rows(x, codes, early, late, before, stats, strip, gram)
    lane = lax.broadcasted_iota(jnp.int32, (1, stats.shape[1]), 1)
    level = level_index[0].astype(jnp.float32)
    theirs = jnp.where(core == 0, fa[block // 2 : block // 2 + 1, 0:1], fb[block : block + 1, 0:1])
    stats[1 + CODES :, :] = jnp.where(lane < 128, level, theirs.astype(jnp.float32))
    keep[0:half, :] = strip[spot(core, half), :]
    send[0:half, :] = strip[spot(1 - core, half), :]
    keep[half:, :] = stats[...]
    send[half:, :] = stats[...]
    left, right = swapped(send[:, -2 * block :], block)
    send[:, -2 * block : -block] = left
    send[:, -block:] = right


class Mixer:
    def __init__(self, own, width, codes, keep, recv, turned):
        _, x, core = position()
        self.codes, self.width = codes, width
        self.rows = rows = keep.shape[0] - 8
        self.student = core == 1
        self.keep, self.recv = keep, recv
        block = 4 * rows
        own = spot(own, block)
        code = codes[:, own].astype(jnp.float32)
        turned[0] = self.pick(rows, rows + 8, own, True).T
        turned[1] = self.pick(rows, rows + 8, own, False).T
        turned[2] = jnp.broadcast_to(code, (8, block)).T
        mine = spot(2 * x + core, rows)
        s, t = turned[0, mine, :], turned[1, mine, :]
        self.beta = widths(turned[2, mine, 0:1], width)
        found = [
            ref[rows + 1 + CODES : rows + 2 + CODES, lane : lane + 1]
            for ref in (keep, recv)
            for lane in (0, 128)
        ]
        self.count = [sum(jnp.where(v == jnp.float32(c), 1.0, 0.0) for v in found) for c in range(CODES)]
        self.s_top, self.t_top = s[:, 0:1], t[:, 0:1]
        self.s_sum = [s[:, 1 + c : 2 + c] for c in range(CODES)]
        self.t_sum = [t[:, 1 + c : 2 + c] for c in range(CODES)]

    def pick(self, low, high, cols, student):
        here, there = self.keep[low:high, cols], self.recv[low:high, cols]
        return jnp.where(self.student == student, here, there)

    def weighted(self, d, beta, sums):
        e = powers(d, beta[5] * LOG2E, beta[4] * LOG2E)
        return sum(v * (n * b / s) for v, n, b, s in zip(e, self.count, beta, sums))

    def part(self, cols):
        rows = self.rows
        gs, gt = self.pick(0, rows, cols, True), self.pick(0, rows, cols, False)
        s, t = self.pick(rows, rows + 8, cols, True), self.pick(rows, rows + 8, cols, False)
        beta = widths(self.codes[:, cols].astype(jnp.float32), self.width)
        lines = lambda a: [a[1 + c : 2 + c] for c in range(CODES)]
        p_row = self.weighted(gt - self.t_top, self.beta, self.t_sum)
        q_row = self.weighted(gs - self.s_top, self.beta, self.s_sum)
        p_col = self.weighted(gt - t[0:1], beta, lines(t))
        q_col = self.weighted(gs - s[0:1], beta, lines(s))
        mix = WEIGHT * ((q_row - p_row) + (q_col - p_col))
        return mix.astype(jnp.bfloat16), jnp.sum(p_row * (gt - gs), axis=1, keepdims=True)

    def store_loss(self, loss, out):
        for c in range(CODES):
            loss = loss + self.count[c] * (
                self.beta[c] * (self.s_top - self.t_top)
                + (jnp.log(self.s_sum[c]) - jnp.log(self.t_sum[c]))
            )
        out[...] = jnp.broadcast_to(loss, (self.rows, 128)).T[0:1, :]


def product(a, b):
    return jnp.dot(a, b, preferred_element_type=jnp.float32)


def mix_kernel(codes, keep, recv, early, late, sooner, later, out, loss, turned, whole):
    mixer = Mixer(0, out.shape[1], codes, keep, recv, turned)
    head, total = early.shape[0], codes.shape[1]
    mix, gap = mixer.part(pl.ds(0, total))
    mixer.store_loss(gap, loss)

    @pl.when(mixer.student)
    def _():
        out[...] = product(mix[:, :head], early[...]) + product(mix[:, head:], late[...])

    @pl.when(jnp.logical_not(mixer.student))
    def _():
        half = late.shape[0] // 2
        for there, places in (
            (sooner, (0, 1, 4, 5, 2, 3, 6, 11, 7)),
            (later, (8, 9, 10, 12, 14, 13, 15)),
        ):
            for i, place in enumerate(places):
                whole[place * half : (place + 1) * half, :] = there[i * half : (i + 1) * half, :]
        out[...] = product(mix, whole[...])


def wide_mix_kernel(codes, keep, recv, student, out, loss, turned):
    total, width = student.shape
    mixer = Mixer(lax.axis_index("batch"), width, codes, keep, recv, turned)
    span = min(SPAN, total)

    def step(i, carry):
        mix, gap = mixer.part(at(i, span))
        return carry[0] + product(mix, student[at(i, span), :]), carry[1] + gap

    zero = jnp.zeros((mixer.rows, width), jnp.float32), jnp.zeros((mixer.rows, 1), jnp.float32)
    out[...], gap = lax.fori_loop(0, total // span, step, zero)
    mixer.store_loss(gap, loss)


def call(kernel, shapes, scratch, limit, *args):
    return pl.pallas_call(
        kernel,
        out_shape=shapes,
        in_specs=[SMEM if a.shape == (1,) else VMEM for a in args],
        out_specs=[VMEM] * len(shapes),
        scratch_shapes=scratch,
        compiler_params=pltpu.CompilerParams(vmem_limit_bytes=limit << 20),
    )(*args)


def join(parts, *behind):
    def kernel(*refs):
        row = 0
        for part in refs[: len(parts)]:
            refs[-1][row : row + part.shape[0], :] = part[...]
            row += part.shape[0]

    dims = sum(p.shape[0] for p in parts), parts[0].shape[1]
    return call(kernel, [shape(*dims, dtype=parts[0].dtype)], [], 16, *parts, *behind)[0]


def shape(*dims, dtype=jnp.float32):
    return jax.ShapeDtypeStruct(dims, dtype)


def shards(mesh, embeddings, spread_code, level_index):
    block, width = embeddings.shape[1:]
    batches, parts = mesh.shape["batch"], mesh.shape["temp"]
    total = block * batches
    me, part = lax.axis_index("batch"), lax.axis_index("temp")
    x, core = part // 2, part % 2
    rows, half = block // 2, block // 4

    def send(a, to):
        pairs = []
        for b in range(batches):
            for t in range(parts):
                there = to(b, t // 2, t % 2)
                pairs.append((b * parts + t, there[0] * parts + there[1] * 2 + there[2]))
        return lax.ppermute(a, ALL, pairs)

    over_core = lambda b, x, c: (b, x, 1 - c)
    over_x = lambda b, x, c: (b, 1 - x, c)
    u = lax.dynamic_index_in_dim(embeddings, core, 0, keepdims=False)
    out_shapes = [shape(half, width), shape(1, half)]
    codes = spread_code[None, :]

    if batches != 8 or parts != 4:
        whole = lax.all_gather(u, "batch", axis=0, tiled=True)
        theirs = send(level_index, over_x)
        stats, strip = call(
            functools.partial(first_kernel, False),
            [shape(8, total), shape(rows, total)],
            [pltpu.VMEM((total, TILE), jnp.float32)],
            56,
            codes,
            whole,
        )
        lane = jnp.arange(total)[None, :]
        line = jnp.where(lane < 128, level_index[0], theirs[0]).astype(jnp.float32)
        stats = jnp.concatenate([stats[: 1 + CODES], line])
        share = lambda c: lax.dynamic_slice_in_dim(strip, c * half, half)
        keep = jnp.concatenate([share(core), stats])
        recv = send(jnp.concatenate([share(1 - core), stats]), over_core)
        student = jnp.where(core == 1, whole, send(whole, over_core))
        out, loss = call(
            wide_mix_kernel,
            out_shapes,
            [pltpu.VMEM((3, block, 8), jnp.float32)],
            56,
            codes,
            keep,
            recv,
            student,
        )
        return out, loss[0]

    near = lambda b, x, c: (b ^ 2, x, c)
    far = lambda b, x, c: (b ^ 4, x, c)
    over_y = lambda b, x, c: (b ^ 1, x, c)
    turn = lambda b, x, c: (over_y if c else over_x)(b, x, c)
    return_turn = lambda b, x, c: (over_x if c else over_y)(b, x, c)
    level = jnp.broadcast_to(level_index.astype(jnp.bfloat16), (16, width))
    f = send(lax.dynamic_slice_in_dim(u, x * rows, rows, 0), far)
    n = send(u, near)
    y = send(u, over_y)
    g = send(f, near)
    ny = send(join([y], g), near)
    fa = send(join([f, level]), turn)
    fb = send(join([f, fa[:rows], level], g), return_turn)
    ga = send(g, turn)
    sooner = send(join([u, n, y, f, fa[:rows], g]), over_core)
    some, head = 4 * block, total - block
    codes, a_stats, a_strip, a_rows = call(
        functools.partial(first_kernel, True),
        [
            shape(1, total, dtype=jnp.int32),
            shape(8, some),
            shape(rows, some),
            shape(some, width, dtype=jnp.bfloat16),
        ],
        [pltpu.VMEM((some, TILE), jnp.float32)],
        16,
        codes,
        u,
        y,
        n,
        f,
        g,
    )
    gb = send(join([g, ga], sooner, a_stats), return_turn)
    b_stats, b_strip, b_rows = call(
        second_kernel,
        [shape(8, head), shape(rows, head), shape(head, width, dtype=jnp.bfloat16)],
        [pltpu.VMEM((head, TILE), jnp.float32)],
        16,
        codes,
        a_rows,
        a_stats,
        a_strip,
        ny,
        fa,
        fb,
        ga,
    )
    later = send(join([ny, fb[:block], ga, gb], b_stats), over_core)
    keep, mail = call(
        third_kernel,
        [shape(half + 8, total), shape(half + 8, total)],
        [
            pltpu.VMEM((8, total), jnp.float32),
            pltpu.VMEM((rows, total), jnp.float32),
            pltpu.VMEM((total, TILE), jnp.float32),
        ],
        16,
        codes,
        b_rows,
        b_stats,
        b_strip,
        level_index,
        fa,
        fb,
        gb,
    )
    recv = send(mail, over_core)
    out, loss = call(
        mix_kernel,
        out_shapes,
        [pltpu.VMEM((3, block, 8), jnp.float32), pltpu.VMEM((total, width), jnp.bfloat16)],
        16,
        codes,
        keep,
        recv,
        b_rows,
        gb,
        sooner,
        later,
    )
    return out, loss[0]


def solution(mesh):
    in_specs = (P(None, "batch", None), P(), P("temp"))
    out_specs = (P(("batch", "temp"), None), P(("batch", "temp")))
    return jax.shard_map(
        functools.partial(shards, mesh),
        mesh=mesh,
        in_specs=in_specs,
        out_specs=out_specs,
        check_vma=False,
    )
```

time: 45.8 us -> 41 us (0.90)
  starting transfers between devices: 16.9 us -> 13.5 us
  Pallas kernels: 9.67 us -> 8.89 us
    ppermute x12, starting transfers between devices: 16.9 us -> 13.5 us  [send(): return lax.ppermute(a, ALL, pairs)]
    pallas_call x3 -> x10, Pallas kernels: 9.67 us -> 8.89 us  [call(): pl.pallas_call(kernel, out_shape=shapes, in_specs=[SMEM if a.shape == (1,...]
    unnamed x5 -> x4, local copies, waits for them, and re-layouts: 1.05 us -> 1.04 us
  transfers between devices with their start and end apart: 12 -> 12, of which waited for: 4 -> 8; matrix products, arithmetic and copies ran while one was open for 1% -> 0% of each run, Pallas kernels for 16% -> 16%
where the time goes in v3:
time: 41 us; the launch traced here: 40.9 us
  waiting for transfers between devices  15.8 us (39%)
  starting transfers between devices  13.5 us (33%)
  Pallas kernels  8.89 us (22%)
  between operations  1.43 us (3%)
  local copies, waits for them, and re-layouts  1.14 us (3%)
    ppermute x12, waiting for transfers between devices, send(): return lax.ppermute(a, ALL, pairs)  15.8 us
    ppermute x12, starting transfers between devices, send(): return lax.ppermute(a, ALL, pairs)  13.5 us
    pallas_call x10, Pallas kernels, call(): pl.pallas_call(kernel, out_shape=shapes, in_specs=[SMEM if a.shape == (1,...  8.89 us
    unnamed x4, local copies, waits for them, and re-layouts  1.04 us
  transfers between devices with their start and end apart: 12, of which 8 were waited for; matrix products, arithmetic and copies ran while one was open for 0% of the time, Pallas kernels for 16%

profile of v3, /device:TPU:0, one launch (start us, length us, event | category | flops | bytes accessed | tf_op | source)
XLA Modules:
  0.0 40.9 jit_solution(7693694089017160959)
XLA Ops:
  0.6 0.0 copy-start
  0.7 1.0 %copy-done = bf16[2,128,1152]{2,1,0:T(8,128)(2,1)S(1)} copy-done((bf16[2,128,1152]{2,1,0:T(8,128)(2,1)S(1)}, bf16[2,128,1152]{2,1,0:T(8,128)(2,1)}, u32[]{:S(2)}) %copy-start) | copy-done | bytes 589848
  1.7 4.1 %collective-permute-start.2 = (bf16[64,1152]{1,0:T(8,128)(2,1)S(1)}, bf16[64,1152]{1,0:T(8,128)(2,1)S(1)}, u32[]{:S(2)}, u32[]{:S(2)}) collective-permute-start(bf16[64,1152]{1,0:T(8,128)(2,1)S(1)} %dynamic-slice_bitcast_fusion.1), channel_id=1, source_target_pairs={{0,16},{1,17},{2,18},{3,19},{4,20},{5,21},{6,22},{7,23},{8,24},{9,... | collective-permute-start | bytes 442376 | tf_op jit(solution)/shard_map/ppermute | solution.py:363
  5.9 1.6 %collective-permute-start = (bf16[128,1152]{1,0:T(8,128)(2,1)S(1)}, bf16[128,1152]{1,0:T(8,128)(2,1)S(1)}, u32[]{:S(2)}, u32[]{:S(2)}) collective-permute-start(bf16[128,1152]{1,0:T(8,128)(2,1)S(1)} %dynamic-slice_bitcast_fusion.refs_0_), channel_id=1, source_target_pairs={{0,4},{1,5},{2,6},{3,7},{4,0},{5,1},{6,2},{7,3},{8,12},{9,13},{10,... | collective-permute-start | bytes 884744 | tf_op jit(solution)/shard_map/ppermute | solution.py:363
  7.5 1.6 %collective-permute-start.1 = (bf16[128,1152]{1,0:T(8,128)(2,1)S(1)}, bf16[128,1152]{1,0:T(8,128)(2,1)S(1)}, u32[]{:S(2)}, u32[]{:S(2)}) collective-permute-start(bf16[128,1152]{1,0:T(8,128)(2,1)S(1)} %dynamic-slice_bitcast_fusion.refs_0_), channel_id=1, source_target_pairs={{0,8},{1,9},{2,10},{3,11},{4,12},{5,13},{6,14},{7,15},{8,0},{9,1},... | collective-permute-start | bytes 884744 | tf_op jit(solution)/shard_map/ppermute | solution.py:363
  9.7 3.3 %collective-permute-done.2.refs_3_.refs_0_ = bf16[64,1152]{1,0:T(8,128)(2,1)S(1)} collective-permute-done((bf16[64,1152]{1,0:T(8,128)(2,1)S(1)}, bf16[64,1152]{1,0:T(8,128)(2,1)S(1)}, u32[]{:S(2)}, u32[]{:S(2)}) %collective-permute-start.2) | collective-permute-done | bytes 147488 | tf_op jit(solution)/shard_map/ppermute | solution.py:363
  13.0 1.6 %collective-permute-start.5 = (bf16[80,1152]{1,0:T(8,128)(2,1)S(1)}, bf16[80,1152]{1,0:T(8,128)(2,1)S(1)}, u32[]{:S(2)}, u32[]{:S(2)}) collective-permute-start(bf16[80,1152]{1,0:T(8,128)(2,1)S(1)} %shard_map.52), channel_id=1, source_target_pairs={{0,2},{1,5},{2,0},{3,7},{4,6},{5,1},{6,4},{7,3},{8,10},{9,13},{10,... | collective-permute-start | bytes 552968 | tf_op jit(solution)/shard_map/ppermute | solution.py:363
  14.6 0.6 %collective-permute-start.3 = (bf16[64,1152]{1,0:T(8,128)(2,1)S(1)}, bf16[64,1152]{1,0:T(8,128)(2,1)S(1)}, u32[]{:S(2)}, u32[]{:S(2)}) collective-permute-start(bf16[64,1152]{1,0:T(8,128)(2,1)S(1)} %collective-permute-done.2.refs_3_.refs_0_), channel_id=1, source_target_pairs={{0,8},{1,9},{2,10},{3,11},{4,12},{5,13},{6,14},{7,15},{8,0},{9,1},... | collective-permute-start | bytes 442376 | tf_op jit(solution)/shard_map/ppermute | solution.py:363
  15.2 3.4 %collective-permute-done.5.fa = bf16[80,1152]{1,0:T(8,128)(2,1)S(1)} collective-permute-done((bf16[80,1152]{1,0:T(8,128)(2,1)S(1)}, bf16[80,1152]{1,0:T(8,128)(2,1)S(1)}, u32[]{:S(2)}, u32[]{:S(2)}) %collective-permute-start.5) | collective-permute-done | bytes 184352 | tf_op jit(solution)/shard_map/ppermute | solution.py:363
  18.6 0.0 collective-permute-done.refs_1_.refs_0_.refs_2_
  18.6 0.2 collective-permute-done.1.refs_2_.refs_1_
  18.8 2.0 %collective-permute-done.3.refs_4_.refs_1_.refs_3_.refs_5_.refs_0_ = bf16[64,1152]{1,0:T(8,128)(2,1)S(1)} collective-permute-done((bf16[64,1152]{1,0:T(8,128)(2,1)S(1)}, bf16[64,1152]{1,0:T(8,128)(2,1)S(1)}, u32[]{:S(2)}, u32[]{:S(2)}) %collective-permute-start.3) | collective-permute-done | bytes 147488 | tf_op jit(solution)/shard_map/ppermute | solution.py:363
  20.8 0.1 shard_map.55
  20.9 0.0 copy-start.1
  20.9 0.1 collective-permute-start.8
  21.0 1.6 %collective-permute-start.7 = (bf16[64,1152]{1,0:T(8,128)(2,1)S(1)}, bf16[64,1152]{1,0:T(8,128)(2,1)S(1)}, u32[]{:S(2)}, u32[]{:S(2)}) collective-permute-start(bf16[64,1152]{1,0:T(8,128)(2,1)S(1)} %collective-permute-done.3.refs_4_.refs_1_.refs_3_.refs_5_.refs_0_), channel_id=1, source_target_pairs={{0,2},{1,5},{2,0},{3,7},{4,6},{5,1},{6,4},{7,3},{8,10},{9,13},{10,... | collective-permute-start | bytes 442376 | tf_op jit(solution)/shard_map/ppermute | solution.py:363
  22.6 0.6 %collective-permute-start.6 = (bf16[144,1152]{1,0:T(8,128)(2,1)S(1)}, bf16[144,1152]{1,0:T(8,128)(2,1)S(1)}, u32[]{:S(2)}, u32[]{:S(2)}) collective-permute-start(bf16[144,1152]{1,0:T(8,128)(2,1)S(1)} %shard_map.53), channel_id=1, source_target_pairs={{0,4},{1,3},{2,6},{3,1},{4,0},{5,7},{6,2},{7,5},{8,12},{9,11},{10,... | collective-permute-start | bytes 995336 | tf_op jit(solution)/shard_map/ppermute | solution.py:363
  23.2 1.2 %collective-permute-start.4 = (bf16[128,1152]{1,0:T(8,128)(2,1)S(1)}, bf16[128,1152]{1,0:T(8,128)(2,1)S(1)}, u32[]{:S(2)}, u32[]{:S(2)}) collective-permute-start(bf16[128,1152]{1,0:T(8,128)(2,1)S(1)} %shard_map.51), channel_id=1, source_target_pairs={{0,8},{1,9},{2,10},{3,11},{4,12},{5,13},{6,14},{7,15},{8,0},{9,1},... | collective-permute-start | bytes 884744 | tf_op jit(solution)/shard_map/ppermute | solution.py:363
  24.4 0.0 copy-done.1
  24.4 1.6 %shard_map.50 = (s32[1,1024]{1,0:T(1,128)S(1)}, f32[8,512]{1,0:T(8,128)S(1)}, f32[64,512]{1,0:T(8,128)S(1)}, bf16[512,1152]{1,0:T(8,128)(2,1)S(1)}) custom-call(s32[1,1024]{1,0:T(1,128)S(1)} %bitcast.7, bf16[128,1152]{1,0:T(8,128)(2,1)S(1)} %dynamic-slice_bitcast_fusion.refs_0_, bf16[128,1152]{1,0:T(8,128)(2,1)S(1)} %collective-permute-done.refs_1_.refs_0_.refs_2_, ...), custom_call_target="tpu_custom_call" | custom-call | tf_op jit(solution)/shard_map/pallas_call | solution.py:324
  26.0 1.8 %collective-permute-done.7.ga.refs_1_.refs_2_ = bf16[64,1152]{1,0:T(8,128)(2,1)S(1)} collective-permute-done((bf16[64,1152]{1,0:T(8,128)(2,1)S(1)}, bf16[64,1152]{1,0:T(8,128)(2,1)S(1)}, u32[]{:S(2)}, u32[]{:S(2)}) %collective-permute-start.7) | collective-permute-done | bytes 147488 | tf_op jit(solution)/shard_map/ppermute | solution.py:363
  27.8 0.0 collective-permute-done.8.refs_2_.sooner
  27.8 0.1 collective-permute-start.9
  27.9 1.9 %collective-permute-done.6.fb = bf16[144,1152]{1,0:T(8,128)(2,1)S(1)} collective-permute-done((bf16[144,1152]{1,0:T(8,128)(2,1)S(1)}, bf16[144,1152]{1,0:T(8,128)(2,1)S(1)}, u32[]{:S(2)}, u32[]{:S(2)}) %collective-permute-start.6) | collective-permute-done | bytes 331808 | tf_op jit(solution)/shard_map/ppermute | solution.py:363
  29.8 2.2 %collective-permute-done.4.ny.refs_0_ = bf16[128,1152]{1,0:T(8,128)(2,1)S(1)} collective-permute-done((bf16[128,1152]{1,0:T(8,128)(2,1)S(1)}, bf16[128,1152]{1,0:T(8,128)(2,1)S(1)}, u32[]{:S(2)}, u32[]{:S(2)}) %collective-permute-start.4) | collective-permute-done | bytes 294944 | tf_op jit(solution)/shard_map/ppermute | solution.py:363
  32.1 3.0 %shard_map.54 = (f32[8,896]{1,0:T(8,128)S(1)}, f32[64,896]{1,0:T(8,128)S(1)}, bf16[896,1152]{1,0:T(8,128)(2,1)S(1)}) custom-call(s32[1,1024]{1,0:T(1,128)S(1)} %get-tuple-element.13.codes, bf16[512,1152]{1,0:T(8,128)(2,1)S(1)} %get-tuple-element.14.early, f32[8,512]{1,0:T(8,128)S(1)} %get-tuple-element.15.before.refs_3_, ...), custom_call_target="tpu_custom_call" | custom-call | tf_op jit(solution)/shard_map/pallas_call | solution.py:324
  35.1 0.0 collective-permute-done.9.late.refs_3_
  35.1 0.1 shard_map.58
  35.2 0.1 collective-permute-start.11
  35.3 2.0 %shard_map.57 = (f32[40,1024]{1,0:T(8,128)S(1)}, f32[40,1024]{1,0:T(8,128)S(1)}) custom-call(s32[1,1024]{1,0:T(1,128)S(1)} %get-tuple-element.13.codes, bf16[896,1152]{1,0:T(8,128)(2,1)S(1)} %get-tuple-element.17.early, f32[8,896]{1,0:T(8,128)S(1)} %get-tuple-element.18.before.refs_4_, f32[64,896]{1,0:T(8,128)S(1)} %get-tuple-element.19.part_strip, ...), custom_call_target="tpu_custom_call" | custom-call | tf_op jit(solution)/shard_map/pallas_call | solution.py:324
  37.3 0.5 %collective-permute-start.10 = (f32[40,1024]{1,0:T(8,128)S(1)}, f32[40,1024]{1,0:T(8,128)S(1)}, u32[]{:S(2)}, u32[]{:S(2)}) collective-permute-start(f32[40,1024]{1,0:T(8,128)S(1)} %get-tuple-element.21), channel_id=1, source_target_pairs={{0,1},{1,0},{2,3},{3,2},{4,5},{5,4},{6,7},{7,6},{8,9},{9,8},{10,11... | collective-permute-start | bytes 491528 | tf_op jit(solution)/shard_map/ppermute | solution.py:363
  37.8 1.0 %collective-permute-done.10.recv = f32[40,1024]{1,0:T(8,128)S(1)} collective-permute-done((f32[40,1024]{1,0:T(8,128)S(1)}, f32[40,1024]{1,0:T(8,128)S(1)}, u32[]{:S(2)}, u32[]{:S(2)}) %collective-permute-start.10) | collective-permute-done | bytes 163872 | tf_op jit(solution)/shard_map/ppermute | solution.py:363
  38.8 0.0 collective-permute-done.11.later
  38.8 2.1 %shard_map.59 = (f32[32,1152]{1,0:T(8,128)}, f32[1,32]{1,0:T(1,128)}) custom-call(s32[1,1024]{1,0:T(1,128)S(1)} %get-tuple-element.13.codes, f32[40,1024]{1,0:T(8,128)S(1)} %get-tuple-element.20.keep, f32[40,1024]{1,0:T(8,128)S(1)} %collective-permute-done.10.recv, bf16[896,1152]{1,0:T(8,128)(2,1)S(1)} %get-tuple-element.17.early, ...), custom_call_target="tpu_custom_call" | custom-call | tf_op jit(solution)/shard_map/pallas_call | solution.py:324
  (9 shorter events, 0.2 us)
Async XLA Ops:
  0.6 1.1 %copy-start = (bf16[2,128,1152]{2,1,0:T(8,128)(2,1)S(1)}, bf16[2,128,1152]{2,1,0:T(8,128)(2,1)}, u32[]{:S(2)}) copy-start(bf16[2,128,1152]{2,1,0:T(8,128)(2,1)} %param.3) | copy-start | bytes 1769476
  1.7 11.2 %collective-permute-start.2 = (bf16[64,1152]{1,0:T(8,128)(2,1)S(1)}, bf16[64,1152]{1,0:T(8,128)(2,1)S(1)}, u32[]{:S(2)}, u32[]{:S(2)}) collective-permute-start(bf16[64,1152]{1,0:T(8,128)(2,1)S(1)} %dynamic-slice_bitcast_fusion.1), channel_id=1, source_target_pairs={{0,16},{1,17},{2,18},{3,19},{4,20},{5,21},{6,22},{7,23},{8,24},{9,... | collective-permute-start | bytes 442376 | tf_op jit(solution)/shard_map/ppermute | solution.py:363
  5.9 12.7 %collective-permute-start = (bf16[128,1152]{1,0:T(8,128)(2,1)S(1)}, bf16[128,1152]{1,0:T(8,128)(2,1)S(1)}, u32[]{:S(2)}, u32[]{:S(2)}) collective-permute-start(bf16[128,1152]{1,0:T(8,128)(2,1)S(1)} %dynamic-slice_bitcast_fusion.refs_0_), channel_id=1, source_target_pairs={{0,4},{1,5},{2,6},{3,7},{4,0},{5,1},{6,2},{7,3},{8,12},{9,13},{10,... | collective-permute-start | bytes 884744 | tf_op jit(solution)/shard_map/ppermute | solution.py:363
  7.5 11.3 %collective-permute-start.1 = (bf16[128,1152]{1,0:T(8,128)(2,1)S(1)}, bf16[128,1152]{1,0:T(8,128)(2,1)S(1)}, u32[]{:S(2)}, u32[]{:S(2)}) collective-permute-start(bf16[128,1152]{1,0:T(8,128)(2,1)S(1)} %dynamic-slice_bitcast_fusion.refs_0_), channel_id=1, source_target_pairs={{0,8},{1,9},{2,10},{3,11},{4,12},{5,13},{6,14},{7,15},{8,0},{9,1},... | collective-permute-start | bytes 884744 | tf_op jit(solution)/shard_map/ppermute | solution.py:363
  13.0 5.6 %collective-permute-start.5 = (bf16[80,1152]{1,0:T(8,128)(2,1)S(1)}, bf16[80,1152]{1,0:T(8,128)(2,1)S(1)}, u32[]{:S(2)}, u32[]{:S(2)}) collective-permute-start(bf16[80,1152]{1,0:T(8,128)(2,1)S(1)} %shard_map.52), channel_id=1, source_target_pairs={{0,2},{1,5},{2,0},{3,7},{4,6},{5,1},{6,4},{7,3},{8,10},{9,13},{10,... | collective-permute-start | bytes 552968 | tf_op jit(solution)/shard_map/ppermute | solution.py:363
  14.6 6.2 %collective-permute-start.3 = (bf16[64,1152]{1,0:T(8,128)(2,1)S(1)}, bf16[64,1152]{1,0:T(8,128)(2,1)S(1)}, u32[]{:S(2)}, u32[]{:S(2)}) collective-permute-start(bf16[64,1152]{1,0:T(8,128)(2,1)S(1)} %collective-permute-done.2.refs_3_.refs_0_), channel_id=1, source_target_pairs={{0,8},{1,9},{2,10},{3,11},{4,12},{5,13},{6,14},{7,15},{8,0},{9,1},... | collective-permute-start | bytes 442376 | tf_op jit(solution)/shard_map/ppermute | solution.py:363
  20.9 3.5 %copy-start.1 = (s32[1024]{0:T(1024)S(1)}, s32[1024]{0:T(1024)}, u32[]{:S(2)}) copy-start(s32[1024]{0:T(1024)} %param.4) | copy-start | bytes 12292
  20.9 6.9 %collective-permute-start.8 = (bf16[576,1152]{1,0:T(8,128)(2,1)S(1)}, bf16[576,1152]{1,0:T(8,128)(2,1)S(1)}, u32[]{:S(2)}, u32[]{:S(2)}) collective-permute-start(bf16[576,1152]{1,0:T(8,128)(2,1)S(1)} %shard_map.55), channel_id=1, source_target_pairs={{0,1},{1,0},{2,3},{3,2},{4,5},{5,4},{6,7},{7,6},{8,9},{9,8},{10,11... | collective-permute-start | bytes 3981320 | tf_op jit(solution)/shard_map/ppermute | solution.py:363
  21.0 6.8 %collective-permute-start.7 = (bf16[64,1152]{1,0:T(8,128)(2,1)S(1)}, bf16[64,1152]{1,0:T(8,128)(2,1)S(1)}, u32[]{:S(2)}, u32[]{:S(2)}) collective-permute-start(bf16[64,1152]{1,0:T(8,128)(2,1)S(1)} %collective-permute-done.3.refs_4_.refs_1_.refs_3_.refs_5_.refs_0_), channel_id=1, source_target_pairs={{0,2},{1,5},{2,0},{3,7},{4,6},{5,1},{6,4},{7,3},{8,10},{9,13},{10,... | collective-permute-start | bytes 442376 | tf_op jit(solution)/shard_map/ppermute | solution.py:363
  22.6 7.2 %collective-permute-start.6 = (bf16[144,1152]{1,0:T(8,128)(2,1)S(1)}, bf16[144,1152]{1,0:T(8,128)(2,1)S(1)}, u32[]{:S(2)}, u32[]{:S(2)}) collective-permute-start(bf16[144,1152]{1,0:T(8,128)(2,1)S(1)} %shard_map.53), channel_id=1, source_target_pairs={{0,4},{1,3},{2,6},{3,1},{4,0},{5,7},{6,2},{7,5},{8,12},{9,11},{10,... | collective-permute-start | bytes 995336 | tf_op jit(solution)/shard_map/ppermute | solution.py:363
  23.2 8.8 %collective-permute-start.4 = (bf16[128,1152]{1,0:T(8,128)(2,1)S(1)}, bf16[128,1152]{1,0:T(8,128)(2,1)S(1)}, u32[]{:S(2)}, u32[]{:S(2)}) collective-permute-start(bf16[128,1152]{1,0:T(8,128)(2,1)S(1)} %shard_map.51), channel_id=1, source_target_pairs={{0,8},{1,9},{2,10},{3,11},{4,12},{5,13},{6,14},{7,15},{8,0},{9,1},... | collective-permute-start | bytes 884744 | tf_op jit(solution)/shard_map/ppermute | solution.py:363
  27.8 7.3 %collective-permute-start.9 = (bf16[128,1152]{1,0:T(8,128)(2,1)S(1)}, bf16[128,1152]{1,0:T(8,128)(2,1)S(1)}, u32[]{:S(2)}, u32[]{:S(2)}) collective-permute-start(bf16[128,1152]{1,0:T(8,128)(2,1)S(1)} %shard_map.56), channel_id=1, source_target_pairs={{0,4},{1,3},{2,6},{3,1},{4,0},{5,7},{6,2},{7,5},{8,12},{9,11},{10,... | collective-permute-start | bytes 884744 | tf_op jit(solution)/shard_map/ppermute | solution.py:363
  35.2 3.6 %collective-permute-start.11 = (bf16[448,1152]{1,0:T(8,128)(2,1)S(1)}, bf16[448,1152]{1,0:T(8,128)(2,1)S(1)}, u32[]{:S(2)}, u32[]{:S(2)}) collective-permute-start(bf16[448,1152]{1,0:T(8,128)(2,1)S(1)} %shard_map.58), channel_id=1, source_target_pairs={{0,1},{1,0},{2,3},{3,2},{4,5},{5,4},{6,7},{7,6},{8,9},{9,8},{10,11... | collective-permute-start | bytes 3096584 | tf_op jit(solution)/shard_map/ppermute | solution.py:363
  37.3 1.5 %collective-permute-start.10 = (f32[40,1024]{1,0:T(8,128)S(1)}, f32[40,1024]{1,0:T(8,128)S(1)}, u32[]{:S(2)}, u32[]{:S(2)}) collective-permute-start(f32[40,1024]{1,0:T(8,128)S(1)} %get-tuple-element.21), channel_id=1, source_target_pairs={{0,1},{1,0},{2,3},{3,2},{4,5},{5,4},{6,7},{7,6},{8,9},{9,8},{10,11... | collective-permute-start | bytes 491528 | tf_op jit(solution)/shard_map/ppermute | solution.py:363

commit v4 on v3

--- a/solution.py
+++ b/solution.py
@@ -101,9 +101,9 @@
     even = core == 0
     order = cut[:3] + [
         jnp.where(left, cut[4], other[6]),
-        cut[3],
         jnp.where(left, other[4], other[5]),
         jnp.where(left, other[5], jnp.where(even, cut[6], other[7])),
+        cut[3],
         jnp.where(left, jnp.where(even, cut[7], other[6]), cut[7]),
     ]
     for m, v in enumerate(order):
@@ -128,8 +128,8 @@
     total, width = whole.shape
     mine = pl.ds(pl.multiple_of(first_row, block // 2), block // 2)
 
-    def tile(cols, size):
-        part = gram.at[:, 0:size]
+    def tile(cols, size, slot=0):
+        part = gram.at[slot, :, 0:size]
         part[...] = times(whole[...], whole[cols, :])
         hide_diagonal(part, cols)
         strip[:, cols] = part[mine, :]
@@ -139,9 +139,9 @@
             stats[1 + level : 2 + level, cols] = sums[level]
         stats[1 + CODES :, cols] = jnp.zeros((stats.shape[0] - 1 - CODES, size), jnp.float32)
 
-    if total <= 4 * TILE:
-        for start, size in tiles(total):
-            tile(pl.ds(start, size), size)
+    if staged:
+        for slot, (start, size) in enumerate(tiles(total)):
+            tile(pl.ds(start, size), size, slot)
     else:
 
         @pl.loop(0, total // TILE)
@@ -150,7 +150,7 @@
 
 
 def swapped(a, block):
-    left, right = a[:, -2 * block : -block], a[:, -block:]
+    left, right = a[:, -3 * block : -2 * block], a[:, -block:]
     half = block // 2
     low = lax.broadcasted_iota(jnp.int32, left.shape, 1) < half
     return jnp.where(low, left, pltpu.roll(right, half, 1)), jnp.where(
@@ -158,12 +158,16 @@
     )
 
 
-def add_rows(x, codes, early, late, before, stats, strip, gram):
+def slots(rows, cols):
+    return pltpu.VMEM((len(tiles(cols)), rows, min(cols, TILE)), jnp.float32)
+
+
+def add_rows(x, codes, early, late, before, stats, strip, gram, wide):
     head, width = early.shape
     tail = late.shape[0]
-    for start, size in tiles(tail):
+    for slot, (start, size) in enumerate(tiles(tail)):
         cols, lines = pl.ds(start, size), slice(head + start, head + start + size)
-        part = gram.at[0 : head + tail, 0:size]
+        part = gram.at[slot, :, 0:size]
         part[0:head, :] = times(early[...], late[cols, :])
         part[head : head + tail, :] = times(late[...], late[cols, :])
         hide_diagonal(part, pl.ds(head + start, size))
@@ -172,9 +176,9 @@
         stats[0:1, lines] = best
         for level in range(CODES):
             stats[1 + level : 2 + level, lines] = sums[level]
-    for start, size in tiles(head):
+    for slot, (start, size) in enumerate(tiles(head)):
         cols = pl.ds(start, size)
-        part = gram.at[0:tail, 0:size]
+        part = wide.at[slot, :, 0:size]
         part[...] = times(late[...], early[cols, :])
         bases = bases_of(codes[:, cols], width)
         best, sums = columns(part, tail, bases)
@@ -187,40 +191,74 @@
             )
 
 
-def second_kernel(codes, early, before, part_strip, ny, fa, fb, ga, stats, strip, whole, gram):
+def second_kernel(codes, early, before, part_strip, fa, fb, ga, stats, strip, whole, gram, wide):
     _, x, core = position()
-    head, block = early.shape[0], ny.shape[0]
-    half = block // 2
+    head, half = early.shape[0], ga.shape[0]
     late = whole.at[head:, :]
-    late[0:block, :] = ny[...]
-    late[spot(2 + core, half), :] = fa[0:half, :]
-    late[spot(3 - core, half), :] = fb[0:half, :]
-    late[4 * half : 5 * half, :] = fb[half : 2 * half, :]
-    late[5 * half : 6 * half, :] = ga[...]
+    late[spot(core, half), :] = fa[0:half, :]
+    late[spot(1 - core, half), :] = fb[0:half, :]
+    late[2 * half : 3 * half, :] = fb[half : 2 * half, :]
+    late[3 * half : 4 * half, :] = ga[...]
     whole[0:head, :] = early[...]
     strip[:, 0:head] = part_strip[...]
-    add_rows(x, codes, early, late, before, stats, strip, gram)
+    add_rows(x, codes, early, late, before, stats, strip, gram, wide)
     stats[1 + CODES :, :] = jnp.zeros((stats.shape[0] - 1 - CODES, stats.shape[1]), jnp.float32)
 
 
-def third_kernel(
-    codes, early, before, part_strip, level_index, fa, fb, late, keep, send, stats, strip, gram
+def third_kernel(codes, early, before, part_strip, late, stats, strip, gram, wide):
+    _, x, _ = position()
+    strip[:, 0 : early.shape[0]] = part_strip[...]
+    add_rows(x, codes, early, late, before, stats, strip, gram, wide)
+    stats[1 + CODES :, :] = jnp.zeros((stats.shape[0] - 1 - CODES, stats.shape[1]), jnp.float32)
+
+
+def last_kernel(
+    codes, early, middle, before, strip, level_index, fa, fb, late, keep, send, wide, square
 ):
     _, x, core = position()
-    head, block = early.shape[0], late.shape[0]
+    block, width = late.shape
     half = block // 4
-    strip[:, 0:head] = part_strip[...]
-    add_rows(x, codes, early, late, before, stats, strip, gram)
-    lane = lax.broadcasted_iota(jnp.int32, (1, stats.shape[1]), 1)
+    head = before.shape[1]
+    last = slice(head, head + block)
+    wide[:, 0 : early.shape[0]] = times(late[...], early[...])
+    wide[:, early.shape[0] : head] = times(late[...], middle[...])
+    gram = times(late[...], late[...])
+    lines, lanes = (lax.broadcasted_iota(jnp.int32, gram.shape, axis) for axis in (0, 1))
+    wide[:, last] = jnp.where(lines == lanes, NEG, gram)
+    square[...] = jnp.broadcast_to(codes[:, last], (8, block)).astype(jnp.float32).T
+    bases = bases_of(square[:, 0:1], width)
+    best = jnp.max(wide[...], axis=1, keepdims=True)
+    part = powers(wide[...] - best, *bases)
+    square[:, 0:1] = best
+    for level in range(CODES):
+        square[:, 1 + level : 2 + level] = jnp.sum(part[level], axis=1, keepdims=True)
+    keep[half:, last] = square[...].T
+    for start, size in tiles(head):
+        cols = pl.ds(start, size)
+        bases = bases_of(codes[:, cols], width)
+        best, sums = columns(wide.at[:, cols], block, bases)
+        top = jnp.maximum(best, before[0:1, cols])
+        was, now = powers(before[0:1, cols] - top, *bases), powers(best - top, *bases)
+        keep[half : half + 1, cols] = top
+        for level in range(CODES):
+            keep[half + 1 + level : half + 2 + level, cols] = (
+                before[1 + level : 2 + level, cols] * was[level] + sums[level] * now[level]
+            )
+    lane = lax.broadcasted_iota(jnp.int32, (1, head + block), 1)
     level = level_index[0].astype(jnp.float32)
     theirs = jnp.where(core == 0, fa[block // 2 : block // 2 + 1, 0:1], fb[block : block + 1, 0:1])
-    stats[1 + CODES :, :] = jnp.where(lane < 128, level, theirs.astype(jnp.float32))
-    keep[0:half, :] = strip[spot(core, half), :]
-    send[0:half, :] = strip[spot(1 - core, half), :]
-    keep[half:, :] = stats[...]
-    send[half:, :] = stats[...]
-    left, right = swapped(send[:, -2 * block :], block)
-    send[:, -2 * block : -block] = left
+    keep[half + 1 + CODES :, :] = jnp.where(lane < 128, level, theirs.astype(jnp.float32))
+    square_t = wide[:, 0:block].T
+    for ref, share in ((keep, core), (send, 1 - core)):
+        ref[0:half, 0:head] = strip[spot(share, half), :]
+        here = jnp.where(share == 0, square_t[0:half], square_t[half : 2 * half])
+        there = jnp.where(
+            share == 0, square_t[2 * half : 3 * half], square_t[3 * half : 4 * half]
+        )
+        ref[0:half, last] = jnp.where(x == 0, here, there)
+    send[half:, :] = keep[half:, :]
+    left, right = swapped(send, block)
+    send[:, -3 * block : -2 * block] = left
     send[:, -block:] = right
 
 
@@ -284,26 +322,25 @@
     return jnp.dot(a, b, preferred_element_type=jnp.float32)
 
 
-def mix_kernel(codes, keep, recv, early, late, sooner, later, out, loss, turned, whole):
+def mix_kernel(codes, keep, recv, early, middle, late, sooner, later, out, loss, turned):
     mixer = Mixer(0, out.shape[1], codes, keep, recv, turned)
-    head, total = early.shape[0], codes.shape[1]
-    mix, gap = mixer.part(pl.ds(0, total))
+    mix, gap = mixer.part(pl.ds(0, codes.shape[1]))
     mixer.store_loss(gap, loss)
+
+    def against(*parts):
+        row, total = 0, None
+        for part in parts:
+            term = product(mix[:, row : row + part.shape[0]], part[...])
+            row, total = row + part.shape[0], term if total is None else total + term
+        out[...] = total
 
     @pl.when(mixer.student)
     def _():
-        out[...] = product(mix[:, :head], early[...]) + product(mix[:, head:], late[...])
+        against(early, middle, late)
 
     @pl.when(jnp.logical_not(mixer.student))
     def _():
-        half = late.shape[0] // 2
-        for there, places in (
-            (sooner, (0, 1, 4, 5, 2, 3, 6, 11, 7)),
-            (later, (8, 9, 10, 12, 14, 13, 15)),
-        ):
-            for i, place in enumerate(places):
-                whole[place * half : (place + 1) * half, :] = there[i * half : (i + 1) * half, :]
-        out[...] = product(mix, whole[...])
+        against(sooner, later)
 
 
 def wide_mix_kernel(codes, keep, recv, student, out, loss, turned):
@@ -374,7 +411,7 @@
         stats, strip = call(
             functools.partial(first_kernel, False),
             [shape(8, total), shape(rows, total)],
-            [pltpu.VMEM((total, TILE), jnp.float32)],
+            [pltpu.VMEM((1, total, TILE), jnp.float32)],
             56,
             codes,
             whole,
@@ -412,8 +449,8 @@
     fa = send(join([f, level]), turn)
     fb = send(join([f, fa[:rows], level], g), return_turn)
     ga = send(g, turn)
-    sooner = send(join([u, n, y, f, fa[:rows], g]), over_core)
-    some, head = 4 * block, total - block
+    sooner = send(join([u, y, n, f, g], fa), over_core)
+    some, head = 4 * block, 6 * block
     codes, a_stats, a_strip, a_rows = call(
         functools.partial(first_kernel, True),
         [
@@ -422,7 +459,7 @@
             shape(rows, some),
             shape(some, width, dtype=jnp.bfloat16),
         ],
-        [pltpu.VMEM((some, TILE), jnp.float32)],
+        [slots(some, some)],
         16,
         codes,
         u,
@@ -435,31 +472,40 @@
     b_stats, b_strip, b_rows = call(
         second_kernel,
         [shape(8, head), shape(rows, head), shape(head, width, dtype=jnp.bfloat16)],
-        [pltpu.VMEM((head, TILE), jnp.float32)],
+        [slots(head, head - some), slots(head - some, some)],
         16,
         codes,
         a_rows,
         a_stats,
         a_strip,
-        ny,
         fa,
         fb,
         ga,
     )
-    later = send(join([ny, fb[:block], ga, gb], b_stats), over_core)
-    keep, mail = call(
+    c_stats, c_strip = call(
         third_kernel,
-        [shape(half + 8, total), shape(half + 8, total)],
-        [
-            pltpu.VMEM((8, total), jnp.float32),
-            pltpu.VMEM((rows, total), jnp.float32),
-            pltpu.VMEM((total, TILE), jnp.float32),
-        ],
+        [shape(8, total - block), shape(rows, total - block)],
+        [slots(total - block, block), slots(block, head)],
         16,
         codes,
         b_rows,
         b_stats,
         b_strip,
+        ny,
+    )
+    later = send(
+        join([b_rows[some : some + 3 * rows], gb[:rows], ny, ga, gb[rows:]], c_stats), over_core
+    )
+    keep, mail = call(
+        last_kernel,
+        [shape(half + 8, total), shape(half + 8, total)],
+        [pltpu.VMEM((block, total), jnp.float32), pltpu.VMEM((block, 8), jnp.float32)],
+        16,
+        codes,
+        b_rows,
+        ny,
+        c_stats,
+        c_strip,
         level_index,
         fa,
         fb,
@@ -469,12 +515,13 @@
     out, loss = call(
         mix_kernel,
         out_shapes,
-        [pltpu.VMEM((3, block, 8), jnp.float32), pltpu.VMEM((total, width), jnp.bfloat16)],
+        [pltpu.VMEM((3, block, 8), jnp.float32)],
         16,
         codes,
         keep,
         recv,
         b_rows,
+        ny,
         gb,
         sooner,
         later,

time: 41 us -> 39.1 us (0.954)
  waiting for transfers between devices: 15.8 us -> 10.5 us
  starting transfers between devices: 13.5 us -> 16.8 us
    ppermute x12, waiting for transfers between devices: 15.8 us -> 10.5 us  [send(): return lax.ppermute(a, ALL, pairs)]
    ppermute x12, starting transfers between devices: 13.5 us -> 16.8 us  [send(): return lax.ppermute(a, ALL, pairs)]
    pallas_call x10 -> x11, Pallas kernels: 8.89 us -> 9 us  [call(): pl.pallas_call(kernel, out_shape=shapes, in_specs=[SMEM if a.shape == (1,...]
  transfers between devices with their start and end apart: 12 -> 12, of which waited for: 8 -> 5; matrix products, arithmetic and copies ran while one was open for 0% -> 0% of each run, Pallas kernels for 16% -> 17%
where the time goes in v4:
time: 39.1 us; the launch traced here: 38.9 us
  starting transfers between devices  16.8 us (43%)
  waiting for transfers between devices  10.5 us (27%)
  Pallas kernels  9 us (23%)
  between operations  1.47 us (4%)
  local copies, waits for them, and re-layouts  1.18 us (3%)
    ppermute x12, starting transfers between devices, send(): return lax.ppermute(a, ALL, pairs)  16.8 us
    ppermute x12, waiting for transfers between devices, send(): return lax.ppermute(a, ALL, pairs)  10.5 us
    pallas_call x11, Pallas kernels, call(): pl.pallas_call(kernel, out_shape=shapes, in_specs=[SMEM if a.shape == (1,...  9 us
    unnamed x4, local copies, waits for them, and re-layouts  1.04 us
  transfers between devices with their start and end apart: 12, of which 5 were waited for; matrix products, arithmetic and copies ran while one was open for 0% of the time, Pallas kernels for 17%

profile of v4, /device:TPU:0, one launch (start us, length us, event | category | flops | bytes accessed | tf_op | source)
XLA Modules:
  0.0 38.9 jit_solution(5096029924333572406)
XLA Ops:
  0.6 0.0 copy-start
  0.7 1.0 %copy-done = bf16[2,128,1152]{2,1,0:T(8,128)(2,1)S(1)} copy-done((bf16[2,128,1152]{2,1,0:T(8,128)(2,1)S(1)}, bf16[2,128,1152]{2,1,0:T(8,128)(2,1)}, u32[]{:S(2)}) %copy-start) | copy-done | bytes 589848
  1.7 4.1 %collective-permute-start.2 = (bf16[64,1152]{1,0:T(8,128)(2,1)S(1)}, bf16[64,1152]{1,0:T(8,128)(2,1)S(1)}, u32[]{:S(2)}, u32[]{:S(2)}) collective-permute-start(bf16[64,1152]{1,0:T(8,128)(2,1)S(1)} %dynamic-slice_bitcast_fusion.1), channel_id=1, source_target_pairs={{0,16},{1,17},{2,18},{3,19},{4,20},{5,21},{6,22},{7,23},{8,24},{9,... | collective-permute-start | bytes 442376 | tf_op jit(solution)/shard_map/ppermute | solution.py:400
  5.9 1.6 %collective-permute-start.1 = (bf16[128,1152]{1,0:T(8,128)(2,1)S(1)}, bf16[128,1152]{1,0:T(8,128)(2,1)S(1)}, u32[]{:S(2)}, u32[]{:S(2)}) collective-permute-start(bf16[128,1152]{1,0:T(8,128)(2,1)S(1)} %dynamic-slice_bitcast_fusion.refs_0_), channel_id=1, source_target_pairs={{0,8},{1,9},{2,10},{3,11},{4,12},{5,13},{6,14},{7,15},{8,0},{9,1},... | collective-permute-start | bytes 884744 | tf_op jit(solution)/shard_map/ppermute | solution.py:400
  7.5 1.5 %collective-permute-start = (bf16[128,1152]{1,0:T(8,128)(2,1)S(1)}, bf16[128,1152]{1,0:T(8,128)(2,1)S(1)}, u32[]{:S(2)}, u32[]{:S(2)}) collective-permute-start(bf16[128,1152]{1,0:T(8,128)(2,1)S(1)} %dynamic-slice_bitcast_fusion.refs_0_), channel_id=1, source_target_pairs={{0,4},{1,5},{2,6},{3,7},{4,0},{5,1},{6,2},{7,3},{8,12},{9,13},{10,... | collective-permute-start | bytes 884744 | tf_op jit(solution)/shard_map/ppermute | solution.py:400
  9.7 3.3 %collective-permute-done.2.refs_3_.refs_0_ = bf16[64,1152]{1,0:T(8,128)(2,1)S(1)} collective-permute-done((bf16[64,1152]{1,0:T(8,128)(2,1)S(1)}, bf16[64,1152]{1,0:T(8,128)(2,1)S(1)}, u32[]{:S(2)}, u32[]{:S(2)}) %collective-permute-start.2) | collective-permute-done | bytes 147488 | tf_op jit(solution)/shard_map/ppermute | solution.py:400
  13.0 1.6 %collective-permute-start.4 = (bf16[80,1152]{1,0:T(8,128)(2,1)S(1)}, bf16[80,1152]{1,0:T(8,128)(2,1)S(1)}, u32[]{:S(2)}, u32[]{:S(2)}) collective-permute-start(bf16[80,1152]{1,0:T(8,128)(2,1)S(1)} %shard_map.51), channel_id=1, source_target_pairs={{0,2},{1,5},{2,0},{3,7},{4,6},{5,1},{6,4},{7,3},{8,10},{9,13},{10,... | collective-permute-start | bytes 552968 | tf_op jit(solution)/shard_map/ppermute | solution.py:400
  14.6 0.6 %collective-permute-start.3 = (bf16[64,1152]{1,0:T(8,128)(2,1)S(1)}, bf16[64,1152]{1,0:T(8,128)(2,1)S(1)}, u32[]{:S(2)}, u32[]{:S(2)}) collective-permute-start(bf16[64,1152]{1,0:T(8,128)(2,1)S(1)} %collective-permute-done.2.refs_3_.refs_0_), channel_id=1, source_target_pairs={{0,8},{1,9},{2,10},{3,11},{4,12},{5,13},{6,14},{7,15},{8,0},{9,1},... | collective-permute-start | bytes 442376 | tf_op jit(solution)/shard_map/ppermute | solution.py:400
  15.2 4.5 %collective-permute-done.3.refs_4_.refs_3_.refs_1_.refs_0_ = bf16[64,1152]{1,0:T(8,128)(2,1)S(1)} collective-permute-done((bf16[64,1152]{1,0:T(8,128)(2,1)S(1)}, bf16[64,1152]{1,0:T(8,128)(2,1)S(1)}, u32[]{:S(2)}, u32[]{:S(2)}) %collective-permute-start.3) | collective-permute-done | bytes 147488 | tf_op jit(solution)/shard_map/ppermute | solution.py:400
  19.7 0.0 collective-permute-done.1.refs_2_
  19.7 0.0 collective-permute-done.refs_1_.refs_0_
  19.7 0.0 collective-permute-done.4.fa.refs_5_
  19.7 0.1 shard_map.56
  19.8 0.0 copy-start.1
  19.9 0.1 collective-permute-start.8
  19.9 1.4 %collective-permute-start.6 = (bf16[64,1152]{1,0:T(8,128)(2,1)S(1)}, bf16[64,1152]{1,0:T(8,128)(2,1)S(1)}, u32[]{:S(2)}, u32[]{:S(2)}) collective-permute-start(bf16[64,1152]{1,0:T(8,128)(2,1)S(1)} %collective-permute-done.3.refs_4_.refs_3_.refs_1_.refs_0_), channel_id=1, source_target_pairs={{0,2},{1,5},{2,0},{3,7},{4,6},{5,1},{6,4},{7,3},{8,10},{9,13},{10,... | collective-permute-start | bytes 442376 | tf_op jit(solution)/shard_map/ppermute | solution.py:400
  21.4 1.6 %collective-permute-start.5 = (bf16[144,1152]{1,0:T(8,128)(2,1)S(1)}, bf16[144,1152]{1,0:T(8,128)(2,1)S(1)}, u32[]{:S(2)}, u32[]{:S(2)}) collective-permute-start(bf16[144,1152]{1,0:T(8,128)(2,1)S(1)} %shard_map.52), channel_id=1, source_target_pairs={{0,4},{1,3},{2,6},{3,1},{4,0},{5,7},{6,2},{7,5},{8,12},{9,11},{10,... | collective-permute-start | bytes 995336 | tf_op jit(solution)/shard_map/ppermute | solution.py:400
  23.0 1.4 %collective-permute-start.7 = (bf16[128,1152]{1,0:T(8,128)(2,1)S(1)}, bf16[128,1152]{1,0:T(8,128)(2,1)S(1)}, u32[]{:S(2)}, u32[]{:S(2)}) collective-permute-start(bf16[128,1152]{1,0:T(8,128)(2,1)S(1)} %shard_map.54), channel_id=1, source_target_pairs={{0,8},{1,9},{2,10},{3,11},{4,12},{5,13},{6,14},{7,15},{8,0},{9,1},... | collective-permute-start | bytes 884744 | tf_op jit(solution)/shard_map/ppermute | solution.py:400
  24.4 0.0 copy-done.1
  24.4 1.6 %shard_map.50 = (s32[1,1024]{1,0:T(1,128)S(1)}, f32[8,512]{1,0:T(8,128)S(1)}, f32[64,512]{1,0:T(8,128)S(1)}, bf16[512,1152]{1,0:T(8,128)(2,1)S(1)}) custom-call(s32[1,1024]{1,0:T(1,128)S(1)} %bitcast.7, bf16[128,1152]{1,0:T(8,128)(2,1)S(1)} %dynamic-slice_bitcast_fusion.refs_0_, bf16[128,1152]{1,0:T(8,128)(2,1)S(1)} %collective-permute-done.refs_1_.refs_0_, ...), custom_call_target="tpu_custom_call" | custom-call | tf_op jit(solution)/shard_map/pallas_call | solution.py:361
  26.0 0.0 collective-permute-done.6.ga.refs_1_.refs_3_
  26.0 0.0 collective-permute-done.8.refs_2_.sooner
  26.1 2.3 %collective-permute-start.9 = (bf16[128,1152]{1,0:T(8,128)(2,1)S(1)}, bf16[128,1152]{1,0:T(8,128)(2,1)S(1)}, u32[]{:S(2)}, u32[]{:S(2)}) collective-permute-start(bf16[128,1152]{1,0:T(8,128)(2,1)S(1)} %shard_map.57), channel_id=1, source_target_pairs={{0,4},{1,3},{2,6},{3,1},{4,0},{5,7},{6,2},{7,5},{8,12},{9,11},{10,... | collective-permute-start | bytes 884744 | tf_op jit(solution)/shard_map/ppermute | solution.py:400
  28.3 0.3 collective-permute-done.5.fb
  28.6 1.9 %shard_map.53 = (f32[8,768]{1,0:T(8,128)S(1)}, f32[64,768]{1,0:T(8,128)S(1)}, bf16[768,1152]{1,0:T(8,128)(2,1)S(1)}) custom-call(s32[1,1024]{1,0:T(1,128)S(1)} %get-tuple-element.15.codes, bf16[512,1152]{1,0:T(8,128)(2,1)S(1)} %get-tuple-element.16.early, f32[8,512]{1,0:T(8,128)S(1)} %get-tuple-element.17.before.refs_3_, ...), custom_call_target="tpu_custom_call" | custom-call | tf_op jit(solution)/shard_map/pallas_call | solution.py:361
  30.5 1.3 %collective-permute-done.7.late.middle.refs_2_ = bf16[128,1152]{1,0:T(8,128)(2,1)S(1)} collective-permute-done((bf16[128,1152]{1,0:T(8,128)(2,1)S(1)}, bf16[128,1152]{1,0:T(8,128)(2,1)S(1)}, u32[]{:S(2)}, u32[]{:S(2)}) %collective-permute-start.7) | collective-permute-done | bytes 294944 | tf_op jit(solution)/shard_map/ppermute | solution.py:400
  31.9 1.6 %shard_map.55 = (f32[8,896]{1,0:T(8,128)S(1)}, f32[64,896]{1,0:T(8,128)S(1)}) custom-call(s32[1,1024]{1,0:T(1,128)S(1)} %get-tuple-element.15.codes, bf16[768,1152]{1,0:T(8,128)(2,1)S(1)} %get-tuple-element.19.early, f32[8,768]{1,0:T(8,128)S(1)} %get-tuple-element.20.before, f32[64,768]{1,0:T(8,128)S(1)} %get-tuple-element.21.part_strip, ...), custom_call_target="tpu_custom_call" | custom-call | tf_op jit(solution)/shard_map/pallas_call | solution.py:361
  33.5 0.0 collective-permute-done.9.late
  33.6 0.1 shard_map.59
  33.7 0.1 collective-permute-start.11
  33.7 1.6 %shard_map.58 = (f32[40,1024]{1,0:T(8,128)S(1)}, f32[40,1024]{1,0:T(8,128)S(1)}) custom-call(s32[1,1024]{1,0:T(1,128)S(1)} %get-tuple-element.15.codes, bf16[768,1152]{1,0:T(8,128)(2,1)S(1)} %get-tuple-element.19.early, bf16[128,1152]{1,0:T(8,128)(2,1)S(1)} %collective-permute-done.7.late.middle.refs_2_, f32[8,896]{1,0:T(8,128)S(1)} %get-tuple-element.22.before.refs_5_, ...), custom_call_target="tpu_custom_call" | custom-call | tf_op jit(solution)/shard_map/pallas_call | solution.py:361
  35.4 0.5 %collective-permute-start.10 = (f32[40,1024]{1,0:T(8,128)S(1)}, f32[40,1024]{1,0:T(8,128)S(1)}, u32[]{:S(2)}, u32[]{:S(2)}) collective-permute-start(f32[40,1024]{1,0:T(8,128)S(1)} %get-tuple-element.25), channel_id=1, source_target_pairs={{0,1},{1,0},{2,3},{3,2},{4,5},{5,4},{6,7},{7,6},{8,9},{9,8},{10,11... | collective-permute-start | bytes 491528 | tf_op jit(solution)/shard_map/ppermute | solution.py:400
  35.9 1.0 %collective-permute-done.10.recv = f32[40,1024]{1,0:T(8,128)S(1)} collective-permute-done((f32[40,1024]{1,0:T(8,128)S(1)}, f32[40,1024]{1,0:T(8,128)S(1)}, u32[]{:S(2)}, u32[]{:S(2)}) %collective-permute-start.10) | collective-permute-done | bytes 163872 | tf_op jit(solution)/shard_map/ppermute | solution.py:400
  36.9 0.0 collective-permute-done.11.later
  36.9 2.0 %shard_map.60 = (f32[32,1152]{1,0:T(8,128)}, f32[1,32]{1,0:T(1,128)}) custom-call(s32[1,1024]{1,0:T(1,128)S(1)} %get-tuple-element.15.codes, f32[40,1024]{1,0:T(8,128)S(1)} %get-tuple-element.24.keep, f32[40,1024]{1,0:T(8,128)S(1)} %collective-permute-done.10.recv, bf16[768,1152]{1,0:T(8,128)(2,1)S(1)} %get-tuple-element.19.early, ...), custom_call_target="tpu_custom_call" | custom-call | tf_op jit(solution)/shard_map/pallas_call | solution.py:361
  (10 shorter events, 0.2 us)
Async XLA Ops:
  0.6 1.1 %copy-start = (bf16[2,128,1152]{2,1,0:T(8,128)(2,1)S(1)}, bf16[2,128,1152]{2,1,0:T(8,128)(2,1)}, u32[]{:S(2)}) copy-start(bf16[2,128,1152]{2,1,0:T(8,128)(2,1)} %param.3) | copy-start | bytes 1769476
  1.7 11.2 %collective-permute-start.2 = (bf16[64,1152]{1,0:T(8,128)(2,1)S(1)}, bf16[64,1152]{1,0:T(8,128)(2,1)S(1)}, u32[]{:S(2)}, u32[]{:S(2)}) collective-permute-start(bf16[64,1152]{1,0:T(8,128)(2,1)S(1)} %dynamic-slice_bitcast_fusion.1), channel_id=1, source_target_pairs={{0,16},{1,17},{2,18},{3,19},{4,20},{5,21},{6,22},{7,23},{8,24},{9,... | collective-permute-start | bytes 442376 | tf_op jit(solution)/shard_map/ppermute | solution.py:400
  5.9 13.9 %collective-permute-start.1 = (bf16[128,1152]{1,0:T(8,128)(2,1)S(1)}, bf16[128,1152]{1,0:T(8,128)(2,1)S(1)}, u32[]{:S(2)}, u32[]{:S(2)}) collective-permute-start(bf16[128,1152]{1,0:T(8,128)(2,1)S(1)} %dynamic-slice_bitcast_fusion.refs_0_), channel_id=1, source_target_pairs={{0,8},{1,9},{2,10},{3,11},{4,12},{5,13},{6,14},{7,15},{8,0},{9,1},... | collective-permute-start | bytes 884744 | tf_op jit(solution)/shard_map/ppermute | solution.py:400
  7.5 12.2 %collective-permute-start = (bf16[128,1152]{1,0:T(8,128)(2,1)S(1)}, bf16[128,1152]{1,0:T(8,128)(2,1)S(1)}, u32[]{:S(2)}, u32[]{:S(2)}) collective-permute-start(bf16[128,1152]{1,0:T(8,128)(2,1)S(1)} %dynamic-slice_bitcast_fusion.refs_0_), channel_id=1, source_target_pairs={{0,4},{1,5},{2,6},{3,7},{4,0},{5,1},{6,2},{7,3},{8,12},{9,13},{10,... | collective-permute-start | bytes 884744 | tf_op jit(solution)/shard_map/ppermute | solution.py:400
  13.0 6.8 %collective-permute-start.4 = (bf16[80,1152]{1,0:T(8,128)(2,1)S(1)}, bf16[80,1152]{1,0:T(8,128)(2,1)S(1)}, u32[]{:S(2)}, u32[]{:S(2)}) collective-permute-start(bf16[80,1152]{1,0:T(8,128)(2,1)S(1)} %shard_map.51), channel_id=1, source_target_pairs={{0,2},{1,5},{2,0},{3,7},{4,6},{5,1},{6,4},{7,3},{8,10},{9,13},{10,... | collective-permute-start | bytes 552968 | tf_op jit(solution)/shard_map/ppermute | solution.py:400
  14.6 5.1 %collective-permute-start.3 = (bf16[64,1152]{1,0:T(8,128)(2,1)S(1)}, bf16[64,1152]{1,0:T(8,128)(2,1)S(1)}, u32[]{:S(2)}, u32[]{:S(2)}) collective-permute-start(bf16[64,1152]{1,0:T(8,128)(2,1)S(1)} %collective-permute-done.2.refs_3_.refs_0_), channel_id=1, source_target_pairs={{0,8},{1,9},{2,10},{3,11},{4,12},{5,13},{6,14},{7,15},{8,0},{9,1},... | collective-permute-start | bytes 442376 | tf_op jit(solution)/shard_map/ppermute | solution.py:400
  19.8 4.6 %copy-start.1 = (s32[1024]{0:T(1024)S(1)}, s32[1024]{0:T(1024)}, u32[]{:S(2)}) copy-start(s32[1024]{0:T(1024)} %param.4) | copy-start | bytes 12292
  19.9 6.2 %collective-permute-start.8 = (bf16[512,1152]{1,0:T(8,128)(2,1)S(1)}, bf16[512,1152]{1,0:T(8,128)(2,1)S(1)}, u32[]{:S(2)}, u32[]{:S(2)}) collective-permute-start(bf16[512,1152]{1,0:T(8,128)(2,1)S(1)} %shard_map.56), channel_id=1, source_target_pairs={{0,1},{1,0},{2,3},{3,2},{4,5},{5,4},{6,7},{7,6},{8,9},{9,8},{10,11... | collective-permute-start | bytes 3538952 | tf_op jit(solution)/shard_map/ppermute | solution.py:400
  19.9 6.1 %collective-permute-start.6 = (bf16[64,1152]{1,0:T(8,128)(2,1)S(1)}, bf16[64,1152]{1,0:T(8,128)(2,1)S(1)}, u32[]{:S(2)}, u32[]{:S(2)}) collective-permute-start(bf16[64,1152]{1,0:T(8,128)(2,1)S(1)} %collective-permute-done.3.refs_4_.refs_3_.refs_1_.refs_0_), channel_id=1, source_target_pairs={{0,2},{1,5},{2,0},{3,7},{4,6},{5,1},{6,4},{7,3},{8,10},{9,13},{10,... | collective-permute-start | bytes 442376 | tf_op jit(solution)/shard_map/ppermute | solution.py:400
  21.4 7.2 %collective-permute-start.5 = (bf16[144,1152]{1,0:T(8,128)(2,1)S(1)}, bf16[144,1152]{1,0:T(8,128)(2,1)S(1)}, u32[]{:S(2)}, u32[]{:S(2)}) collective-permute-start(bf16[144,1152]{1,0:T(8,128)(2,1)S(1)} %shard_map.52), channel_id=1, source_target_pairs={{0,4},{1,3},{2,6},{3,1},{4,0},{5,7},{6,2},{7,5},{8,12},{9,11},{10,... | collective-permute-start | bytes 995336 | tf_op jit(solution)/shard_map/ppermute | solution.py:400
  23.0 8.8 %collective-permute-start.7 = (bf16[128,1152]{1,0:T(8,128)(2,1)S(1)}, bf16[128,1152]{1,0:T(8,128)(2,1)S(1)}, u32[]{:S(2)}, u32[]{:S(2)}) collective-permute-start(bf16[128,1152]{1,0:T(8,128)(2,1)S(1)} %shard_map.54), channel_id=1, source_target_pairs={{0,8},{1,9},{2,10},{3,11},{4,12},{5,13},{6,14},{7,15},{8,0},{9,1},... | collective-permute-start | bytes 884744 | tf_op jit(solution)/shard_map/ppermute | solution.py:400
  26.1 7.5 %collective-permute-start.9 = (bf16[128,1152]{1,0:T(8,128)(2,1)S(1)}, bf16[128,1152]{1,0:T(8,128)(2,1)S(1)}, u32[]{:S(2)}, u32[]{:S(2)}) collective-permute-start(bf16[128,1152]{1,0:T(8,128)(2,1)S(1)} %shard_map.57), channel_id=1, source_target_pairs={{0,4},{1,3},{2,6},{3,1},{4,0},{5,7},{6,2},{7,5},{8,12},{9,11},{10,... | collective-permute-start | bytes 884744 | tf_op jit(solution)/shard_map/ppermute | solution.py:400
  33.7 3.3 %collective-permute-start.11 = (bf16[512,1152]{1,0:T(8,128)(2,1)S(1)}, bf16[512,1152]{1,0:T(8,128)(2,1)S(1)}, u32[]{:S(2)}, u32[]{:S(2)}) collective-permute-start(bf16[512,1152]{1,0:T(8,128)(2,1)S(1)} %shard_map.59), channel_id=1, source_target_pairs={{0,1},{1,0},{2,3},{3,2},{4,5},{5,4},{6,7},{7,6},{8,9},{9,8},{10,11... | collective-permute-start | bytes 3538952 | tf_op jit(solution)/shard_map/ppermute | solution.py:400
  35.4 1.5 %collective-permute-start.10 = (f32[40,1024]{1,0:T(8,128)S(1)}, f32[40,1024]{1,0:T(8,128)S(1)}, u32[]{:S(2)}, u32[]{:S(2)}) collective-permute-start(f32[40,1024]{1,0:T(8,128)S(1)} %get-tuple-element.25), channel_id=1, source_target_pairs={{0,1},{1,0},{2,3},{3,2},{4,5},{5,4},{6,7},{7,6},{8,9},{9,8},{10,11... | collective-permute-start | bytes 491528 | tf_op jit(solution)/shard_map/ppermute | solution.py:400

commit v5 on v4

--- a/solution.py
+++ b/solution.py
@@ -158,30 +158,29 @@
     )
 
 
-def slots(rows, cols):
-    return pltpu.VMEM((len(tiles(cols)), rows, min(cols, TILE)), jnp.float32)
-
-
-def add_rows(x, codes, early, late, before, stats, strip, gram, wide):
-    head, width = early.shape
-    tail = late.shape[0]
-    for slot, (start, size) in enumerate(tiles(tail)):
-        cols, lines = pl.ds(start, size), slice(head + start, head + start + size)
-        part = gram.at[slot, :, 0:size]
-        part[0:head, :] = times(early[...], late[cols, :])
-        part[head : head + tail, :] = times(late[...], late[cols, :])
-        hide_diagonal(part, pl.ds(head + start, size))
-        strip[:, lines] = part[spot(x, strip.shape[0]), :]
-        best, sums = columns(part, head + tail, bases_of(codes[:, lines], width))
-        stats[0:1, lines] = best
-        for level in range(CODES):
-            stats[1 + level : 2 + level, lines] = sums[level]
-    for slot, (start, size) in enumerate(tiles(head)):
+def add_rows(codes, early, late, before, stats, strip, wide, square):
+    tail, width = late.shape
+    head, block = before.shape[1], 2 * strip.shape[0]
+    last = slice(head, head + tail)
+    row = 0
+    for part in early:
+        wide[:, row : row + part.shape[0]] = times(late[...], part[...])
+        row += part.shape[0]
+    gram = times(late[...], late[...])
+    lines, lanes = (lax.broadcasted_iota(jnp.int32, gram.shape, axis) for axis in (0, 1))
+    wide[:, last] = jnp.where(lines == lanes, NEG, gram)
+    square[...] = jnp.broadcast_to(codes[:, last], (8, tail)).astype(jnp.float32).T
+    bases = bases_of(square[:, 0:1], width)
+    best = jnp.max(wide[...], axis=1, keepdims=True)
+    part = powers(wide[...] - best, *bases)
+    square[:, 0:1] = best
+    for level in range(CODES):
+        square[:, 1 + level : 2 + level] = jnp.sum(part[level], axis=1, keepdims=True)
+    stats[:, last] = square[...].T
+    for start, size in tiles(head):
         cols = pl.ds(start, size)
-        part = wide.at[slot, :, 0:size]
-        part[...] = times(late[...], early[cols, :])
         bases = bases_of(codes[:, cols], width)
-        best, sums = columns(part, tail, bases)
+        best, sums = columns(wide.at[:, cols], tail, bases)
         top = jnp.maximum(best, before[0:1, cols])
         was, now = powers(before[0:1, cols] - top, *bases), powers(best - top, *bases)
         stats[0:1, cols] = top
@@ -189,9 +188,12 @@
             stats[1 + level : 2 + level, cols] = (
                 before[1 + level : 2 + level, cols] * was[level] + sums[level] * now[level]
             )
-
-
-def second_kernel(codes, early, before, part_strip, fa, fb, ga, stats, strip, whole, gram, wide):
+    _, x, _ = position()
+    turned = wide[:, 0:block].T
+    strip[:, last] = jnp.where(x == 0, turned[: block // 2], turned[block // 2 :])
+
+
+def second_kernel(codes, early, before, part_strip, fa, fb, ga, stats, strip, whole, wide, square):
     _, x, core = position()
     head, half = early.shape[0], ga.shape[0]
     late = whole.at[head:, :]
@@ -201,62 +203,32 @@
     late[3 * half : 4 * half, :] = ga[...]
     whole[0:head, :] = early[...]
     strip[:, 0:head] = part_strip[...]
-    add_rows(x, codes, early, late, before, stats, strip, gram, wide)
+    add_rows(codes, [early], late, before, stats, strip, wide, square)
     stats[1 + CODES :, :] = jnp.zeros((stats.shape[0] - 1 - CODES, stats.shape[1]), jnp.float32)
 
 
-def third_kernel(codes, early, before, part_strip, late, stats, strip, gram, wide):
-    _, x, _ = position()
+def third_kernel(codes, early, before, part_strip, late, stats, strip, wide, square):
     strip[:, 0 : early.shape[0]] = part_strip[...]
-    add_rows(x, codes, early, late, before, stats, strip, gram, wide)
+    add_rows(codes, [early], late, before, stats, strip, wide, square)
     stats[1 + CODES :, :] = jnp.zeros((stats.shape[0] - 1 - CODES, stats.shape[1]), jnp.float32)
 
 
 def last_kernel(
-    codes, early, middle, before, strip, level_index, fa, fb, late, keep, send, wide, square
+    codes, early, middle, before, part_strip, level_index, fa, fb, late, keep, send, strip, wide, square
 ):
     _, x, core = position()
-    block, width = late.shape
+    block = late.shape[0]
     half = block // 4
-    head = before.shape[1]
-    last = slice(head, head + block)
-    wide[:, 0 : early.shape[0]] = times(late[...], early[...])
-    wide[:, early.shape[0] : head] = times(late[...], middle[...])
-    gram = times(late[...], late[...])
-    lines, lanes = (lax.broadcasted_iota(jnp.int32, gram.shape, axis) for axis in (0, 1))
-    wide[:, last] = jnp.where(lines == lanes, NEG, gram)
-    square[...] = jnp.broadcast_to(codes[:, last], (8, block)).astype(jnp.float32).T
-    bases = bases_of(square[:, 0:1], width)
-    best = jnp.max(wide[...], axis=1, keepdims=True)
-    part = powers(wide[...] - best, *bases)
-    square[:, 0:1] = best
-    for level in range(CODES):
-        square[:, 1 + level : 2 + level] = jnp.sum(part[level], axis=1, keepdims=True)
-    keep[half:, last] = square[...].T
-    for start, size in tiles(head):
-        cols = pl.ds(start, size)
-        bases = bases_of(codes[:, cols], width)
-        best, sums = columns(wide.at[:, cols], block, bases)
-        top = jnp.maximum(best, before[0:1, cols])
-        was, now = powers(before[0:1, cols] - top, *bases), powers(best - top, *bases)
-        keep[half : half + 1, cols] = top
-        for level in range(CODES):
-            keep[half + 1 + level : half + 2 + level, cols] = (
-                before[1 + level : 2 + level, cols] * was[level] + sums[level] * now[level]
-            )
-    lane = lax.broadcasted_iota(jnp.int32, (1, head + block), 1)
+    strip[:, 0 : before.shape[1]] = part_strip[...]
+    stats = keep.at[half:, :]
+    add_rows(codes, [early, middle], late, before, stats, strip, wide, square)
+    lane = lax.broadcasted_iota(jnp.int32, (1, stats.shape[1]), 1)
     level = level_index[0].astype(jnp.float32)
     theirs = jnp.where(core == 0, fa[block // 2 : block // 2 + 1, 0:1], fb[block : block + 1, 0:1])
-    keep[half + 1 + CODES :, :] = jnp.where(lane < 128, level, theirs.astype(jnp.float32))
-    square_t = wide[:, 0:block].T
-    for ref, share in ((keep, core), (send, 1 - core)):
-        ref[0:half, 0:head] = strip[spot(share, half), :]
-        here = jnp.where(share == 0, square_t[0:half], square_t[half : 2 * half])
-        there = jnp.where(
-            share == 0, square_t[2 * half : 3 * half], square_t[3 * half : 4 * half]
-        )
-        ref[0:half, last] = jnp.where(x == 0, here, there)
-    send[half:, :] = keep[half:, :]
+    stats[1 + CODES :, :] = jnp.where(lane < 128, level, theirs.astype(jnp.float32))
+    keep[0:half, :] = strip[spot(core, half), :]
+    send[0:half, :] = strip[spot(1 - core, half), :]
+    send[half:, :] = stats[...]
     left, right = swapped(send, block)
     send[:, -3 * block : -2 * block] = left
     send[:, -block:] = right
@@ -366,6 +338,10 @@
         scratch_shapes=scratch,
         compiler_params=pltpu.CompilerParams(vmem_limit_bytes=limit << 20),
     )(*args)
+
+
+def room(rows, cols):
+    return [pltpu.VMEM((rows, cols), jnp.float32), pltpu.VMEM((rows, 8), jnp.float32)]
 
 
 def join(parts, *behind):
@@ -459,7 +435,7 @@
             shape(rows, some),
             shape(some, width, dtype=jnp.bfloat16),
         ],
-        [slots(some, some)],
+        [pltpu.VMEM((some // TILE, some, TILE), jnp.float32)],
         16,
         codes,
         u,
@@ -472,7 +448,7 @@
     b_stats, b_strip, b_rows = call(
         second_kernel,
         [shape(8, head), shape(rows, head), shape(head, width, dtype=jnp.bfloat16)],
-        [slots(head, head - some), slots(head - some, some)],
+        room(head - some, head),
         16,
         codes,
         a_rows,
@@ -485,7 +461,7 @@
     c_stats, c_strip = call(
         third_kernel,
         [shape(8, total - block), shape(rows, total - block)],
-        [slots(total - block, block), slots(block, head)],
+        room(block, total - block),
         16,
         codes,
         b_rows,
@@ -499,7 +475,7 @@
     keep, mail = call(
         last_kernel,
         [shape(half + 8, total), shape(half + 8, total)],
-        [pltpu.VMEM((block, total), jnp.float32), pltpu.VMEM((block, 8), jnp.float32)],
+        [pltpu.VMEM((rows, total), jnp.float32)] + room(block, total),
         16,
         codes,
         b_rows,

time: 39.1 us -> 38.7 us (0.990)
  Pallas kernels: 9 us -> 8.22 us
    pallas_call x11, Pallas kernels: 9 us -> 8.22 us  [call(): pl.pallas_call(kernel, out_shape=shapes, in_specs=[SMEM if a.shape == (1,...]
  transfers between devices with their start and end apart: 12 -> 12, of which waited for: 5 -> 5; matrix products, arithmetic and copies ran while one was open for 0% -> 0% of each run, Pallas kernels for 17% -> 16%
where the time goes in v5:
time: 38.7 us; the launch traced here: 38.5 us
  starting transfers between devices  16.9 us (44%)
  waiting for transfers between devices  10.7 us (28%)
  Pallas kernels  8.22 us (21%)
  between operations  1.48 us (4%)
  local copies, waits for them, and re-layouts  1.18 us (3%)
    ppermute x12, starting transfers between devices, send(): return lax.ppermute(a, ALL, pairs)  16.9 us
    ppermute x12, waiting for transfers between devices, send(): return lax.ppermute(a, ALL, pairs)  10.7 us
    pallas_call x11, Pallas kernels, call(): pl.pallas_call(kernel, out_shape=shapes, in_specs=[SMEM if a.shape == (1,...  8.22 us
    unnamed x4, local copies, waits for them, and re-layouts  1.04 us
  transfers between devices with their start and end apart: 12, of which 5 were waited for; matrix products, arithmetic and copies ran while one was open for 0% of the time, Pallas kernels for 16%

profile of v5, /device:TPU:0, one launch (start us, length us, event | category | flops | bytes accessed | tf_op | source)
XLA Modules:
  0.0 38.5 jit_solution(13929793019004622366)
XLA Ops:
  0.6 0.0 copy-start
  0.7 1.0 %copy-done = bf16[2,128,1152]{2,1,0:T(8,128)(2,1)S(1)} copy-done((bf16[2,128,1152]{2,1,0:T(8,128)(2,1)S(1)}, bf16[2,128,1152]{2,1,0:T(8,128)(2,1)}, u32[]{:S(2)}) %copy-start) | copy-done | bytes 589848
  1.7 4.1 %collective-permute-start.2 = (bf16[64,1152]{1,0:T(8,128)(2,1)S(1)}, bf16[64,1152]{1,0:T(8,128)(2,1)S(1)}, u32[]{:S(2)}, u32[]{:S(2)}) collective-permute-start(bf16[64,1152]{1,0:T(8,128)(2,1)S(1)} %dynamic-slice_bitcast_fusion.1), channel_id=1, source_target_pairs={{0,16},{1,17},{2,18},{3,19},{4,20},{5,21},{6,22},{7,23},{8,24},{9,... | collective-permute-start | bytes 442376 | tf_op jit(solution)/shard_map/ppermute | solution.py:376
  5.9 1.6 %collective-permute-start.1 = (bf16[128,1152]{1,0:T(8,128)(2,1)S(1)}, bf16[128,1152]{1,0:T(8,128)(2,1)S(1)}, u32[]{:S(2)}, u32[]{:S(2)}) collective-permute-start(bf16[128,1152]{1,0:T(8,128)(2,1)S(1)} %dynamic-slice_bitcast_fusion.refs_0_), channel_id=1, source_target_pairs={{0,8},{1,9},{2,10},{3,11},{4,12},{5,13},{6,14},{7,15},{8,0},{9,1},... | collective-permute-start | bytes 884744 | tf_op jit(solution)/shard_map/ppermute | solution.py:376
  7.5 1.5 %collective-permute-start = (bf16[128,1152]{1,0:T(8,128)(2,1)S(1)}, bf16[128,1152]{1,0:T(8,128)(2,1)S(1)}, u32[]{:S(2)}, u32[]{:S(2)}) collective-permute-start(bf16[128,1152]{1,0:T(8,128)(2,1)S(1)} %dynamic-slice_bitcast_fusion.refs_0_), channel_id=1, source_target_pairs={{0,4},{1,5},{2,6},{3,7},{4,0},{5,1},{6,2},{7,3},{8,12},{9,13},{10,... | collective-permute-start | bytes 884744 | tf_op jit(solution)/shard_map/ppermute | solution.py:376
  9.7 3.3 %collective-permute-done.2.refs_3_.refs_0_ = bf16[64,1152]{1,0:T(8,128)(2,1)S(1)} collective-permute-done((bf16[64,1152]{1,0:T(8,128)(2,1)S(1)}, bf16[64,1152]{1,0:T(8,128)(2,1)S(1)}, u32[]{:S(2)}, u32[]{:S(2)}) %collective-permute-start.2) | collective-permute-done | bytes 147488 | tf_op jit(solution)/shard_map/ppermute | solution.py:376
  13.0 1.6 %collective-permute-start.4 = (bf16[80,1152]{1,0:T(8,128)(2,1)S(1)}, bf16[80,1152]{1,0:T(8,128)(2,1)S(1)}, u32[]{:S(2)}, u32[]{:S(2)}) collective-permute-start(bf16[80,1152]{1,0:T(8,128)(2,1)S(1)} %shard_map.51), channel_id=1, source_target_pairs={{0,2},{1,5},{2,0},{3,7},{4,6},{5,1},{6,4},{7,3},{8,10},{9,13},{10,... | collective-permute-start | bytes 552968 | tf_op jit(solution)/shard_map/ppermute | solution.py:376
  14.6 0.6 %collective-permute-start.3 = (bf16[64,1152]{1,0:T(8,128)(2,1)S(1)}, bf16[64,1152]{1,0:T(8,128)(2,1)S(1)}, u32[]{:S(2)}, u32[]{:S(2)}) collective-permute-start(bf16[64,1152]{1,0:T(8,128)(2,1)S(1)} %collective-permute-done.2.refs_3_.refs_0_), channel_id=1, source_target_pairs={{0,8},{1,9},{2,10},{3,11},{4,12},{5,13},{6,14},{7,15},{8,0},{9,1},... | collective-permute-start | bytes 442376 | tf_op jit(solution)/shard_map/ppermute | solution.py:376
  15.2 4.5 %collective-permute-done.3.refs_4_.refs_3_.refs_1_.refs_0_ = bf16[64,1152]{1,0:T(8,128)(2,1)S(1)} collective-permute-done((bf16[64,1152]{1,0:T(8,128)(2,1)S(1)}, bf16[64,1152]{1,0:T(8,128)(2,1)S(1)}, u32[]{:S(2)}, u32[]{:S(2)}) %collective-permute-start.3) | collective-permute-done | bytes 147488 | tf_op jit(solution)/shard_map/ppermute | solution.py:376
  19.7 0.0 collective-permute-done.1.refs_2_
  19.7 0.0 collective-permute-done.refs_1_.refs_0_
  19.7 0.0 collective-permute-done.4.fa.refs_5_
  19.7 0.1 shard_map.56
  19.8 0.0 copy-start.1
  19.9 0.1 collective-permute-start.8
  19.9 1.4 %collective-permute-start.6 = (bf16[64,1152]{1,0:T(8,128)(2,1)S(1)}, bf16[64,1152]{1,0:T(8,128)(2,1)S(1)}, u32[]{:S(2)}, u32[]{:S(2)}) collective-permute-start(bf16[64,1152]{1,0:T(8,128)(2,1)S(1)} %collective-permute-done.3.refs_4_.refs_3_.refs_1_.refs_0_), channel_id=1, source_target_pairs={{0,2},{1,5},{2,0},{3,7},{4,6},{5,1},{6,4},{7,3},{8,10},{9,13},{10,... | collective-permute-start | bytes 442376 | tf_op jit(solution)/shard_map/ppermute | solution.py:376
  21.4 1.6 %collective-permute-start.5 = (bf16[144,1152]{1,0:T(8,128)(2,1)S(1)}, bf16[144,1152]{1,0:T(8,128)(2,1)S(1)}, u32[]{:S(2)}, u32[]{:S(2)}) collective-permute-start(bf16[144,1152]{1,0:T(8,128)(2,1)S(1)} %shard_map.52), channel_id=1, source_target_pairs={{0,4},{1,3},{2,6},{3,1},{4,0},{5,7},{6,2},{7,5},{8,12},{9,11},{10,... | collective-permute-start | bytes 995336 | tf_op jit(solution)/shard_map/ppermute | solution.py:376
  23.0 1.4 %collective-permute-start.7 = (bf16[128,1152]{1,0:T(8,128)(2,1)S(1)}, bf16[128,1152]{1,0:T(8,128)(2,1)S(1)}, u32[]{:S(2)}, u32[]{:S(2)}) collective-permute-start(bf16[128,1152]{1,0:T(8,128)(2,1)S(1)} %shard_map.54), channel_id=1, source_target_pairs={{0,8},{1,9},{2,10},{3,11},{4,12},{5,13},{6,14},{7,15},{8,0},{9,1},... | collective-permute-start | bytes 884744 | tf_op jit(solution)/shard_map/ppermute | solution.py:376
  24.4 0.0 copy-done.1
  24.4 1.6 %shard_map.50 = (s32[1,1024]{1,0:T(1,128)S(1)}, f32[8,512]{1,0:T(8,128)S(1)}, f32[64,512]{1,0:T(8,128)S(1)}, bf16[512,1152]{1,0:T(8,128)(2,1)S(1)}) custom-call(s32[1,1024]{1,0:T(1,128)S(1)} %bitcast.7, bf16[128,1152]{1,0:T(8,128)(2,1)S(1)} %dynamic-slice_bitcast_fusion.refs_0_, bf16[128,1152]{1,0:T(8,128)(2,1)S(1)} %collective-permute-done.refs_1_.refs_0_, ...), custom_call_target="tpu_custom_call" | custom-call | tf_op jit(solution)/shard_map/pallas_call | solution.py:333
  26.0 0.0 collective-permute-done.6.ga.refs_1_.refs_3_
  26.0 0.0 collective-permute-done.8.refs_2_.sooner
  26.1 2.3 %collective-permute-start.9 = (bf16[128,1152]{1,0:T(8,128)(2,1)S(1)}, bf16[128,1152]{1,0:T(8,128)(2,1)S(1)}, u32[]{:S(2)}, u32[]{:S(2)}) collective-permute-start(bf16[128,1152]{1,0:T(8,128)(2,1)S(1)} %shard_map.57), channel_id=1, source_target_pairs={{0,4},{1,3},{2,6},{3,1},{4,0},{5,7},{6,2},{7,5},{8,12},{9,11},{10,... | collective-permute-start | bytes 884744 | tf_op jit(solution)/shard_map/ppermute | solution.py:376
  28.3 0.3 collective-permute-done.5.fb
  28.6 1.6 %shard_map.53 = (f32[8,768]{1,0:T(8,128)S(1)}, f32[64,768]{1,0:T(8,128)S(1)}, bf16[768,1152]{1,0:T(8,128)(2,1)S(1)}) custom-call(s32[1,1024]{1,0:T(1,128)S(1)} %get-tuple-element.15.codes, bf16[512,1152]{1,0:T(8,128)(2,1)S(1)} %get-tuple-element.16.early, f32[8,512]{1,0:T(8,128)S(1)} %get-tuple-element.17.before.refs_3_, ...), custom_call_target="tpu_custom_call" | custom-call | tf_op jit(solution)/shard_map/pallas_call | solution.py:333
  30.3 1.6 %collective-permute-done.7.late.middle.refs_2_ = bf16[128,1152]{1,0:T(8,128)(2,1)S(1)} collective-permute-done((bf16[128,1152]{1,0:T(8,128)(2,1)S(1)}, bf16[128,1152]{1,0:T(8,128)(2,1)S(1)}, u32[]{:S(2)}, u32[]{:S(2)}) %collective-permute-start.7) | collective-permute-done | bytes 294944 | tf_op jit(solution)/shard_map/ppermute | solution.py:376
  31.9 1.2 %shard_map.55 = (f32[8,896]{1,0:T(8,128)S(1)}, f32[64,896]{1,0:T(8,128)S(1)}) custom-call(s32[1,1024]{1,0:T(1,128)S(1)} %get-tuple-element.15.codes, bf16[768,1152]{1,0:T(8,128)(2,1)S(1)} %get-tuple-element.19.early, f32[8,768]{1,0:T(8,128)S(1)} %get-tuple-element.20.before, f32[64,768]{1,0:T(8,128)S(1)} %get-tuple-element.21.part_strip, ...), custom_call_target="tpu_custom_call" | custom-call | tf_op jit(solution)/shard_map/pallas_call | solution.py:333
  33.1 0.0 collective-permute-done.9.late
  33.1 0.1 shard_map.59
  33.2 0.1 collective-permute-start.11
  33.3 1.6 %shard_map.58 = (f32[40,1024]{1,0:T(8,128)S(1)}, f32[40,1024]{1,0:T(8,128)S(1)}) custom-call(s32[1,1024]{1,0:T(1,128)S(1)} %get-tuple-element.15.codes, bf16[768,1152]{1,0:T(8,128)(2,1)S(1)} %get-tuple-element.19.early, bf16[128,1152]{1,0:T(8,128)(2,1)S(1)} %collective-permute-done.7.late.middle.refs_2_, f32[8,896]{1,0:T(8,128)S(1)} %get-tuple-element.22.before.refs_5_, ...), custom_call_target="tpu_custom_call" | custom-call | tf_op jit(solution)/shard_map/pallas_call | solution.py:333
  34.9 0.6 %collective-permute-start.10 = (f32[40,1024]{1,0:T(8,128)S(1)}, f32[40,1024]{1,0:T(8,128)S(1)}, u32[]{:S(2)}, u32[]{:S(2)}) collective-permute-start(f32[40,1024]{1,0:T(8,128)S(1)} %get-tuple-element.25), channel_id=1, source_target_pairs={{0,1},{1,0},{2,3},{3,2},{4,5},{5,4},{6,7},{7,6},{8,9},{9,8},{10,11... | collective-permute-start | bytes 491528 | tf_op jit(solution)/shard_map/ppermute | solution.py:376
  35.4 1.0 %collective-permute-done.10.recv = f32[40,1024]{1,0:T(8,128)S(1)} collective-permute-done((f32[40,1024]{1,0:T(8,128)S(1)}, f32[40,1024]{1,0:T(8,128)S(1)}, u32[]{:S(2)}, u32[]{:S(2)}) %collective-permute-start.10) | collective-permute-done | bytes 163872 | tf_op jit(solution)/shard_map/ppermute | solution.py:376
  36.5 0.0 collective-permute-done.11.later
  36.5 2.0 %shard_map.60 = (f32[32,1152]{1,0:T(8,128)}, f32[1,32]{1,0:T(1,128)}) custom-call(s32[1,1024]{1,0:T(1,128)S(1)} %get-tuple-element.15.codes, f32[40,1024]{1,0:T(8,128)S(1)} %get-tuple-element.24.keep, f32[40,1024]{1,0:T(8,128)S(1)} %collective-permute-done.10.recv, bf16[768,1152]{1,0:T(8,128)(2,1)S(1)} %get-tuple-element.19.early, ...), custom_call_target="tpu_custom_call" | custom-call | tf_op jit(solution)/shard_map/pallas_call | solution.py:333
  (10 shorter events, 0.2 us)
Async XLA Ops:
  0.6 1.1 %copy-start = (bf16[2,128,1152]{2,1,0:T(8,128)(2,1)S(1)}, bf16[2,128,1152]{2,1,0:T(8,128)(2,1)}, u32[]{:S(2)}) copy-start(bf16[2,128,1152]{2,1,0:T(8,128)(2,1)} %param.3) | copy-start | bytes 1769476
  1.7 11.2 %collective-permute-start.2 = (bf16[64,1152]{1,0:T(8,128)(2,1)S(1)}, bf16[64,1152]{1,0:T(8,128)(2,1)S(1)}, u32[]{:S(2)}, u32[]{:S(2)}) collective-permute-start(bf16[64,1152]{1,0:T(8,128)(2,1)S(1)} %dynamic-slice_bitcast_fusion.1), channel_id=1, source_target_pairs={{0,16},{1,17},{2,18},{3,19},{4,20},{5,21},{6,22},{7,23},{8,24},{9,... | collective-permute-start | bytes 442376 | tf_op jit(solution)/shard_map/ppermute | solution.py:376
  5.9 13.9 %collective-permute-start.1 = (bf16[128,1152]{1,0:T(8,128)(2,1)S(1)}, bf16[128,1152]{1,0:T(8,128)(2,1)S(1)}, u32[]{:S(2)}, u32[]{:S(2)}) collective-permute-start(bf16[128,1152]{1,0:T(8,128)(2,1)S(1)} %dynamic-slice_bitcast_fusion.refs_0_), channel_id=1, source_target_pairs={{0,8},{1,9},{2,10},{3,11},{4,12},{5,13},{6,14},{7,15},{8,0},{9,1},... | collective-permute-start | bytes 884744 | tf_op jit(solution)/shard_map/ppermute | solution.py:376
  7.5 12.2 %collective-permute-start = (bf16[128,1152]{1,0:T(8,128)(2,1)S(1)}, bf16[128,1152]{1,0:T(8,128)(2,1)S(1)}, u32[]{:S(2)}, u32[]{:S(2)}) collective-permute-start(bf16[128,1152]{1,0:T(8,128)(2,1)S(1)} %dynamic-slice_bitcast_fusion.refs_0_), channel_id=1, source_target_pairs={{0,4},{1,5},{2,6},{3,7},{4,0},{5,1},{6,2},{7,3},{8,12},{9,13},{10,... | collective-permute-start | bytes 884744 | tf_op jit(solution)/shard_map/ppermute | solution.py:376
  13.0 6.8 %collective-permute-start.4 = (bf16[80,1152]{1,0:T(8,128)(2,1)S(1)}, bf16[80,1152]{1,0:T(8,128)(2,1)S(1)}, u32[]{:S(2)}, u32[]{:S(2)}) collective-permute-start(bf16[80,1152]{1,0:T(8,128)(2,1)S(1)} %shard_map.51), channel_id=1, source_target_pairs={{0,2},{1,5},{2,0},{3,7},{4,6},{5,1},{6,4},{7,3},{8,10},{9,13},{10,... | collective-permute-start | bytes 552968 | tf_op jit(solution)/shard_map/ppermute | solution.py:376
  14.6 5.1 %collective-permute-start.3 = (bf16[64,1152]{1,0:T(8,128)(2,1)S(1)}, bf16[64,1152]{1,0:T(8,128)(2,1)S(1)}, u32[]{:S(2)}, u32[]{:S(2)}) collective-permute-start(bf16[64,1152]{1,0:T(8,128)(2,1)S(1)} %collective-permute-done.2.refs_3_.refs_0_), channel_id=1, source_target_pairs={{0,8},{1,9},{2,10},{3,11},{4,12},{5,13},{6,14},{7,15},{8,0},{9,1},... | collective-permute-start | bytes 442376 | tf_op jit(solution)/shard_map/ppermute | solution.py:376
  19.8 4.6 %copy-start.1 = (s32[1024]{0:T(1024)S(1)}, s32[1024]{0:T(1024)}, u32[]{:S(2)}) copy-start(s32[1024]{0:T(1024)} %param.4) | copy-start | bytes 12292
  19.9 6.2 %collective-permute-start.8 = (bf16[512,1152]{1,0:T(8,128)(2,1)S(1)}, bf16[512,1152]{1,0:T(8,128)(2,1)S(1)}, u32[]{:S(2)}, u32[]{:S(2)}) collective-permute-start(bf16[512,1152]{1,0:T(8,128)(2,1)S(1)} %shard_map.56), channel_id=1, source_target_pairs={{0,1},{1,0},{2,3},{3,2},{4,5},{5,4},{6,7},{7,6},{8,9},{9,8},{10,11... | collective-permute-start | bytes 3538952 | tf_op jit(solution)/shard_map/ppermute | solution.py:376
  19.9 6.1 %collective-permute-start.6 = (bf16[64,1152]{1,0:T(8,128)(2,1)S(1)}, bf16[64,1152]{1,0:T(8,128)(2,1)S(1)}, u32[]{:S(2)}, u32[]{:S(2)}) collective-permute-start(bf16[64,1152]{1,0:T(8,128)(2,1)S(1)} %collective-permute-done.3.refs_4_.refs_3_.refs_1_.refs_0_), channel_id=1, source_target_pairs={{0,2},{1,5},{2,0},{3,7},{4,6},{5,1},{6,4},{7,3},{8,10},{9,13},{10,... | collective-permute-start | bytes 442376 | tf_op jit(solution)/shard_map/ppermute | solution.py:376
  21.4 7.2 %collective-permute-start.5 = (bf16[144,1152]{1,0:T(8,128)(2,1)S(1)}, bf16[144,1152]{1,0:T(8,128)(2,1)S(1)}, u32[]{:S(2)}, u32[]{:S(2)}) collective-permute-start(bf16[144,1152]{1,0:T(8,128)(2,1)S(1)} %shard_map.52), channel_id=1, source_target_pairs={{0,4},{1,3},{2,6},{3,1},{4,0},{5,7},{6,2},{7,5},{8,12},{9,11},{10,... | collective-permute-start | bytes 995336 | tf_op jit(solution)/shard_map/ppermute | solution.py:376
  23.0 8.8 %collective-permute-start.7 = (bf16[128,1152]{1,0:T(8,128)(2,1)S(1)}, bf16[128,1152]{1,0:T(8,128)(2,1)S(1)}, u32[]{:S(2)}, u32[]{:S(2)}) collective-permute-start(bf16[128,1152]{1,0:T(8,128)(2,1)S(1)} %shard_map.54), channel_id=1, source_target_pairs={{0,8},{1,9},{2,10},{3,11},{4,12},{5,13},{6,14},{7,15},{8,0},{9,1},... | collective-permute-start | bytes 884744 | tf_op jit(solution)/shard_map/ppermute | solution.py:376
  26.1 7.0 %collective-permute-start.9 = (bf16[128,1152]{1,0:T(8,128)(2,1)S(1)}, bf16[128,1152]{1,0:T(8,128)(2,1)S(1)}, u32[]{:S(2)}, u32[]{:S(2)}) collective-permute-start(bf16[128,1152]{1,0:T(8,128)(2,1)S(1)} %shard_map.57), channel_id=1, source_target_pairs={{0,4},{1,3},{2,6},{3,1},{4,0},{5,7},{6,2},{7,5},{8,12},{9,11},{10,... | collective-permute-start | bytes 884744 | tf_op jit(solution)/shard_map/ppermute | solution.py:376
  33.2 3.2 %collective-permute-start.11 = (bf16[512,1152]{1,0:T(8,128)(2,1)S(1)}, bf16[512,1152]{1,0:T(8,128)(2,1)S(1)}, u32[]{:S(2)}, u32[]{:S(2)}) collective-permute-start(bf16[512,1152]{1,0:T(8,128)(2,1)S(1)} %shard_map.59), channel_id=1, source_target_pairs={{0,1},{1,0},{2,3},{3,2},{4,5},{5,4},{6,7},{7,6},{8,9},{9,8},{10,11... | collective-permute-start | bytes 3538952 | tf_op jit(solution)/shard_map/ppermute | solution.py:376
  34.9 1.6 %collective-permute-start.10 = (f32[40,1024]{1,0:T(8,128)S(1)}, f32[40,1024]{1,0:T(8,128)S(1)}, u32[]{:S(2)}, u32[]{:S(2)}) collective-permute-start(f32[40,1024]{1,0:T(8,128)S(1)} %get-tuple-element.25), channel_id=1, source_target_pairs={{0,1},{1,0},{2,3},{3,2},{4,5},{5,4},{6,7},{7,6},{8,9},{9,8},{10,11... | collective-permute-start | bytes 491528 | tf_op jit(solution)/shard_map/ppermute | solution.py:376

commit v6 on v5

--- a/solution.py
+++ b/solution.py
@@ -99,7 +99,10 @@
     left = lax.broadcasted_iota(jnp.int32, cut[0].shape, 1) < half
     other = [None] * 4 + [pltpu.roll(v, half, 1) for v in cut[4:]]
     even = core == 0
-    order = cut[:3] + [
+    order = [
+        cut[0],
+        cut[2],
+        cut[1],
         jnp.where(left, cut[4], other[6]),
         jnp.where(left, other[4], other[5]),
         jnp.where(left, other[5], jnp.where(even, cut[6], other[7])),
@@ -193,7 +196,9 @@
     strip[:, last] = jnp.where(x == 0, turned[: block // 2], turned[block // 2 :])
 
 
-def second_kernel(codes, early, before, part_strip, fa, fb, ga, stats, strip, whole, wide, square):
+def second_kernel(
+    codes, early, before, part_strip, level_index, fa, fb, ga, stats, strip, whole, level, wide, square
+):
     _, x, core = position()
     head, half = early.shape[0], ga.shape[0]
     late = whole.at[head:, :]
@@ -205,27 +210,27 @@
     strip[:, 0:head] = part_strip[...]
     add_rows(codes, [early], late, before, stats, strip, wide, square)
     stats[1 + CODES :, :] = jnp.zeros((stats.shape[0] - 1 - CODES, stats.shape[1]), jnp.float32)
-
-
-def third_kernel(codes, early, before, part_strip, late, stats, strip, wide, square):
+    theirs = jnp.where(
+        core == 0, fa[half : half + 1, 0:1], fb[2 * half : 2 * half + 1, 0:1]
+    ).astype(jnp.float32)
+    row = lax.broadcasted_iota(jnp.int32, level.shape, 0)
+    level[...] = jnp.where(row == 0, level_index[0].astype(jnp.float32), theirs)
+
+
+def third_kernel(codes, early, before, part_strip, late, _, stats, strip, wide, square):
     strip[:, 0 : early.shape[0]] = part_strip[...]
     add_rows(codes, [early], late, before, stats, strip, wide, square)
     stats[1 + CODES :, :] = jnp.zeros((stats.shape[0] - 1 - CODES, stats.shape[1]), jnp.float32)
 
 
-def last_kernel(
-    codes, early, middle, before, part_strip, level_index, fa, fb, late, keep, send, strip, wide, square
-):
+def last_kernel(codes, early, middle, before, part_strip, late, keep, send, strip, wide, square):
     _, x, core = position()
     block = late.shape[0]
     half = block // 4
     strip[:, 0 : before.shape[1]] = part_strip[...]
     stats = keep.at[half:, :]
     add_rows(codes, [early, middle], late, before, stats, strip, wide, square)
-    lane = lax.broadcasted_iota(jnp.int32, (1, stats.shape[1]), 1)
-    level = level_index[0].astype(jnp.float32)
-    theirs = jnp.where(core == 0, fa[block // 2 : block // 2 + 1, 0:1], fb[block : block + 1, 0:1])
-    stats[1 + CODES :, :] = jnp.where(lane < 128, level, theirs.astype(jnp.float32))
+    stats[1 + CODES :, :] = jnp.zeros((stats.shape[0] - 1 - CODES, stats.shape[1]), jnp.float32)
     keep[0:half, :] = strip[spot(core, half), :]
     send[0:half, :] = strip[spot(1 - core, half), :]
     send[half:, :] = stats[...]
@@ -234,70 +239,78 @@
     send[:, -block:] = right
 
 
-class Mixer:
-    def __init__(self, own, width, codes, keep, recv, turned):
+def counted(*levels):
+    row = lax.broadcasted_iota(jnp.int32, (8, 1), 0).astype(jnp.float32) - 1.0
+    found = [ref[i : i + 1, 0:1] for ref in levels for i in (0, 1)]
+    return sum(jnp.where(row == level, 1.0, 0.0) for level in found)
+
+
+class Half:
+    def __init__(self, own, width, codes, box, count, turned):
         _, x, core = position()
-        self.codes, self.width = codes, width
-        self.rows = rows = keep.shape[0] - 8
-        self.student = core == 1
-        self.keep, self.recv = keep, recv
-        block = 4 * rows
-        own = spot(own, block)
-        code = codes[:, own].astype(jnp.float32)
-        turned[0] = self.pick(rows, rows + 8, own, True).T
-        turned[1] = self.pick(rows, rows + 8, own, False).T
-        turned[2] = jnp.broadcast_to(code, (8, block)).T
+        rows = box.shape[0] - 8
+        self.codes, self.width, self.count = codes, width, count
+        self.gram, self.stats = box.at[0:rows, :], box.at[rows : rows + 8, :]
+        own = spot(own, 4 * rows)
+        beta, weight, stats = self.lines(own)
+        row = lax.broadcasted_iota(jnp.int32, stats.shape, 0)
+        inner = (row > 0) & (row <= CODES)
+        lse = jnp.where(inner, count * (beta * stats[0:1] + jnp.log(stats)), 0.0)
+        lse = jnp.sum(lse, axis=0, keepdims=True)
+        turned[0] = jnp.where(inner, weight, jnp.where(row == 0, stats, lse)).T
+        turned[1] = (beta * LOG2E).T
         mine = spot(2 * x + core, rows)
-        s, t = turned[0, mine, :], turned[1, mine, :]
-        self.beta = widths(turned[2, mine, 0:1], width)
-        found = [
-            ref[rows + 1 + CODES : rows + 2 + CODES, lane : lane + 1]
-            for ref in (keep, recv)
-            for lane in (0, 128)
-        ]
-        self.count = [sum(jnp.where(v == jnp.float32(c), 1.0, 0.0) for v in found) for c in range(CODES)]
-        self.s_top, self.t_top = s[:, 0:1], t[:, 0:1]
-        self.s_sum = [s[:, 1 + c : 2 + c] for c in range(CODES)]
-        self.t_sum = [t[:, 1 + c : 2 + c] for c in range(CODES)]
-
-    def pick(self, low, high, cols, student):
-        here, there = self.keep[low:high, cols], self.recv[low:high, cols]
-        return jnp.where(self.student == student, here, there)
-
-    def weighted(self, d, beta, sums):
-        e = powers(d, beta[5] * LOG2E, beta[4] * LOG2E)
-        return sum(v * (n * b / s) for v, n, b, s in zip(e, self.count, beta, sums))
+        lead, base = turned[0, mine, :], turned[1, mine, :]
+        self.top, self.lse = lead[:, 0:1], lead[:, 7:8]
+        self.weight = [lead[:, 1 + c : 2 + c] for c in range(CODES)]
+        self.bases = base[:, 6:7], base[:, 5:6]
+
+    def lines(self, cols):
+        stats = self.stats[:, cols]
+        row = lax.broadcasted_iota(jnp.int32, stats.shape, 0)
+        code = self.codes[:, cols].astype(jnp.float32)
+        beta = jnp.exp2(0.5 * (code - (row.astype(jnp.float32) - 1.0))) / jnp.sqrt(
+            jnp.float32(self.width)
+        )
+        stats = jnp.where((row > CODES), 1.0, stats)
+        return beta, self.count * beta / jnp.where(row == 0, 1.0, stats), stats
 
     def part(self, cols):
-        rows = self.rows
-        gs, gt = self.pick(0, rows, cols, True), self.pick(0, rows, cols, False)
-        s, t = self.pick(rows, rows + 8, cols, True), self.pick(rows, rows + 8, cols, False)
-        beta = widths(self.codes[:, cols].astype(jnp.float32), self.width)
-        lines = lambda a: [a[1 + c : 2 + c] for c in range(CODES)]
-        p_row = self.weighted(gt - self.t_top, self.beta, self.t_sum)
-        q_row = self.weighted(gs - self.s_top, self.beta, self.s_sum)
-        p_col = self.weighted(gt - t[0:1], beta, lines(t))
-        q_col = self.weighted(gs - s[0:1], beta, lines(s))
-        mix = WEIGHT * ((q_row - p_row) + (q_col - p_col))
-        return mix.astype(jnp.bfloat16), jnp.sum(p_row * (gt - gs), axis=1, keepdims=True)
-
-    def store_loss(self, loss, out):
-        for c in range(CODES):
-            loss = loss + self.count[c] * (
-                self.beta[c] * (self.s_top - self.t_top)
-                + (jnp.log(self.s_sum[c]) - jnp.log(self.t_sum[c]))
-            )
-        out[...] = jnp.broadcast_to(loss, (self.rows, 128)).T[0:1, :]
+        gram = self.gram[:, cols]
+        beta, weight, stats = self.lines(cols)
+        by_row = sum(v * w for v, w in zip(powers(gram - self.top, *self.bases), self.weight))
+        e = powers(gram - stats[0:1], beta[6:7] * LOG2E, beta[5:6] * LOG2E)
+        by_col = sum(v * weight[1 + c : 2 + c] for c, v in enumerate(e))
+        return by_row, by_row + by_col
 
 
 def product(a, b):
     return jnp.dot(a, b, preferred_element_type=jnp.float32)
 
 
-def mix_kernel(codes, keep, recv, early, middle, late, sooner, later, out, loss, turned):
-    mixer = Mixer(0, out.shape[1], codes, keep, recv, turned)
-    mix, gap = mixer.part(pl.ds(0, codes.shape[1]))
-    mixer.store_loss(gap, loss)
+def store_loss(gap, difference, out):
+    out[...] = jnp.broadcast_to(gap + difference, (gap.shape[0], 128)).T[0:1, :]
+
+
+def half_kernel(width, codes, keep, level, their_level, by_row, both, lse, turned):
+    half = Half(0, width, codes, keep, counted(level, their_level), turned)
+    by_row[...], both[...] = half.part(pl.ds(0, codes.shape[1]))
+    lse[...] = jnp.broadcast_to(half.lse, lse.shape)
+
+
+def mix_kernel(
+    codes, keep, recv, level, their_level, by_row, both, lse, early, middle, late, sooner, later,
+    out, loss, turned
+):
+    half = Half(0, out.shape[1], codes, recv, counted(level, their_level), turned)
+    student = position()[2] == 1
+    their_row, their_both = half.part(pl.ds(0, codes.shape[1]))
+    sign = jnp.where(student, 1.0, -1.0)
+    mix = ((WEIGHT * sign) * (both[...] - their_both)).astype(jnp.bfloat16)
+    rows = by_row.shape[0]
+    p_row = jnp.where(student, their_row, by_row[...])
+    gap = jnp.sum(p_row * (recv[0:rows, :] - keep[0:rows, :]), axis=1, keepdims=True)
+    store_loss(sign * gap, sign * (lse[:, 0:1] - half.lse), loss)
 
     def against(*parts):
         row, total = 0, None
@@ -306,27 +319,32 @@
             row, total = row + part.shape[0], term if total is None else total + term
         out[...] = total
 
-    @pl.when(mixer.student)
+    @pl.when(student)
     def _():
         against(early, middle, late)
 
-    @pl.when(jnp.logical_not(mixer.student))
+    @pl.when(jnp.logical_not(student))
     def _():
         against(sooner, later)
 
 
-def wide_mix_kernel(codes, keep, recv, student, out, loss, turned):
+def wide_mix_kernel(codes, s_box, t_box, level, their_level, student, out, loss, turned):
     total, width = student.shape
-    mixer = Mixer(lax.axis_index("batch"), width, codes, keep, recv, turned)
-    span = min(SPAN, total)
+    own, count = lax.axis_index("batch"), counted(level, their_level)
+    s = Half(own, width, codes, s_box, count, turned.at[0:2])
+    t = Half(own, width, codes, t_box, count, turned.at[2:4])
+    span, rows = min(SPAN, total), out.shape[0]
 
     def step(i, carry):
-        mix, gap = mixer.part(at(i, span))
-        return carry[0] + product(mix, student[at(i, span), :]), carry[1] + gap
-
-    zero = jnp.zeros((mixer.rows, width), jnp.float32), jnp.zeros((mixer.rows, 1), jnp.float32)
+        cols = at(i, span)
+        (_, q), (p_row, p) = s.part(cols), t.part(cols)
+        gap = jnp.sum(p_row * (t_box[0:rows, cols] - s_box[0:rows, cols]), axis=1, keepdims=True)
+        mix = (WEIGHT * (q - p)).astype(jnp.bfloat16)
+        return carry[0] + product(mix, student[cols, :]), carry[1] + gap
+
+    zero = jnp.zeros((rows, width), jnp.float32), jnp.zeros((rows, 1), jnp.float32)
     out[...], gap = lax.fori_loop(0, total // span, step, zero)
-    mixer.store_loss(gap, loss)
+    store_loss(gap, s.lse - t.lse, loss)
 
 
 def call(kernel, shapes, scratch, limit, *args):
@@ -392,9 +410,8 @@
             codes,
             whole,
         )
-        lane = jnp.arange(total)[None, :]
-        line = jnp.where(lane < 128, level_index[0], theirs[0]).astype(jnp.float32)
-        stats = jnp.concatenate([stats[: 1 + CODES], line])
+        level = jnp.stack([level_index, theirs] + [theirs] * 6).astype(jnp.float32)
+        level = jnp.broadcast_to(level, (8, 128))
         share = lambda c: lax.dynamic_slice_in_dim(strip, c * half, half)
         keep = jnp.concatenate([share(core), stats])
         recv = send(jnp.concatenate([share(1 - core), stats]), over_core)
@@ -402,11 +419,13 @@
         out, loss = call(
             wide_mix_kernel,
             out_shapes,
-            [pltpu.VMEM((3, block, 8), jnp.float32)],
+            [pltpu.VMEM((4, block, 8), jnp.float32)],
             56,
             codes,
-            keep,
-            recv,
+            jnp.where(core == 1, keep, recv),
+            jnp.where(core == 1, recv, keep),
+            level,
+            send(level, over_core),
             student,
         )
         return out, loss[0]
@@ -425,7 +444,7 @@
     fa = send(join([f, level]), turn)
     fb = send(join([f, fa[:rows], level], g), return_turn)
     ga = send(g, turn)
-    sooner = send(join([u, y, n, f, g], fa), over_core)
+    sooner = send(join([join([u, n]), y, f, g], fa), over_core)
     some, head = 4 * block, 6 * block
     codes, a_stats, a_strip, a_rows = call(
         functools.partial(first_kernel, True),
@@ -439,25 +458,32 @@
         16,
         codes,
         u,
+        n,
         y,
-        n,
         f,
         g,
     )
     gb = send(join([g, ga], sooner, a_stats), return_turn)
-    b_stats, b_strip, b_rows = call(
+    b_stats, b_strip, b_rows, levels = call(
         second_kernel,
-        [shape(8, head), shape(rows, head), shape(head, width, dtype=jnp.bfloat16)],
+        [
+            shape(8, head),
+            shape(rows, head),
+            shape(head, width, dtype=jnp.bfloat16),
+            shape(8, 128),
+        ],
         room(head - some, head),
         16,
         codes,
         a_rows,
         a_stats,
         a_strip,
+        level_index,
         fa,
         fb,
         ga,
     )
+    their_levels = send(levels, over_core)
     c_stats, c_strip = call(
         third_kernel,
         [shape(8, total - block), shape(rows, total - block)],
@@ -468,6 +494,7 @@
         b_stats,
         b_strip,
         ny,
+        their_levels,
     )
     later = send(
         join([b_rows[some : some + 3 * rows], gb[:rows], ny, ga, gb[rows:]], c_stats), over_core
@@ -482,20 +509,32 @@
         ny,
         c_stats,
         c_strip,
-        level_index,
-        fa,
-        fb,
         gb,
     )
     recv = send(mail, over_core)
+    by_row, both, lse = call(
+        functools.partial(half_kernel, width),
+        [shape(half, total), shape(half, total), shape(half, 8)],
+        [pltpu.VMEM((2, block, 8), jnp.float32)],
+        16,
+        codes,
+        keep,
+        levels,
+        their_levels,
+    )
     out, loss = call(
         mix_kernel,
         out_shapes,
-        [pltpu.VMEM((3, block, 8), jnp.float32)],
+        [pltpu.VMEM((2, block, 8), jnp.float32)],
         16,
         codes,
         keep,
         recv,
+        levels,
+        their_levels,
+        by_row,
+        both,
+        lse,
         b_rows,
         ny,
         gb,

time: 38.7 us -> 38.4 us (level)
  waiting for transfers between devices: 10.7 us -> 10 us
    ppermute x12 -> x13, waiting for transfers between devices: 10.7 us -> 10 us  [send(): return lax.ppermute(a, ALL, pairs)]
    ppermute x12 -> x13, starting transfers between devices: 16.9 us -> 17.2 us  [send(): return lax.ppermute(a, ALL, pairs)]
    pallas_call x11 -> x13, Pallas kernels: 8.22 us -> 8.44 us  [call(): pl.pallas_call(kernel, out_shape=shapes, in_specs=[SMEM if a.shape == (1,...]
  transfers between devices with their start and end apart: 12 -> 13, of which waited for: 5 -> 6; matrix products, arithmetic and copies ran while one was open for 0% -> 0% of each run, Pallas kernels for 16% -> 17%
where the time goes in v6:
time: 38.4 us; the launch traced here: 38.3 us
  starting transfers between devices  17.2 us (45%)
  waiting for transfers between devices  10 us (26%)
  Pallas kernels  8.44 us (22%)
  between operations  1.49 us (4%)
  local copies, waits for them, and re-layouts  1.18 us (3%)
    ppermute x13, starting transfers between devices, send(): return lax.ppermute(a, ALL, pairs)  17.2 us
    ppermute x13, waiting for transfers between devices, send(): return lax.ppermute(a, ALL, pairs)  10 us
    pallas_call x13, Pallas kernels, call(): pl.pallas_call(kernel, out_shape=shapes, in_specs=[SMEM if a.shape == (1,...  8.44 us
    unnamed x4, local copies, waits for them, and re-layouts  1.04 us
  transfers between devices with their start and end apart: 13, of which 6 were waited for; matrix products, arithmetic and copies ran while one was open for 0% of the time, Pallas kernels for 17%

profile of v6, /device:TPU:0, one launch (start us, length us, event | category | flops | bytes accessed | tf_op | source)
XLA Modules:
  0.0 38.3 jit_solution(9738225223640167770)
XLA Ops:
  0.6 0.0 copy-start
  0.7 1.0 %copy-done = bf16[2,128,1152]{2,1,0:T(8,128)(2,1)S(1)} copy-done((bf16[2,128,1152]{2,1,0:T(8,128)(2,1)S(1)}, bf16[2,128,1152]{2,1,0:T(8,128)(2,1)}, u32[]{:S(2)}) %copy-start) | copy-done | bytes 589848
  1.7 4.1 %collective-permute-start.2 = (bf16[64,1152]{1,0:T(8,128)(2,1)S(1)}, bf16[64,1152]{1,0:T(8,128)(2,1)S(1)}, u32[]{:S(2)}, u32[]{:S(2)}) collective-permute-start(bf16[64,1152]{1,0:T(8,128)(2,1)S(1)} %dynamic-slice_bitcast_fusion.1), channel_id=1, source_target_pairs={{0,16},{1,17},{2,18},{3,19},{4,20},{5,21},{6,22},{7,23},{8,24},{9,... | collective-permute-start | bytes 442376 | tf_op jit(solution)/shard_map/ppermute | solution.py:394
  5.9 1.6 %collective-permute-start = (bf16[128,1152]{1,0:T(8,128)(2,1)S(1)}, bf16[128,1152]{1,0:T(8,128)(2,1)S(1)}, u32[]{:S(2)}, u32[]{:S(2)}) collective-permute-start(bf16[128,1152]{1,0:T(8,128)(2,1)S(1)} %dynamic-slice_bitcast_fusion.refs_0_), channel_id=1, source_target_pairs={{0,8},{1,9},{2,10},{3,11},{4,12},{5,13},{6,14},{7,15},{8,0},{9,1},... | collective-permute-start | bytes 884744 | tf_op jit(solution)/shard_map/ppermute | solution.py:394
  7.5 1.5 %collective-permute-start.1 = (bf16[128,1152]{1,0:T(8,128)(2,1)S(1)}, bf16[128,1152]{1,0:T(8,128)(2,1)S(1)}, u32[]{:S(2)}, u32[]{:S(2)}) collective-permute-start(bf16[128,1152]{1,0:T(8,128)(2,1)S(1)} %dynamic-slice_bitcast_fusion.refs_0_), channel_id=1, source_target_pairs={{0,4},{1,5},{2,6},{3,7},{4,0},{5,1},{6,2},{7,3},{8,12},{9,13},{10,... | collective-permute-start | bytes 884744 | tf_op jit(solution)/shard_map/ppermute | solution.py:394
  9.7 3.3 %collective-permute-done.2.refs_3_.refs_0_.refs_2_ = bf16[64,1152]{1,0:T(8,128)(2,1)S(1)} collective-permute-done((bf16[64,1152]{1,0:T(8,128)(2,1)S(1)}, bf16[64,1152]{1,0:T(8,128)(2,1)S(1)}, u32[]{:S(2)}, u32[]{:S(2)}) %collective-permute-start.2) | collective-permute-done | bytes 147488 | tf_op jit(solution)/shard_map/ppermute | solution.py:394
  13.0 1.6 %collective-permute-start.4 = (bf16[80,1152]{1,0:T(8,128)(2,1)S(1)}, bf16[80,1152]{1,0:T(8,128)(2,1)S(1)}, u32[]{:S(2)}, u32[]{:S(2)}) collective-permute-start(bf16[80,1152]{1,0:T(8,128)(2,1)S(1)} %shard_map.51), channel_id=1, source_target_pairs={{0,2},{1,5},{2,0},{3,7},{4,6},{5,1},{6,4},{7,3},{8,10},{9,13},{10,... | collective-permute-start | bytes 552968 | tf_op jit(solution)/shard_map/ppermute | solution.py:394
  14.6 0.6 %collective-permute-start.3 = (bf16[64,1152]{1,0:T(8,128)(2,1)S(1)}, bf16[64,1152]{1,0:T(8,128)(2,1)S(1)}, u32[]{:S(2)}, u32[]{:S(2)}) collective-permute-start(bf16[64,1152]{1,0:T(8,128)(2,1)S(1)} %collective-permute-done.2.refs_3_.refs_0_.refs_2_), channel_id=1, source_target_pairs={{0,8},{1,9},{2,10},{3,11},{4,12},{5,13},{6,14},{7,15},{8,0},{9,1},... | collective-permute-start | bytes 442376 | tf_op jit(solution)/shard_map/ppermute | solution.py:394
  15.2 1.7 %collective-permute-done.refs_1_ = bf16[128,1152]{1,0:T(8,128)(2,1)S(1)} collective-permute-done((bf16[128,1152]{1,0:T(8,128)(2,1)S(1)}, bf16[128,1152]{1,0:T(8,128)(2,1)S(1)}, u32[]{:S(2)}, u32[]{:S(2)}) %collective-permute-start) | collective-permute-done | bytes 294944 | tf_op jit(solution)/shard_map/ppermute | solution.py:394
  17.0 0.0 collective-permute-done.1.refs_2_.refs_0_.refs_1_
  17.0 2.8 %collective-permute-done.3.refs_4_.refs_3_.refs_1_.refs_0_ = bf16[64,1152]{1,0:T(8,128)(2,1)S(1)} collective-permute-done((bf16[64,1152]{1,0:T(8,128)(2,1)S(1)}, bf16[64,1152]{1,0:T(8,128)(2,1)S(1)}, u32[]{:S(2)}, u32[]{:S(2)}) %collective-permute-start.3) | collective-permute-done | bytes 147488 | tf_op jit(solution)/shard_map/ppermute | solution.py:394
  19.7 0.0 collective-permute-done.4.fa.refs_4_
  19.7 0.1 shard_map.57
  19.8 0.0 copy-start.1
  19.8 0.1 collective-permute-start.9
  19.9 1.4 %collective-permute-start.6 = (bf16[64,1152]{1,0:T(8,128)(2,1)S(1)}, bf16[64,1152]{1,0:T(8,128)(2,1)S(1)}, u32[]{:S(2)}, u32[]{:S(2)}) collective-permute-start(bf16[64,1152]{1,0:T(8,128)(2,1)S(1)} %collective-permute-done.3.refs_4_.refs_3_.refs_1_.refs_0_), channel_id=1, source_target_pairs={{0,2},{1,5},{2,0},{3,7},{4,6},{5,1},{6,4},{7,3},{8,10},{9,13},{10,... | collective-permute-start | bytes 442376 | tf_op jit(solution)/shard_map/ppermute | solution.py:394
  21.4 1.6 %collective-permute-start.5 = (bf16[144,1152]{1,0:T(8,128)(2,1)S(1)}, bf16[144,1152]{1,0:T(8,128)(2,1)S(1)}, u32[]{:S(2)}, u32[]{:S(2)}) collective-permute-start(bf16[144,1152]{1,0:T(8,128)(2,1)S(1)} %shard_map.52), channel_id=1, source_target_pairs={{0,4},{1,3},{2,6},{3,1},{4,0},{5,7},{6,2},{7,5},{8,12},{9,11},{10,... | collective-permute-start | bytes 995336 | tf_op jit(solution)/shard_map/ppermute | solution.py:394
  23.0 1.4 %collective-permute-start.7 = (bf16[128,1152]{1,0:T(8,128)(2,1)S(1)}, bf16[128,1152]{1,0:T(8,128)(2,1)S(1)}, u32[]{:S(2)}, u32[]{:S(2)}) collective-permute-start(bf16[128,1152]{1,0:T(8,128)(2,1)S(1)} %shard_map.54), channel_id=1, source_target_pairs={{0,8},{1,9},{2,10},{3,11},{4,12},{5,13},{6,14},{7,15},{8,0},{9,1},... | collective-permute-start | bytes 884744 | tf_op jit(solution)/shard_map/ppermute | solution.py:394
  24.4 0.0 copy-done.1
  24.4 1.6 %shard_map.50 = (s32[1,1024]{1,0:T(1,128)S(1)}, f32[8,512]{1,0:T(8,128)S(1)}, f32[64,512]{1,0:T(8,128)S(1)}, bf16[512,1152]{1,0:T(8,128)(2,1)S(1)}) custom-call(s32[1,1024]{1,0:T(1,128)S(1)} %bitcast.7, bf16[128,1152]{1,0:T(8,128)(2,1)S(1)} %dynamic-slice_bitcast_fusion.refs_0_, bf16[128,1152]{1,0:T(8,128)(2,1)S(1)} %collective-permute-done.refs_1_, ...), custom_call_target="tpu_custom_call" | custom-call | tf_op jit(solution)/shard_map/pallas_call | solution.py:351
  26.0 0.0 collective-permute-done.6.ga.refs_1_.refs_3_
  26.0 0.0 collective-permute-done.9.refs_2_.sooner
  26.0 2.3 %collective-permute-start.10 = (bf16[128,1152]{1,0:T(8,128)(2,1)S(1)}, bf16[128,1152]{1,0:T(8,128)(2,1)S(1)}, u32[]{:S(2)}, u32[]{:S(2)}) collective-permute-start(bf16[128,1152]{1,0:T(8,128)(2,1)S(1)} %shard_map.58), channel_id=1, source_target_pairs={{0,4},{1,3},{2,6},{3,1},{4,0},{5,7},{6,2},{7,5},{8,12},{9,11},{10,... | collective-permute-start | bytes 884744 | tf_op jit(solution)/shard_map/ppermute | solution.py:394
  28.3 0.3 collective-permute-done.5.fb
  28.6 1.6 %shard_map.53 = (f32[8,768]{1,0:T(8,128)S(1)}, f32[64,768]{1,0:T(8,128)S(1)}, bf16[768,1152]{1,0:T(8,128)(2,1)S(1)}, f32[8,128]{1,0:T(8,128)S(1)}) custom-call(s32[1,1024]{1,0:T(1,128)S(1)} %get-tuple-element.19.codes, bf16[512,1152]{1,0:T(8,128)(2,1)S(1)} %get-tuple-element.20.early, f32[8,512]{1,0:T(8,128)S(1)} %get-tuple-element.21.before.refs_3_, ...), custom_call_target="tpu_custom_call" | custom-call | tf_op jit(solution)/shard_map/pallas_call | solution.py:351
  30.2 0.3 collective-permute-start.8
  30.5 1.3 %collective-permute-done.7.late.middle.refs_2_ = bf16[128,1152]{1,0:T(8,128)(2,1)S(1)} collective-permute-done((bf16[128,1152]{1,0:T(8,128)(2,1)S(1)}, bf16[128,1152]{1,0:T(8,128)(2,1)S(1)}, u32[]{:S(2)}, u32[]{:S(2)}) %collective-permute-start.7) | collective-permute-done | bytes 294944 | tf_op jit(solution)/shard_map/ppermute | solution.py:394
  31.9 0.0 collective-permute-done.8._.their_level
  31.9 1.2 %shard_map.55 = (f32[8,896]{1,0:T(8,128)S(1)}, f32[64,896]{1,0:T(8,128)S(1)}) custom-call(s32[1,1024]{1,0:T(1,128)S(1)} %get-tuple-element.19.codes, bf16[768,1152]{1,0:T(8,128)(2,1)S(1)} %get-tuple-element.23.early, f32[8,768]{1,0:T(8,128)S(1)} %get-tuple-element.24.before, f32[64,768]{1,0:T(8,128)S(1)} %get-tuple-element.25.part_strip, ...), custom_call_target="tpu_custom_call" | custom-call | tf_op jit(solution)/shard_map/pallas_call | solution.py:351
  33.1 0.0 collective-permute-done.10.late
  33.1 0.1 shard_map.61
  33.2 0.1 collective-permute-start.12
  33.3 1.5 %shard_map.59 = (f32[40,1024]{1,0:T(8,128)S(1)}, f32[40,1024]{1,0:T(8,128)S(1)}) custom-call(s32[1,1024]{1,0:T(1,128)S(1)} %get-tuple-element.19.codes, bf16[768,1152]{1,0:T(8,128)(2,1)S(1)} %get-tuple-element.23.early, bf16[128,1152]{1,0:T(8,128)(2,1)S(1)} %collective-permute-done.7.late.middle.refs_2_, f32[8,896]{1,0:T(8,128)S(1)} %get-tuple-element.27.before.refs_5_, ...), custom_call_target="tpu_custom_call" | custom-call | tf_op jit(solution)/shard_map/pallas_call | solution.py:351
  34.8 0.6 %collective-permute-start.11 = (f32[40,1024]{1,0:T(8,128)S(1)}, f32[40,1024]{1,0:T(8,128)S(1)}, u32[]{:S(2)}, u32[]{:S(2)}) collective-permute-start(f32[40,1024]{1,0:T(8,128)S(1)} %get-tuple-element.30), channel_id=1, source_target_pairs={{0,1},{1,0},{2,3},{3,2},{4,5},{5,4},{6,7},{7,6},{8,9},{9,8},{10,11... | collective-permute-start | bytes 491528 | tf_op jit(solution)/shard_map/ppermute | solution.py:394
  35.4 0.4 %shard_map.60 = (f32[32,1024]{1,0:T(8,128)S(1)}, f32[32,1024]{1,0:T(8,128)S(1)}, f32[32,8]{1,0:T(8,128)S(1)}) custom-call(s32[1,1024]{1,0:T(1,128)S(1)} %get-tuple-element.19.codes, f32[40,1024]{1,0:T(8,128)S(1)} %get-tuple-element.29.keep, f32[8,128]{1,0:T(8,128)S(1)} %get-tuple-element.26.level, f32[8,128]{1,0:T(8,128)S(1)} %collective-permute-done.8._.their_level), custom_call_target="tpu_custom_call" | custom-call | tf_op jit(solution)/shard_map/pallas_call | solution.py:351
  35.8 0.6 %collective-permute-done.11.recv = f32[40,1024]{1,0:T(8,128)S(1)} collective-permute-done((f32[40,1024]{1,0:T(8,128)S(1)}, f32[40,1024]{1,0:T(8,128)S(1)}, u32[]{:S(2)}, u32[]{:S(2)}) %collective-permute-start.11) | collective-permute-done | bytes 163872 | tf_op jit(solution)/shard_map/ppermute | solution.py:394
  36.4 0.0 collective-permute-done.12.later
  36.4 1.8 %shard_map.62 = (f32[32,1152]{1,0:T(8,128)}, f32[1,32]{1,0:T(1,128)}) custom-call(s32[1,1024]{1,0:T(1,128)S(1)} %get-tuple-element.19.codes, f32[40,1024]{1,0:T(8,128)S(1)} %get-tuple-element.29.keep, f32[40,1024]{1,0:T(8,128)S(1)} %collective-permute-done.11.recv, f32[8,128]{1,0:T(8,128)S(1)} %get-tuple-element.26.level, ...), custom_call_target="tpu_custom_call" | custom-call | tf_op jit(solution)/shard_map/pallas_call | solution.py:351
  (11 shorter events, 0.3 us)
Async XLA Ops:
  0.6 1.1 %copy-start = (bf16[2,128,1152]{2,1,0:T(8,128)(2,1)S(1)}, bf16[2,128,1152]{2,1,0:T(8,128)(2,1)}, u32[]{:S(2)}) copy-start(bf16[2,128,1152]{2,1,0:T(8,128)(2,1)} %param.3) | copy-start | bytes 1769476
  1.7 11.2 %collective-permute-start.2 = (bf16[64,1152]{1,0:T(8,128)(2,1)S(1)}, bf16[64,1152]{1,0:T(8,128)(2,1)S(1)}, u32[]{:S(2)}, u32[]{:S(2)}) collective-permute-start(bf16[64,1152]{1,0:T(8,128)(2,1)S(1)} %dynamic-slice_bitcast_fusion.1), channel_id=1, source_target_pairs={{0,16},{1,17},{2,18},{3,19},{4,20},{5,21},{6,22},{7,23},{8,24},{9,... | collective-permute-start | bytes 442376 | tf_op jit(solution)/shard_map/ppermute | solution.py:394
  5.9 11.0 %collective-permute-start = (bf16[128,1152]{1,0:T(8,128)(2,1)S(1)}, bf16[128,1152]{1,0:T(8,128)(2,1)S(1)}, u32[]{:S(2)}, u32[]{:S(2)}) collective-permute-start(bf16[128,1152]{1,0:T(8,128)(2,1)S(1)} %dynamic-slice_bitcast_fusion.refs_0_), channel_id=1, source_target_pairs={{0,8},{1,9},{2,10},{3,11},{4,12},{5,13},{6,14},{7,15},{8,0},{9,1},... | collective-permute-start | bytes 884744 | tf_op jit(solution)/shard_map/ppermute | solution.py:394
  7.5 9.5 %collective-permute-start.1 = (bf16[128,1152]{1,0:T(8,128)(2,1)S(1)}, bf16[128,1152]{1,0:T(8,128)(2,1)S(1)}, u32[]{:S(2)}, u32[]{:S(2)}) collective-permute-start(bf16[128,1152]{1,0:T(8,128)(2,1)S(1)} %dynamic-slice_bitcast_fusion.refs_0_), channel_id=1, source_target_pairs={{0,4},{1,5},{2,6},{3,7},{4,0},{5,1},{6,2},{7,3},{8,12},{9,13},{10,... | collective-permute-start | bytes 884744 | tf_op jit(solution)/shard_map/ppermute | solution.py:394
  13.0 6.8 %collective-permute-start.4 = (bf16[80,1152]{1,0:T(8,128)(2,1)S(1)}, bf16[80,1152]{1,0:T(8,128)(2,1)S(1)}, u32[]{:S(2)}, u32[]{:S(2)}) collective-permute-start(bf16[80,1152]{1,0:T(8,128)(2,1)S(1)} %shard_map.51), channel_id=1, source_target_pairs={{0,2},{1,5},{2,0},{3,7},{4,6},{5,1},{6,4},{7,3},{8,10},{9,13},{10,... | collective-permute-start | bytes 552968 | tf_op jit(solution)/shard_map/ppermute | solution.py:394
  14.6 5.1 %collective-permute-start.3 = (bf16[64,1152]{1,0:T(8,128)(2,1)S(1)}, bf16[64,1152]{1,0:T(8,128)(2,1)S(1)}, u32[]{:S(2)}, u32[]{:S(2)}) collective-permute-start(bf16[64,1152]{1,0:T(8,128)(2,1)S(1)} %collective-permute-done.2.refs_3_.refs_0_.refs_2_), channel_id=1, source_target_pairs={{0,8},{1,9},{2,10},{3,11},{4,12},{5,13},{6,14},{7,15},{8,0},{9,1},... | collective-permute-start | bytes 442376 | tf_op jit(solution)/shard_map/ppermute | solution.py:394
  19.8 4.6 %copy-start.1 = (s32[1024]{0:T(1024)S(1)}, s32[1024]{0:T(1024)}, u32[]{:S(2)}) copy-start(s32[1024]{0:T(1024)} %param.4) | copy-start | bytes 12292
  19.8 6.2 %collective-permute-start.9 = (bf16[512,1152]{1,0:T(8,128)(2,1)S(1)}, bf16[512,1152]{1,0:T(8,128)(2,1)S(1)}, u32[]{:S(2)}, u32[]{:S(2)}) collective-permute-start(bf16[512,1152]{1,0:T(8,128)(2,1)S(1)} %shard_map.57), channel_id=1, source_target_pairs={{0,1},{1,0},{2,3},{3,2},{4,5},{5,4},{6,7},{7,6},{8,9},{9,8},{10,11... | collective-permute-start | bytes 3538952 | tf_op jit(solution)/shard_map/ppermute | solution.py:394
  19.9 6.1 %collective-permute-start.6 = (bf16[64,1152]{1,0:T(8,128)(2,1)S(1)}, bf16[64,1152]{1,0:T(8,128)(2,1)S(1)}, u32[]{:S(2)}, u32[]{:S(2)}) collective-permute-start(bf16[64,1152]{1,0:T(8,128)(2,1)S(1)} %collective-permute-done.3.refs_4_.refs_3_.refs_1_.refs_0_), channel_id=1, source_target_pairs={{0,2},{1,5},{2,0},{3,7},{4,6},{5,1},{6,4},{7,3},{8,10},{9,13},{10,... | collective-permute-start | bytes 442376 | tf_op jit(solution)/shard_map/ppermute | solution.py:394
  21.4 7.2 %collective-permute-start.5 = (bf16[144,1152]{1,0:T(8,128)(2,1)S(1)}, bf16[144,1152]{1,0:T(8,128)(2,1)S(1)}, u32[]{:S(2)}, u32[]{:S(2)}) collective-permute-start(bf16[144,1152]{1,0:T(8,128)(2,1)S(1)} %shard_map.52), channel_id=1, source_target_pairs={{0,4},{1,3},{2,6},{3,1},{4,0},{5,7},{6,2},{7,5},{8,12},{9,11},{10,... | collective-permute-start | bytes 995336 | tf_op jit(solution)/shard_map/ppermute | solution.py:394
  23.0 8.8 %collective-permute-start.7 = (bf16[128,1152]{1,0:T(8,128)(2,1)S(1)}, bf16[128,1152]{1,0:T(8,128)(2,1)S(1)}, u32[]{:S(2)}, u32[]{:S(2)}) collective-permute-start(bf16[128,1152]{1,0:T(8,128)(2,1)S(1)} %shard_map.54), channel_id=1, source_target_pairs={{0,8},{1,9},{2,10},{3,11},{4,12},{5,13},{6,14},{7,15},{8,0},{9,1},... | collective-permute-start | bytes 884744 | tf_op jit(solution)/shard_map/ppermute | solution.py:394
  26.0 7.0 %collective-permute-start.10 = (bf16[128,1152]{1,0:T(8,128)(2,1)S(1)}, bf16[128,1152]{1,0:T(8,128)(2,1)S(1)}, u32[]{:S(2)}, u32[]{:S(2)}) collective-permute-start(bf16[128,1152]{1,0:T(8,128)(2,1)S(1)} %shard_map.58), channel_id=1, source_target_pairs={{0,4},{1,3},{2,6},{3,1},{4,0},{5,7},{6,2},{7,5},{8,12},{9,11},{10,... | collective-permute-start | bytes 884744 | tf_op jit(solution)/shard_map/ppermute | solution.py:394
  30.2 1.7 %collective-permute-start.8 = (f32[8,128]{1,0:T(8,128)S(1)}, f32[8,128]{1,0:T(8,128)S(1)}, u32[]{:S(2)}, u32[]{:S(2)}) collective-permute-start(f32[8,128]{1,0:T(8,128)S(1)} %get-tuple-element.26.level), channel_id=1, source_target_pairs={{0,1},{1,0},{2,3},{3,2},{4,5},{5,4},{6,7},{7,6},{8,9},{9,8},{10,11... | collective-permute-start | bytes 12296 | tf_op jit(solution)/shard_map/ppermute | solution.py:394
  33.2 3.2 %collective-permute-start.12 = (bf16[512,1152]{1,0:T(8,128)(2,1)S(1)}, bf16[512,1152]{1,0:T(8,128)(2,1)S(1)}, u32[]{:S(2)}, u32[]{:S(2)}) collective-permute-start(bf16[512,1152]{1,0:T(8,128)(2,1)S(1)} %shard_map.61), channel_id=1, source_target_pairs={{0,1},{1,0},{2,3},{3,2},{4,5},{5,4},{6,7},{7,6},{8,9},{9,8},{10,11... | collective-permute-start | bytes 3538952 | tf_op jit(solution)/shard_map/ppermute | solution.py:394
  34.8 1.6 %collective-permute-start.11 = (f32[40,1024]{1,0:T(8,128)S(1)}, f32[40,1024]{1,0:T(8,128)S(1)}, u32[]{:S(2)}, u32[]{:S(2)}) collective-permute-start(f32[40,1024]{1,0:T(8,128)S(1)} %get-tuple-element.30), channel_id=1, source_target_pairs={{0,1},{1,0},{2,3},{3,2},{4,5},{5,4},{6,7},{7,6},{8,9},{9,8},{10,11... | collective-permute-start | bytes 491528 | tf_op jit(solution)/shard_map/ppermute | solution.py:394

commit v7 on v6

--- a/solution.py
+++ b/solution.py
@@ -46,19 +46,28 @@
 
 def columns(gram, count, bases):
     size = min(CHUNK, count)
-    steps = count // size
     tile = gram.shape[1]
-    best = carried(
-        steps,
-        lambda i, best: jnp.maximum(best, jnp.max(gram[at(i, size), :], axis=0, keepdims=True)),
-        jnp.full((1, tile), NEG, jnp.float32),
-    )
+
+    def lines(i):
+        for j in range(0, size, 8):
+            start = i * size + j
+            yield gram[pl.ds(start if isinstance(i, int) else pl.multiple_of(start, 8), 8), :]
+
+    def top(i, best):
+        for line in lines(i):
+            best = jnp.maximum(best, line)
+        return best
+
+    best = carried(count // size, top, jnp.full((8, tile), NEG, jnp.float32))
+    best = jnp.max(best, axis=0, keepdims=True)
 
     def add(i, sums):
-        e = powers(gram[at(i, size), :] - best, *bases)
-        return tuple(s + jnp.sum(v, axis=0, keepdims=True) for s, v in zip(sums, e))
-
-    return best, carried(steps, add, (jnp.zeros((1, tile), jnp.float32),) * CODES)
+        for line in lines(i):
+            sums = tuple(s + v for s, v in zip(sums, powers(line - best, *bases)))
+        return sums
+
+    sums = carried(count // size, add, (jnp.zeros((8, tile), jnp.float32),) * CODES)
+    return best, [jnp.sum(s, axis=0, keepdims=True) for s in sums]
 
 
 def times(a, b):
@@ -173,12 +182,20 @@
     lines, lanes = (lax.broadcasted_iota(jnp.int32, gram.shape, axis) for axis in (0, 1))
     wide[:, last] = jnp.where(lines == lanes, NEG, gram)
     square[...] = jnp.broadcast_to(codes[:, last], (8, tail)).astype(jnp.float32).T
-    bases = bases_of(square[:, 0:1], width)
-    best = jnp.max(wide[...], axis=1, keepdims=True)
-    part = powers(wide[...] - best, *bases)
-    square[:, 0:1] = best
-    for level in range(CODES):
-        square[:, 1 + level : 2 + level] = jnp.sum(part[level], axis=1, keepdims=True)
+    for row in range(0, tail, 32):
+        rows = slice(row, row + 32)
+        bases = bases_of(square[rows, 0:1], width)
+        best = jnp.full((32, 128), NEG, jnp.float32)
+        for col in range(0, head + tail, 128):
+            best = jnp.maximum(best, wide[rows, col : col + 128])
+        best = jnp.max(best, axis=1, keepdims=True)
+        sums = (jnp.zeros((32, 128), jnp.float32),) * CODES
+        for col in range(0, head + tail, 128):
+            part = powers(wide[rows, col : col + 128] - best, *bases)
+            sums = tuple(s + v for s, v in zip(sums, part))
+        square[rows, 0:1] = best
+        for level in range(CODES):
+            square[rows, 1 + level : 2 + level] = jnp.sum(sums[level], axis=1, keepdims=True)
     stats[:, last] = square[...].T
     for start, size in tiles(head):
         cols = pl.ds(start, size)
@@ -294,22 +311,28 @@
 
 def half_kernel(width, codes, keep, level, their_level, by_row, both, lse, turned):
     half = Half(0, width, codes, keep, counted(level, their_level), turned)
-    by_row[...], both[...] = half.part(pl.ds(0, codes.shape[1]))
+    for col in range(0, codes.shape[1], 128):
+        cols = pl.ds(col, 128)
+        by_row[:, cols], both[:, cols] = half.part(cols)
     lse[...] = jnp.broadcast_to(half.lse, lse.shape)
 
 
 def mix_kernel(
     codes, keep, recv, level, their_level, by_row, both, lse, early, middle, late, sooner, later,
-    out, loss, turned
+    out, loss, turned, mix
 ):
     half = Half(0, out.shape[1], codes, recv, counted(level, their_level), turned)
     student = position()[2] == 1
-    their_row, their_both = half.part(pl.ds(0, codes.shape[1]))
     sign = jnp.where(student, 1.0, -1.0)
-    mix = ((WEIGHT * sign) * (both[...] - their_both)).astype(jnp.bfloat16)
     rows = by_row.shape[0]
-    p_row = jnp.where(student, their_row, by_row[...])
-    gap = jnp.sum(p_row * (recv[0:rows, :] - keep[0:rows, :]), axis=1, keepdims=True)
+    gap = jnp.zeros((rows, 128), jnp.float32)
+    for col in range(0, codes.shape[1], 128):
+        cols = pl.ds(col, 128)
+        their_row, their_both = half.part(cols)
+        mix[:, cols] = ((WEIGHT * sign) * (both[:, cols] - their_both)).astype(jnp.bfloat16)
+        p_row = jnp.where(student, their_row, by_row[:, cols])
+        gap = gap + p_row * (recv[0:rows, cols] - keep[0:rows, cols])
+    gap = jnp.sum(gap, axis=1, keepdims=True)
     store_loss(sign * gap, sign * (lse[:, 0:1] - half.lse), loss)
 
     def against(*parts):
@@ -525,7 +548,7 @@
     out, loss = call(
         mix_kernel,
         out_shapes,
-        [pltpu.VMEM((2, block, 8), jnp.float32)],
+        [pltpu.VMEM((2, block, 8), jnp.float32), pltpu.VMEM((half, total), jnp.bfloat16)],
         16,
         codes,
         keep,

time: 38.4 us -> 38.4 us (level)
  no operation moved by 1% of the time
where the time goes in v7:
time: 38.4 us; the launch traced here: 38.2 us
  starting transfers between devices  17.2 us (45%)
  waiting for transfers between devices  9.98 us (26%)
  Pallas kernels  8.35 us (22%)
  between operations  1.49 us (4%)
  local copies, waits for them, and re-layouts  1.18 us (3%)
    ppermute x13, starting transfers between devices, send(): return lax.ppermute(a, ALL, pairs)  17.2 us
    ppermute x13, waiting for transfers between devices, send(): return lax.ppermute(a, ALL, pairs)  9.98 us
    pallas_call x13, Pallas kernels, call(): pl.pallas_call(kernel, out_shape=shapes, in_specs=[SMEM if a.shape == (1,...  8.35 us
    unnamed x4, local copies, waits for them, and re-layouts  1.04 us
  transfers between devices with their start and end apart: 13, of which 6 were waited for; matrix products, arithmetic and copies ran while one was open for 0% of the time, Pallas kernels for 17%

profile of v7, /device:TPU:0, one launch (start us, length us, event | category | flops | bytes accessed | tf_op | source)
XLA Modules:
  0.0 38.2 jit_solution(3631112058917740560)
XLA Ops:
  0.6 0.0 copy-start
  0.7 1.0 %copy-done = bf16[2,128,1152]{2,1,0:T(8,128)(2,1)S(1)} copy-done((bf16[2,128,1152]{2,1,0:T(8,128)(2,1)S(1)}, bf16[2,128,1152]{2,1,0:T(8,128)(2,1)}, u32[]{:S(2)}) %copy-start) | copy-done | bytes 589848
  1.7 4.1 %collective-permute-start.2 = (bf16[64,1152]{1,0:T(8,128)(2,1)S(1)}, bf16[64,1152]{1,0:T(8,128)(2,1)S(1)}, u32[]{:S(2)}, u32[]{:S(2)}) collective-permute-start(bf16[64,1152]{1,0:T(8,128)(2,1)S(1)} %dynamic-slice_bitcast_fusion.1), channel_id=1, source_target_pairs={{0,16},{1,17},{2,18},{3,19},{4,20},{5,21},{6,22},{7,23},{8,24},{9,... | collective-permute-start | bytes 442376 | tf_op jit(solution)/shard_map/ppermute | solution.py:417
  5.9 1.6 %collective-permute-start = (bf16[128,1152]{1,0:T(8,128)(2,1)S(1)}, bf16[128,1152]{1,0:T(8,128)(2,1)S(1)}, u32[]{:S(2)}, u32[]{:S(2)}) collective-permute-start(bf16[128,1152]{1,0:T(8,128)(2,1)S(1)} %dynamic-slice_bitcast_fusion.refs_0_), channel_id=1, source_target_pairs={{0,8},{1,9},{2,10},{3,11},{4,12},{5,13},{6,14},{7,15},{8,0},{9,1},... | collective-permute-start | bytes 884744 | tf_op jit(solution)/shard_map/ppermute | solution.py:417
  7.5 1.5 %collective-permute-start.1 = (bf16[128,1152]{1,0:T(8,128)(2,1)S(1)}, bf16[128,1152]{1,0:T(8,128)(2,1)S(1)}, u32[]{:S(2)}, u32[]{:S(2)}) collective-permute-start(bf16[128,1152]{1,0:T(8,128)(2,1)S(1)} %dynamic-slice_bitcast_fusion.refs_0_), channel_id=1, source_target_pairs={{0,4},{1,5},{2,6},{3,7},{4,0},{5,1},{6,2},{7,3},{8,12},{9,13},{10,... | collective-permute-start | bytes 884744 | tf_op jit(solution)/shard_map/ppermute | solution.py:417
  9.7 3.3 %collective-permute-done.2.refs_3_.refs_0_.refs_2_ = bf16[64,1152]{1,0:T(8,128)(2,1)S(1)} collective-permute-done((bf16[64,1152]{1,0:T(8,128)(2,1)S(1)}, bf16[64,1152]{1,0:T(8,128)(2,1)S(1)}, u32[]{:S(2)}, u32[]{:S(2)}) %collective-permute-start.2) | collective-permute-done | bytes 147488 | tf_op jit(solution)/shard_map/ppermute | solution.py:417
  13.0 1.6 %collective-permute-start.4 = (bf16[80,1152]{1,0:T(8,128)(2,1)S(1)}, bf16[80,1152]{1,0:T(8,128)(2,1)S(1)}, u32[]{:S(2)}, u32[]{:S(2)}) collective-permute-start(bf16[80,1152]{1,0:T(8,128)(2,1)S(1)} %shard_map.51), channel_id=1, source_target_pairs={{0,2},{1,5},{2,0},{3,7},{4,6},{5,1},{6,4},{7,3},{8,10},{9,13},{10,... | collective-permute-start | bytes 552968 | tf_op jit(solution)/shard_map/ppermute | solution.py:417
  14.6 0.6 %collective-permute-start.3 = (bf16[64,1152]{1,0:T(8,128)(2,1)S(1)}, bf16[64,1152]{1,0:T(8,128)(2,1)S(1)}, u32[]{:S(2)}, u32[]{:S(2)}) collective-permute-start(bf16[64,1152]{1,0:T(8,128)(2,1)S(1)} %collective-permute-done.2.refs_3_.refs_0_.refs_2_), channel_id=1, source_target_pairs={{0,8},{1,9},{2,10},{3,11},{4,12},{5,13},{6,14},{7,15},{8,0},{9,1},... | collective-permute-start | bytes 442376 | tf_op jit(solution)/shard_map/ppermute | solution.py:417
  15.2 1.7 %collective-permute-done.refs_1_ = bf16[128,1152]{1,0:T(8,128)(2,1)S(1)} collective-permute-done((bf16[128,1152]{1,0:T(8,128)(2,1)S(1)}, bf16[128,1152]{1,0:T(8,128)(2,1)S(1)}, u32[]{:S(2)}, u32[]{:S(2)}) %collective-permute-start) | collective-permute-done | bytes 294944 | tf_op jit(solution)/shard_map/ppermute | solution.py:417
  17.0 0.0 collective-permute-done.1.refs_2_.refs_0_.refs_1_
  17.0 2.8 %collective-permute-done.3.refs_4_.refs_3_.refs_1_.refs_0_ = bf16[64,1152]{1,0:T(8,128)(2,1)S(1)} collective-permute-done((bf16[64,1152]{1,0:T(8,128)(2,1)S(1)}, bf16[64,1152]{1,0:T(8,128)(2,1)S(1)}, u32[]{:S(2)}, u32[]{:S(2)}) %collective-permute-start.3) | collective-permute-done | bytes 147488 | tf_op jit(solution)/shard_map/ppermute | solution.py:417
  19.7 0.0 collective-permute-done.4.fa.refs_4_
  19.7 0.1 shard_map.57
  19.8 0.0 copy-start.1
  19.8 0.1 collective-permute-start.9
  19.9 1.4 %collective-permute-start.6 = (bf16[64,1152]{1,0:T(8,128)(2,1)S(1)}, bf16[64,1152]{1,0:T(8,128)(2,1)S(1)}, u32[]{:S(2)}, u32[]{:S(2)}) collective-permute-start(bf16[64,1152]{1,0:T(8,128)(2,1)S(1)} %collective-permute-done.3.refs_4_.refs_3_.refs_1_.refs_0_), channel_id=1, source_target_pairs={{0,2},{1,5},{2,0},{3,7},{4,6},{5,1},{6,4},{7,3},{8,10},{9,13},{10,... | collective-permute-start | bytes 442376 | tf_op jit(solution)/shard_map/ppermute | solution.py:417
  21.4 1.6 %collective-permute-start.5 = (bf16[144,1152]{1,0:T(8,128)(2,1)S(1)}, bf16[144,1152]{1,0:T(8,128)(2,1)S(1)}, u32[]{:S(2)}, u32[]{:S(2)}) collective-permute-start(bf16[144,1152]{1,0:T(8,128)(2,1)S(1)} %shard_map.52), channel_id=1, source_target_pairs={{0,4},{1,3},{2,6},{3,1},{4,0},{5,7},{6,2},{7,5},{8,12},{9,11},{10,... | collective-permute-start | bytes 995336 | tf_op jit(solution)/shard_map/ppermute | solution.py:417
  23.0 1.4 %collective-permute-start.7 = (bf16[128,1152]{1,0:T(8,128)(2,1)S(1)}, bf16[128,1152]{1,0:T(8,128)(2,1)S(1)}, u32[]{:S(2)}, u32[]{:S(2)}) collective-permute-start(bf16[128,1152]{1,0:T(8,128)(2,1)S(1)} %shard_map.54), channel_id=1, source_target_pairs={{0,8},{1,9},{2,10},{3,11},{4,12},{5,13},{6,14},{7,15},{8,0},{9,1},... | collective-permute-start | bytes 884744 | tf_op jit(solution)/shard_map/ppermute | solution.py:417
  24.4 0.0 copy-done.1
  24.4 1.5 %shard_map.50 = (s32[1,1024]{1,0:T(1,128)S(1)}, f32[8,512]{1,0:T(8,128)S(1)}, f32[64,512]{1,0:T(8,128)S(1)}, bf16[512,1152]{1,0:T(8,128)(2,1)S(1)}) custom-call(s32[1,1024]{1,0:T(1,128)S(1)} %bitcast.7, bf16[128,1152]{1,0:T(8,128)(2,1)S(1)} %dynamic-slice_bitcast_fusion.refs_0_, bf16[128,1152]{1,0:T(8,128)(2,1)S(1)} %collective-permute-done.refs_1_, ...), custom_call_target="tpu_custom_call" | custom-call | tf_op jit(solution)/shard_map/pallas_call | solution.py:374
  25.9 0.0 collective-permute-done.6.ga.refs_1_.refs_3_
  26.0 0.0 collective-permute-done.9.refs_2_.sooner
  26.0 2.3 %collective-permute-start.10 = (bf16[128,1152]{1,0:T(8,128)(2,1)S(1)}, bf16[128,1152]{1,0:T(8,128)(2,1)S(1)}, u32[]{:S(2)}, u32[]{:S(2)}) collective-permute-start(bf16[128,1152]{1,0:T(8,128)(2,1)S(1)} %shard_map.58), channel_id=1, source_target_pairs={{0,4},{1,3},{2,6},{3,1},{4,0},{5,7},{6,2},{7,5},{8,12},{9,11},{10,... | collective-permute-start | bytes 884744 | tf_op jit(solution)/shard_map/ppermute | solution.py:417
  28.3 0.3 collective-permute-done.5.fb
  28.6 1.6 %shard_map.53 = (f32[8,768]{1,0:T(8,128)S(1)}, f32[64,768]{1,0:T(8,128)S(1)}, bf16[768,1152]{1,0:T(8,128)(2,1)S(1)}, f32[8,128]{1,0:T(8,128)S(1)}) custom-call(s32[1,1024]{1,0:T(1,128)S(1)} %get-tuple-element.19.codes, bf16[512,1152]{1,0:T(8,128)(2,1)S(1)} %get-tuple-element.20.early, f32[8,512]{1,0:T(8,128)S(1)} %get-tuple-element.21.before.refs_3_, ...), custom_call_target="tpu_custom_call" | custom-call | tf_op jit(solution)/shard_map/pallas_call | solution.py:374
  30.2 0.3 collective-permute-start.8
  30.5 1.3 %collective-permute-done.7.late.middle.refs_2_ = bf16[128,1152]{1,0:T(8,128)(2,1)S(1)} collective-permute-done((bf16[128,1152]{1,0:T(8,128)(2,1)S(1)}, bf16[128,1152]{1,0:T(8,128)(2,1)S(1)}, u32[]{:S(2)}, u32[]{:S(2)}) %collective-permute-start.7) | collective-permute-done | bytes 294944 | tf_op jit(solution)/shard_map/ppermute | solution.py:417
  31.9 0.0 collective-permute-done.8._.their_level
  31.9 1.2 %shard_map.55 = (f32[8,896]{1,0:T(8,128)S(1)}, f32[64,896]{1,0:T(8,128)S(1)}) custom-call(s32[1,1024]{1,0:T(1,128)S(1)} %get-tuple-element.19.codes, bf16[768,1152]{1,0:T(8,128)(2,1)S(1)} %get-tuple-element.23.early, f32[8,768]{1,0:T(8,128)S(1)} %get-tuple-element.24.before, f32[64,768]{1,0:T(8,128)S(1)} %get-tuple-element.25.part_strip, ...), custom_call_target="tpu_custom_call" | custom-call | tf_op jit(solution)/shard_map/pallas_call | solution.py:374
  33.1 0.0 collective-permute-done.10.late
  33.1 0.1 shard_map.61
  33.2 0.1 collective-permute-start.12
  33.3 1.5 %shard_map.59 = (f32[40,1024]{1,0:T(8,128)S(1)}, f32[40,1024]{1,0:T(8,128)S(1)}) custom-call(s32[1,1024]{1,0:T(1,128)S(1)} %get-tuple-element.19.codes, bf16[768,1152]{1,0:T(8,128)(2,1)S(1)} %get-tuple-element.23.early, bf16[128,1152]{1,0:T(8,128)(2,1)S(1)} %collective-permute-done.7.late.middle.refs_2_, f32[8,896]{1,0:T(8,128)S(1)} %get-tuple-element.27.before.refs_5_, ...), custom_call_target="tpu_custom_call" | custom-call | tf_op jit(solution)/shard_map/pallas_call | solution.py:374
  34.8 0.6 %collective-permute-start.11 = (f32[40,1024]{1,0:T(8,128)S(1)}, f32[40,1024]{1,0:T(8,128)S(1)}, u32[]{:S(2)}, u32[]{:S(2)}) collective-permute-start(f32[40,1024]{1,0:T(8,128)S(1)} %get-tuple-element.30), channel_id=1, source_target_pairs={{0,1},{1,0},{2,3},{3,2},{4,5},{5,4},{6,7},{7,6},{8,9},{9,8},{10,11... | collective-permute-start | bytes 491528 | tf_op jit(solution)/shard_map/ppermute | solution.py:417
  35.3 0.4 %shard_map.60 = (f32[32,1024]{1,0:T(8,128)S(1)}, f32[32,1024]{1,0:T(8,128)S(1)}, f32[32,8]{1,0:T(8,128)S(1)}) custom-call(s32[1,1024]{1,0:T(1,128)S(1)} %get-tuple-element.19.codes, f32[40,1024]{1,0:T(8,128)S(1)} %get-tuple-element.29.keep, f32[8,128]{1,0:T(8,128)S(1)} %get-tuple-element.26.level, f32[8,128]{1,0:T(8,128)S(1)} %collective-permute-done.8._.their_level), custom_call_target="tpu_custom_call" | custom-call | tf_op jit(solution)/shard_map/pallas_call | solution.py:374
  35.8 0.6 %collective-permute-done.11.recv = f32[40,1024]{1,0:T(8,128)S(1)} collective-permute-done((f32[40,1024]{1,0:T(8,128)S(1)}, f32[40,1024]{1,0:T(8,128)S(1)}, u32[]{:S(2)}, u32[]{:S(2)}) %collective-permute-start.11) | collective-permute-done | bytes 163872 | tf_op jit(solution)/shard_map/ppermute | solution.py:417
  36.4 0.0 collective-permute-done.12.later
  36.4 1.8 %shard_map.62 = (f32[32,1152]{1,0:T(8,128)}, f32[1,32]{1,0:T(1,128)}) custom-call(s32[1,1024]{1,0:T(1,128)S(1)} %get-tuple-element.19.codes, f32[40,1024]{1,0:T(8,128)S(1)} %get-tuple-element.29.keep, f32[40,1024]{1,0:T(8,128)S(1)} %collective-permute-done.11.recv, f32[8,128]{1,0:T(8,128)S(1)} %get-tuple-element.26.level, ...), custom_call_target="tpu_custom_call" | custom-call | tf_op jit(solution)/shard_map/pallas_call | solution.py:374
  (11 shorter events, 0.3 us)
Async XLA Ops:
  0.6 1.1 %copy-start = (bf16[2,128,1152]{2,1,0:T(8,128)(2,1)S(1)}, bf16[2,128,1152]{2,1,0:T(8,128)(2,1)}, u32[]{:S(2)}) copy-start(bf16[2,128,1152]{2,1,0:T(8,128)(2,1)} %param.3) | copy-start | bytes 1769476
  1.7 11.2 %collective-permute-start.2 = (bf16[64,1152]{1,0:T(8,128)(2,1)S(1)}, bf16[64,1152]{1,0:T(8,128)(2,1)S(1)}, u32[]{:S(2)}, u32[]{:S(2)}) collective-permute-start(bf16[64,1152]{1,0:T(8,128)(2,1)S(1)} %dynamic-slice_bitcast_fusion.1), channel_id=1, source_target_pairs={{0,16},{1,17},{2,18},{3,19},{4,20},{5,21},{6,22},{7,23},{8,24},{9,... | collective-permute-start | bytes 442376 | tf_op jit(solution)/shard_map/ppermute | solution.py:417
  5.9 11.0 %collective-permute-start = (bf16[128,1152]{1,0:T(8,128)(2,1)S(1)}, bf16[128,1152]{1,0:T(8,128)(2,1)S(1)}, u32[]{:S(2)}, u32[]{:S(2)}) collective-permute-start(bf16[128,1152]{1,0:T(8,128)(2,1)S(1)} %dynamic-slice_bitcast_fusion.refs_0_), channel_id=1, source_target_pairs={{0,8},{1,9},{2,10},{3,11},{4,12},{5,13},{6,14},{7,15},{8,0},{9,1},... | collective-permute-start | bytes 884744 | tf_op jit(solution)/shard_map/ppermute | solution.py:417
  7.5 9.5 %collective-permute-start.1 = (bf16[128,1152]{1,0:T(8,128)(2,1)S(1)}, bf16[128,1152]{1,0:T(8,128)(2,1)S(1)}, u32[]{:S(2)}, u32[]{:S(2)}) collective-permute-start(bf16[128,1152]{1,0:T(8,128)(2,1)S(1)} %dynamic-slice_bitcast_fusion.refs_0_), channel_id=1, source_target_pairs={{0,4},{1,5},{2,6},{3,7},{4,0},{5,1},{6,2},{7,3},{8,12},{9,13},{10,... | collective-permute-start | bytes 884744 | tf_op jit(solution)/shard_map/ppermute | solution.py:417
  13.0 6.8 %collective-permute-start.4 = (bf16[80,1152]{1,0:T(8,128)(2,1)S(1)}, bf16[80,1152]{1,0:T(8,128)(2,1)S(1)}, u32[]{:S(2)}, u32[]{:S(2)}) collective-permute-start(bf16[80,1152]{1,0:T(8,128)(2,1)S(1)} %shard_map.51), channel_id=1, source_target_pairs={{0,2},{1,5},{2,0},{3,7},{4,6},{5,1},{6,4},{7,3},{8,10},{9,13},{10,... | collective-permute-start | bytes 552968 | tf_op jit(solution)/shard_map/ppermute | solution.py:417
  14.6 5.1 %collective-permute-start.3 = (bf16[64,1152]{1,0:T(8,128)(2,1)S(1)}, bf16[64,1152]{1,0:T(8,128)(2,1)S(1)}, u32[]{:S(2)}, u32[]{:S(2)}) collective-permute-start(bf16[64,1152]{1,0:T(8,128)(2,1)S(1)} %collective-permute-done.2.refs_3_.refs_0_.refs_2_), channel_id=1, source_target_pairs={{0,8},{1,9},{2,10},{3,11},{4,12},{5,13},{6,14},{7,15},{8,0},{9,1},... | collective-permute-start | bytes 442376 | tf_op jit(solution)/shard_map/ppermute | solution.py:417
  19.8 4.6 %copy-start.1 = (s32[1024]{0:T(1024)S(1)}, s32[1024]{0:T(1024)}, u32[]{:S(2)}) copy-start(s32[1024]{0:T(1024)} %param.4) | copy-start | bytes 12292
  19.8 6.1 %collective-permute-start.9 = (bf16[512,1152]{1,0:T(8,128)(2,1)S(1)}, bf16[512,1152]{1,0:T(8,128)(2,1)S(1)}, u32[]{:S(2)}, u32[]{:S(2)}) collective-permute-start(bf16[512,1152]{1,0:T(8,128)(2,1)S(1)} %shard_map.57), channel_id=1, source_target_pairs={{0,1},{1,0},{2,3},{3,2},{4,5},{5,4},{6,7},{7,6},{8,9},{9,8},{10,11... | collective-permute-start | bytes 3538952 | tf_op jit(solution)/shard_map/ppermute | solution.py:417
  19.9 6.0 %collective-permute-start.6 = (bf16[64,1152]{1,0:T(8,128)(2,1)S(1)}, bf16[64,1152]{1,0:T(8,128)(2,1)S(1)}, u32[]{:S(2)}, u32[]{:S(2)}) collective-permute-start(bf16[64,1152]{1,0:T(8,128)(2,1)S(1)} %collective-permute-done.3.refs_4_.refs_3_.refs_1_.refs_0_), channel_id=1, source_target_pairs={{0,2},{1,5},{2,0},{3,7},{4,6},{5,1},{6,4},{7,3},{8,10},{9,13},{10,... | collective-permute-start | bytes 442376 | tf_op jit(solution)/shard_map/ppermute | solution.py:417
  21.4 7.2 %collective-permute-start.5 = (bf16[144,1152]{1,0:T(8,128)(2,1)S(1)}, bf16[144,1152]{1,0:T(8,128)(2,1)S(1)}, u32[]{:S(2)}, u32[]{:S(2)}) collective-permute-start(bf16[144,1152]{1,0:T(8,128)(2,1)S(1)} %shard_map.52), channel_id=1, source_target_pairs={{0,4},{1,3},{2,6},{3,1},{4,0},{5,7},{6,2},{7,5},{8,12},{9,11},{10,... | collective-permute-start | bytes 995336 | tf_op jit(solution)/shard_map/ppermute | solution.py:417
  23.0 8.8 %collective-permute-start.7 = (bf16[128,1152]{1,0:T(8,128)(2,1)S(1)}, bf16[128,1152]{1,0:T(8,128)(2,1)S(1)}, u32[]{:S(2)}, u32[]{:S(2)}) collective-permute-start(bf16[128,1152]{1,0:T(8,128)(2,1)S(1)} %shard_map.54), channel_id=1, source_target_pairs={{0,8},{1,9},{2,10},{3,11},{4,12},{5,13},{6,14},{7,15},{8,0},{9,1},... | collective-permute-start | bytes 884744 | tf_op jit(solution)/shard_map/ppermute | solution.py:417
  26.0 7.1 %collective-permute-start.10 = (bf16[128,1152]{1,0:T(8,128)(2,1)S(1)}, bf16[128,1152]{1,0:T(8,128)(2,1)S(1)}, u32[]{:S(2)}, u32[]{:S(2)}) collective-permute-start(bf16[128,1152]{1,0:T(8,128)(2,1)S(1)} %shard_map.58), channel_id=1, source_target_pairs={{0,4},{1,3},{2,6},{3,1},{4,0},{5,7},{6,2},{7,5},{8,12},{9,11},{10,... | collective-permute-start | bytes 884744 | tf_op jit(solution)/shard_map/ppermute | solution.py:417
  30.2 1.6 %collective-permute-start.8 = (f32[8,128]{1,0:T(8,128)S(1)}, f32[8,128]{1,0:T(8,128)S(1)}, u32[]{:S(2)}, u32[]{:S(2)}) collective-permute-start(f32[8,128]{1,0:T(8,128)S(1)} %get-tuple-element.26.level), channel_id=1, source_target_pairs={{0,1},{1,0},{2,3},{3,2},{4,5},{5,4},{6,7},{7,6},{8,9},{9,8},{10,11... | collective-permute-start | bytes 12296 | tf_op jit(solution)/shard_map/ppermute | solution.py:417
  33.2 3.2 %collective-permute-start.12 = (bf16[512,1152]{1,0:T(8,128)(2,1)S(1)}, bf16[512,1152]{1,0:T(8,128)(2,1)S(1)}, u32[]{:S(2)}, u32[]{:S(2)}) collective-permute-start(bf16[512,1152]{1,0:T(8,128)(2,1)S(1)} %shard_map.61), channel_id=1, source_target_pairs={{0,1},{1,0},{2,3},{3,2},{4,5},{5,4},{6,7},{7,6},{8,9},{9,8},{10,11... | collective-permute-start | bytes 3538952 | tf_op jit(solution)/shard_map/ppermute | solution.py:417
  34.8 1.6 %collective-permute-start.11 = (f32[40,1024]{1,0:T(8,128)S(1)}, f32[40,1024]{1,0:T(8,128)S(1)}, u32[]{:S(2)}, u32[]{:S(2)}) collective-permute-start(f32[40,1024]{1,0:T(8,128)S(1)} %get-tuple-element.30), channel_id=1, source_target_pairs={{0,1},{1,0},{2,3},{3,2},{4,5},{5,4},{6,7},{7,6},{8,9},{9,8},{10,11... | collective-permute-start | bytes 491528 | tf_op jit(solution)/shard_map/ppermute | solution.py:417

commit v8 on v7

--- a/solution.py
+++ b/solution.py
@@ -228,8 +228,8 @@
     add_rows(codes, [early], late, before, stats, strip, wide, square)
     stats[1 + CODES :, :] = jnp.zeros((stats.shape[0] - 1 - CODES, stats.shape[1]), jnp.float32)
     theirs = jnp.where(
-        core == 0, fa[half : half + 1, 0:1], fb[2 * half : 2 * half + 1, 0:1]
-    ).astype(jnp.float32)
+        core == 0, fa[half : half + 16, 0:128], fb[2 * half : 2 * half + 16, 0:128]
+    ).astype(jnp.float32)[0:1, 0:1]
     row = lax.broadcasted_iota(jnp.int32, level.shape, 0)
     level[...] = jnp.where(row == 0, level_index[0].astype(jnp.float32), theirs)
 

time: 38.4 us -> 38.4 us (level)
  no operation moved by 1% of the time
where the time goes in v8:
time: 38.4 us; the launch traced here: 38.2 us
  starting transfers between devices  17.2 us (45%)
  waiting for transfers between devices  9.98 us (26%)
  Pallas kernels  8.35 us (22%)
  between operations  1.49 us (4%)
  local copies, waits for them, and re-layouts  1.18 us (3%)
    ppermute x13, starting transfers between devices, send(): return lax.ppermute(a, ALL, pairs)  17.2 us
    ppermute x13, waiting for transfers between devices, send(): return lax.ppermute(a, ALL, pairs)  9.98 us
    pallas_call x13, Pallas kernels, call(): pl.pallas_call(kernel, out_shape=shapes, in_specs=[SMEM if a.shape == (1,...  8.35 us
    unnamed x4, local copies, waits for them, and re-layouts  1.04 us
  transfers between devices with their start and end apart: 13, of which 6 were waited for; matrix products, arithmetic and copies ran while one was open for 0% of the time, Pallas kernels for 17%

profile of v8, /device:TPU:0, one launch (start us, length us, event | category | flops | bytes accessed | tf_op | source)
XLA Modules:
  0.0 38.2 jit_solution(5413667633117340243)
XLA Ops:
  0.6 0.0 copy-start
  0.7 1.0 %copy-done = bf16[2,128,1152]{2,1,0:T(8,128)(2,1)S(1)} copy-done((bf16[2,128,1152]{2,1,0:T(8,128)(2,1)S(1)}, bf16[2,128,1152]{2,1,0:T(8,128)(2,1)}, u32[]{:S(2)}) %copy-start) | copy-done | bytes 589848
  1.7 4.1 %collective-permute-start.2 = (bf16[64,1152]{1,0:T(8,128)(2,1)S(1)}, bf16[64,1152]{1,0:T(8,128)(2,1)S(1)}, u32[]{:S(2)}, u32[]{:S(2)}) collective-permute-start(bf16[64,1152]{1,0:T(8,128)(2,1)S(1)} %dynamic-slice_bitcast_fusion.1), channel_id=1, source_target_pairs={{0,16},{1,17},{2,18},{3,19},{4,20},{5,21},{6,22},{7,23},{8,24},{9,... | collective-permute-start | bytes 442376 | tf_op jit(solution)/shard_map/ppermute | solution.py:417
  5.9 1.6 %collective-permute-start = (bf16[128,1152]{1,0:T(8,128)(2,1)S(1)}, bf16[128,1152]{1,0:T(8,128)(2,1)S(1)}, u32[]{:S(2)}, u32[]{:S(2)}) collective-permute-start(bf16[128,1152]{1,0:T(8,128)(2,1)S(1)} %dynamic-slice_bitcast_fusion.refs_0_), channel_id=1, source_target_pairs={{0,8},{1,9},{2,10},{3,11},{4,12},{5,13},{6,14},{7,15},{8,0},{9,1},... | collective-permute-start | bytes 884744 | tf_op jit(solution)/shard_map/ppermute | solution.py:417
  7.5 1.5 %collective-permute-start.1 = (bf16[128,1152]{1,0:T(8,128)(2,1)S(1)}, bf16[128,1152]{1,0:T(8,128)(2,1)S(1)}, u32[]{:S(2)}, u32[]{:S(2)}) collective-permute-start(bf16[128,1152]{1,0:T(8,128)(2,1)S(1)} %dynamic-slice_bitcast_fusion.refs_0_), channel_id=1, source_target_pairs={{0,4},{1,5},{2,6},{3,7},{4,0},{5,1},{6,2},{7,3},{8,12},{9,13},{10,... | collective-permute-start | bytes 884744 | tf_op jit(solution)/shard_map/ppermute | solution.py:417
  9.7 3.3 %collective-permute-done.2.refs_3_.refs_0_.refs_2_ = bf16[64,1152]{1,0:T(8,128)(2,1)S(1)} collective-permute-done((bf16[64,1152]{1,0:T(8,128)(2,1)S(1)}, bf16[64,1152]{1,0:T(8,128)(2,1)S(1)}, u32[]{:S(2)}, u32[]{:S(2)}) %collective-permute-start.2) | collective-permute-done | bytes 147488 | tf_op jit(solution)/shard_map/ppermute | solution.py:417
  13.0 1.6 %collective-permute-start.4 = (bf16[80,1152]{1,0:T(8,128)(2,1)S(1)}, bf16[80,1152]{1,0:T(8,128)(2,1)S(1)}, u32[]{:S(2)}, u32[]{:S(2)}) collective-permute-start(bf16[80,1152]{1,0:T(8,128)(2,1)S(1)} %shard_map.51), channel_id=1, source_target_pairs={{0,2},{1,5},{2,0},{3,7},{4,6},{5,1},{6,4},{7,3},{8,10},{9,13},{10,... | collective-permute-start | bytes 552968 | tf_op jit(solution)/shard_map/ppermute | solution.py:417
  14.6 0.6 %collective-permute-start.3 = (bf16[64,1152]{1,0:T(8,128)(2,1)S(1)}, bf16[64,1152]{1,0:T(8,128)(2,1)S(1)}, u32[]{:S(2)}, u32[]{:S(2)}) collective-permute-start(bf16[64,1152]{1,0:T(8,128)(2,1)S(1)} %collective-permute-done.2.refs_3_.refs_0_.refs_2_), channel_id=1, source_target_pairs={{0,8},{1,9},{2,10},{3,11},{4,12},{5,13},{6,14},{7,15},{8,0},{9,1},... | collective-permute-start | bytes 442376 | tf_op jit(solution)/shard_map/ppermute | solution.py:417
  15.2 1.7 %collective-permute-done.refs_1_ = bf16[128,1152]{1,0:T(8,128)(2,1)S(1)} collective-permute-done((bf16[128,1152]{1,0:T(8,128)(2,1)S(1)}, bf16[128,1152]{1,0:T(8,128)(2,1)S(1)}, u32[]{:S(2)}, u32[]{:S(2)}) %collective-permute-start) | collective-permute-done | bytes 294944 | tf_op jit(solution)/shard_map/ppermute | solution.py:417
  17.0 0.0 collective-permute-done.1.refs_2_.refs_0_.refs_1_
  17.0 2.8 %collective-permute-done.3.refs_4_.refs_3_.refs_1_.refs_0_ = bf16[64,1152]{1,0:T(8,128)(2,1)S(1)} collective-permute-done((bf16[64,1152]{1,0:T(8,128)(2,1)S(1)}, bf16[64,1152]{1,0:T(8,128)(2,1)S(1)}, u32[]{:S(2)}, u32[]{:S(2)}) %collective-permute-start.3) | collective-permute-done | bytes 147488 | tf_op jit(solution)/shard_map/ppermute | solution.py:417
  19.7 0.0 collective-permute-done.4.fa.refs_4_
  19.7 0.1 shard_map.57
  19.8 0.0 copy-start.1
  19.8 0.1 collective-permute-start.9
  19.9 1.4 %collective-permute-start.6 = (bf16[64,1152]{1,0:T(8,128)(2,1)S(1)}, bf16[64,1152]{1,0:T(8,128)(2,1)S(1)}, u32[]{:S(2)}, u32[]{:S(2)}) collective-permute-start(bf16[64,1152]{1,0:T(8,128)(2,1)S(1)} %collective-permute-done.3.refs_4_.refs_3_.refs_1_.refs_0_), channel_id=1, source_target_pairs={{0,2},{1,5},{2,0},{3,7},{4,6},{5,1},{6,4},{7,3},{8,10},{9,13},{10,... | collective-permute-start | bytes 442376 | tf_op jit(solution)/shard_map/ppermute | solution.py:417
  21.4 1.6 %collective-permute-start.5 = (bf16[144,1152]{1,0:T(8,128)(2,1)S(1)}, bf16[144,1152]{1,0:T(8,128)(2,1)S(1)}, u32[]{:S(2)}, u32[]{:S(2)}) collective-permute-start(bf16[144,1152]{1,0:T(8,128)(2,1)S(1)} %shard_map.52), channel_id=1, source_target_pairs={{0,4},{1,3},{2,6},{3,1},{4,0},{5,7},{6,2},{7,5},{8,12},{9,11},{10,... | collective-permute-start | bytes 995336 | tf_op jit(solution)/shard_map/ppermute | solution.py:417
  23.0 1.4 %collective-permute-start.7 = (bf16[128,1152]{1,0:T(8,128)(2,1)S(1)}, bf16[128,1152]{1,0:T(8,128)(2,1)S(1)}, u32[]{:S(2)}, u32[]{:S(2)}) collective-permute-start(bf16[128,1152]{1,0:T(8,128)(2,1)S(1)} %shard_map.54), channel_id=1, source_target_pairs={{0,8},{1,9},{2,10},{3,11},{4,12},{5,13},{6,14},{7,15},{8,0},{9,1},... | collective-permute-start | bytes 884744 | tf_op jit(solution)/shard_map/ppermute | solution.py:417
  24.4 0.0 copy-done.1
  24.4 1.5 %shard_map.50 = (s32[1,1024]{1,0:T(1,128)S(1)}, f32[8,512]{1,0:T(8,128)S(1)}, f32[64,512]{1,0:T(8,128)S(1)}, bf16[512,1152]{1,0:T(8,128)(2,1)S(1)}) custom-call(s32[1,1024]{1,0:T(1,128)S(1)} %bitcast.7, bf16[128,1152]{1,0:T(8,128)(2,1)S(1)} %dynamic-slice_bitcast_fusion.refs_0_, bf16[128,1152]{1,0:T(8,128)(2,1)S(1)} %collective-permute-done.refs_1_, ...), custom_call_target="tpu_custom_call" | custom-call | tf_op jit(solution)/shard_map/pallas_call | solution.py:374
  25.9 0.0 collective-permute-done.6.ga.refs_1_.refs_3_
  26.0 0.0 collective-permute-done.9.refs_2_.sooner
  26.0 2.3 %collective-permute-start.10 = (bf16[128,1152]{1,0:T(8,128)(2,1)S(1)}, bf16[128,1152]{1,0:T(8,128)(2,1)S(1)}, u32[]{:S(2)}, u32[]{:S(2)}) collective-permute-start(bf16[128,1152]{1,0:T(8,128)(2,1)S(1)} %shard_map.58), channel_id=1, source_target_pairs={{0,4},{1,3},{2,6},{3,1},{4,0},{5,7},{6,2},{7,5},{8,12},{9,11},{10,... | collective-permute-start | bytes 884744 | tf_op jit(solution)/shard_map/ppermute | solution.py:417
  28.3 0.3 collective-permute-done.5.fb
  28.6 1.6 %shard_map.53 = (f32[8,768]{1,0:T(8,128)S(1)}, f32[64,768]{1,0:T(8,128)S(1)}, bf16[768,1152]{1,0:T(8,128)(2,1)S(1)}, f32[8,128]{1,0:T(8,128)S(1)}) custom-call(s32[1,1024]{1,0:T(1,128)S(1)} %get-tuple-element.19.codes, bf16[512,1152]{1,0:T(8,128)(2,1)S(1)} %get-tuple-element.20.early, f32[8,512]{1,0:T(8,128)S(1)} %get-tuple-element.21.before.refs_3_, ...), custom_call_target="tpu_custom_call" | custom-call | tf_op jit(solution)/shard_map/pallas_call | solution.py:374
  30.2 0.3 collective-permute-start.8
  30.5 1.3 %collective-permute-done.7.late.middle.refs_2_ = bf16[128,1152]{1,0:T(8,128)(2,1)S(1)} collective-permute-done((bf16[128,1152]{1,0:T(8,128)(2,1)S(1)}, bf16[128,1152]{1,0:T(8,128)(2,1)S(1)}, u32[]{:S(2)}, u32[]{:S(2)}) %collective-permute-start.7) | collective-permute-done | bytes 294944 | tf_op jit(solution)/shard_map/ppermute | solution.py:417
  31.9 0.0 collective-permute-done.8._.their_level
  31.9 1.2 %shard_map.55 = (f32[8,896]{1,0:T(8,128)S(1)}, f32[64,896]{1,0:T(8,128)S(1)}) custom-call(s32[1,1024]{1,0:T(1,128)S(1)} %get-tuple-element.19.codes, bf16[768,1152]{1,0:T(8,128)(2,1)S(1)} %get-tuple-element.23.early, f32[8,768]{1,0:T(8,128)S(1)} %get-tuple-element.24.before, f32[64,768]{1,0:T(8,128)S(1)} %get-tuple-element.25.part_strip, ...), custom_call_target="tpu_custom_call" | custom-call | tf_op jit(solution)/shard_map/pallas_call | solution.py:374
  33.1 0.0 collective-permute-done.10.late
  33.1 0.1 shard_map.61
  33.2 0.1 collective-permute-start.12
  33.3 1.5 %shard_map.59 = (f32[40,1024]{1,0:T(8,128)S(1)}, f32[40,1024]{1,0:T(8,128)S(1)}) custom-call(s32[1,1024]{1,0:T(1,128)S(1)} %get-tuple-element.19.codes, bf16[768,1152]{1,0:T(8,128)(2,1)S(1)} %get-tuple-element.23.early, bf16[128,1152]{1,0:T(8,128)(2,1)S(1)} %collective-permute-done.7.late.middle.refs_2_, f32[8,896]{1,0:T(8,128)S(1)} %get-tuple-element.27.before.refs_5_, ...), custom_call_target="tpu_custom_call" | custom-call | tf_op jit(solution)/shard_map/pallas_call | solution.py:374
  34.8 0.6 %collective-permute-start.11 = (f32[40,1024]{1,0:T(8,128)S(1)}, f32[40,1024]{1,0:T(8,128)S(1)}, u32[]{:S(2)}, u32[]{:S(2)}) collective-permute-start(f32[40,1024]{1,0:T(8,128)S(1)} %get-tuple-element.30), channel_id=1, source_target_pairs={{0,1},{1,0},{2,3},{3,2},{4,5},{5,4},{6,7},{7,6},{8,9},{9,8},{10,11... | collective-permute-start | bytes 491528 | tf_op jit(solution)/shard_map/ppermute | solution.py:417
  35.3 0.4 %shard_map.60 = (f32[32,1024]{1,0:T(8,128)S(1)}, f32[32,1024]{1,0:T(8,128)S(1)}, f32[32,8]{1,0:T(8,128)S(1)}) custom-call(s32[1,1024]{1,0:T(1,128)S(1)} %get-tuple-element.19.codes, f32[40,1024]{1,0:T(8,128)S(1)} %get-tuple-element.29.keep, f32[8,128]{1,0:T(8,128)S(1)} %get-tuple-element.26.level, f32[8,128]{1,0:T(8,128)S(1)} %collective-permute-done.8._.their_level), custom_call_target="tpu_custom_call" | custom-call | tf_op jit(solution)/shard_map/pallas_call | solution.py:374
  35.8 0.6 %collective-permute-done.11.recv = f32[40,1024]{1,0:T(8,128)S(1)} collective-permute-done((f32[40,1024]{1,0:T(8,128)S(1)}, f32[40,1024]{1,0:T(8,128)S(1)}, u32[]{:S(2)}, u32[]{:S(2)}) %collective-permute-start.11) | collective-permute-done | bytes 163872 | tf_op jit(solution)/shard_map/ppermute | solution.py:417
  36.4 0.0 collective-permute-done.12.later
  36.4 1.8 %shard_map.62 = (f32[32,1152]{1,0:T(8,128)}, f32[1,32]{1,0:T(1,128)}) custom-call(s32[1,1024]{1,0:T(1,128)S(1)} %get-tuple-element.19.codes, f32[40,1024]{1,0:T(8,128)S(1)} %get-tuple-element.29.keep, f32[40,1024]{1,0:T(8,128)S(1)} %collective-permute-done.11.recv, f32[8,128]{1,0:T(8,128)S(1)} %get-tuple-element.26.level, ...), custom_call_target="tpu_custom_call" | custom-call | tf_op jit(solution)/shard_map/pallas_call | solution.py:374
  (11 shorter events, 0.3 us)
Async XLA Ops:
  0.6 1.1 %copy-start = (bf16[2,128,1152]{2,1,0:T(8,128)(2,1)S(1)}, bf16[2,128,1152]{2,1,0:T(8,128)(2,1)}, u32[]{:S(2)}) copy-start(bf16[2,128,1152]{2,1,0:T(8,128)(2,1)} %param.3) | copy-start | bytes 1769476
  1.7 11.2 %collective-permute-start.2 = (bf16[64,1152]{1,0:T(8,128)(2,1)S(1)}, bf16[64,1152]{1,0:T(8,128)(2,1)S(1)}, u32[]{:S(2)}, u32[]{:S(2)}) collective-permute-start(bf16[64,1152]{1,0:T(8,128)(2,1)S(1)} %dynamic-slice_bitcast_fusion.1), channel_id=1, source_target_pairs={{0,16},{1,17},{2,18},{3,19},{4,20},{5,21},{6,22},{7,23},{8,24},{9,... | collective-permute-start | bytes 442376 | tf_op jit(solution)/shard_map/ppermute | solution.py:417
  5.9 11.0 %collective-permute-start = (bf16[128,1152]{1,0:T(8,128)(2,1)S(1)}, bf16[128,1152]{1,0:T(8,128)(2,1)S(1)}, u32[]{:S(2)}, u32[]{:S(2)}) collective-permute-start(bf16[128,1152]{1,0:T(8,128)(2,1)S(1)} %dynamic-slice_bitcast_fusion.refs_0_), channel_id=1, source_target_pairs={{0,8},{1,9},{2,10},{3,11},{4,12},{5,13},{6,14},{7,15},{8,0},{9,1},... | collective-permute-start | bytes 884744 | tf_op jit(solution)/shard_map/ppermute | solution.py:417
  7.5 9.5 %collective-permute-start.1 = (bf16[128,1152]{1,0:T(8,128)(2,1)S(1)}, bf16[128,1152]{1,0:T(8,128)(2,1)S(1)}, u32[]{:S(2)}, u32[]{:S(2)}) collective-permute-start(bf16[128,1152]{1,0:T(8,128)(2,1)S(1)} %dynamic-slice_bitcast_fusion.refs_0_), channel_id=1, source_target_pairs={{0,4},{1,5},{2,6},{3,7},{4,0},{5,1},{6,2},{7,3},{8,12},{9,13},{10,... | collective-permute-start | bytes 884744 | tf_op jit(solution)/shard_map/ppermute | solution.py:417
  13.0 6.8 %collective-permute-start.4 = (bf16[80,1152]{1,0:T(8,128)(2,1)S(1)}, bf16[80,1152]{1,0:T(8,128)(2,1)S(1)}, u32[]{:S(2)}, u32[]{:S(2)}) collective-permute-start(bf16[80,1152]{1,0:T(8,128)(2,1)S(1)} %shard_map.51), channel_id=1, source_target_pairs={{0,2},{1,5},{2,0},{3,7},{4,6},{5,1},{6,4},{7,3},{8,10},{9,13},{10,... | collective-permute-start | bytes 552968 | tf_op jit(solution)/shard_map/ppermute | solution.py:417
  14.6 5.1 %collective-permute-start.3 = (bf16[64,1152]{1,0:T(8,128)(2,1)S(1)}, bf16[64,1152]{1,0:T(8,128)(2,1)S(1)}, u32[]{:S(2)}, u32[]{:S(2)}) collective-permute-start(bf16[64,1152]{1,0:T(8,128)(2,1)S(1)} %collective-permute-done.2.refs_3_.refs_0_.refs_2_), channel_id=1, source_target_pairs={{0,8},{1,9},{2,10},{3,11},{4,12},{5,13},{6,14},{7,15},{8,0},{9,1},... | collective-permute-start | bytes 442376 | tf_op jit(solution)/shard_map/ppermute | solution.py:417
  19.8 4.6 %copy-start.1 = (s32[1024]{0:T(1024)S(1)}, s32[1024]{0:T(1024)}, u32[]{:S(2)}) copy-start(s32[1024]{0:T(1024)} %param.4) | copy-start | bytes 12292
  19.8 6.1 %collective-permute-start.9 = (bf16[512,1152]{1,0:T(8,128)(2,1)S(1)}, bf16[512,1152]{1,0:T(8,128)(2,1)S(1)}, u32[]{:S(2)}, u32[]{:S(2)}) collective-permute-start(bf16[512,1152]{1,0:T(8,128)(2,1)S(1)} %shard_map.57), channel_id=1, source_target_pairs={{0,1},{1,0},{2,3},{3,2},{4,5},{5,4},{6,7},{7,6},{8,9},{9,8},{10,11... | collective-permute-start | bytes 3538952 | tf_op jit(solution)/shard_map/ppermute | solution.py:417
  19.9 6.0 %collective-permute-start.6 = (bf16[64,1152]{1,0:T(8,128)(2,1)S(1)}, bf16[64,1152]{1,0:T(8,128)(2,1)S(1)}, u32[]{:S(2)}, u32[]{:S(2)}) collective-permute-start(bf16[64,1152]{1,0:T(8,128)(2,1)S(1)} %collective-permute-done.3.refs_4_.refs_3_.refs_1_.refs_0_), channel_id=1, source_target_pairs={{0,2},{1,5},{2,0},{3,7},{4,6},{5,1},{6,4},{7,3},{8,10},{9,13},{10,... | collective-permute-start | bytes 442376 | tf_op jit(solution)/shard_map/ppermute | solution.py:417
  21.4 7.2 %collective-permute-start.5 = (bf16[144,1152]{1,0:T(8,128)(2,1)S(1)}, bf16[144,1152]{1,0:T(8,128)(2,1)S(1)}, u32[]{:S(2)}, u32[]{:S(2)}) collective-permute-start(bf16[144,1152]{1,0:T(8,128)(2,1)S(1)} %shard_map.52), channel_id=1, source_target_pairs={{0,4},{1,3},{2,6},{3,1},{4,0},{5,7},{6,2},{7,5},{8,12},{9,11},{10,... | collective-permute-start | bytes 995336 | tf_op jit(solution)/shard_map/ppermute | solution.py:417
  23.0 8.8 %collective-permute-start.7 = (bf16[128,1152]{1,0:T(8,128)(2,1)S(1)}, bf16[128,1152]{1,0:T(8,128)(2,1)S(1)}, u32[]{:S(2)}, u32[]{:S(2)}) collective-permute-start(bf16[128,1152]{1,0:T(8,128)(2,1)S(1)} %shard_map.54), channel_id=1, source_target_pairs={{0,8},{1,9},{2,10},{3,11},{4,12},{5,13},{6,14},{7,15},{8,0},{9,1},... | collective-permute-start | bytes 884744 | tf_op jit(solution)/shard_map/ppermute | solution.py:417
  26.0 7.1 %collective-permute-start.10 = (bf16[128,1152]{1,0:T(8,128)(2,1)S(1)}, bf16[128,1152]{1,0:T(8,128)(2,1)S(1)}, u32[]{:S(2)}, u32[]{:S(2)}) collective-permute-start(bf16[128,1152]{1,0:T(8,128)(2,1)S(1)} %shard_map.58), channel_id=1, source_target_pairs={{0,4},{1,3},{2,6},{3,1},{4,0},{5,7},{6,2},{7,5},{8,12},{9,11},{10,... | collective-permute-start | bytes 884744 | tf_op jit(solution)/shard_map/ppermute | solution.py:417
  30.2 1.6 %collective-permute-start.8 = (f32[8,128]{1,0:T(8,128)S(1)}, f32[8,128]{1,0:T(8,128)S(1)}, u32[]{:S(2)}, u32[]{:S(2)}) collective-permute-start(f32[8,128]{1,0:T(8,128)S(1)} %get-tuple-element.26.level), channel_id=1, source_target_pairs={{0,1},{1,0},{2,3},{3,2},{4,5},{5,4},{6,7},{7,6},{8,9},{9,8},{10,11... | collective-permute-start | bytes 12296 | tf_op jit(solution)/shard_map/ppermute | solution.py:417
  33.2 3.2 %collective-permute-start.12 = (bf16[512,1152]{1,0:T(8,128)(2,1)S(1)}, bf16[512,1152]{1,0:T(8,128)(2,1)S(1)}, u32[]{:S(2)}, u32[]{:S(2)}) collective-permute-start(bf16[512,1152]{1,0:T(8,128)(2,1)S(1)} %shard_map.61), channel_id=1, source_target_pairs={{0,1},{1,0},{2,3},{3,2},{4,5},{5,4},{6,7},{7,6},{8,9},{9,8},{10,11... | collective-permute-start | bytes 3538952 | tf_op jit(solution)/shard_map/ppermute | solution.py:417
  34.8 1.6 %collective-permute-start.11 = (f32[40,1024]{1,0:T(8,128)S(1)}, f32[40,1024]{1,0:T(8,128)S(1)}, u32[]{:S(2)}, u32[]{:S(2)}) collective-permute-start(f32[40,1024]{1,0:T(8,128)S(1)} %get-tuple-element.30), channel_id=1, source_target_pairs={{0,1},{1,0},{2,3},{3,2},{4,5},{5,4},{6,7},{7,6},{8,9},{9,8},{10,11... | collective-permute-start | bytes 491528 | tf_op jit(solution)/shard_map/ppermute | solution.py:417

commit v9 on v8

--- a/solution.py
+++ b/solution.py
@@ -230,8 +230,10 @@
     theirs = jnp.where(
         core == 0, fa[half : half + 16, 0:128], fb[2 * half : 2 * half + 16, 0:128]
     ).astype(jnp.float32)[0:1, 0:1]
-    row = lax.broadcasted_iota(jnp.int32, level.shape, 0)
-    level[...] = jnp.where(row == 0, level_index[0].astype(jnp.float32), theirs)
+    share = level.shape[0] - 8
+    level[0:share, :] = strip[spot(1 - core, share), 0 : level.shape[1]]
+    row = lax.broadcasted_iota(jnp.int32, (8, level.shape[1]), 0)
+    level[share:, :] = jnp.where(row == 0, level_index[0].astype(jnp.float32), theirs)
 
 
 def third_kernel(codes, early, before, part_strip, late, _, stats, strip, wide, square):
@@ -240,7 +242,7 @@
     stats[1 + CODES :, :] = jnp.zeros((stats.shape[0] - 1 - CODES, stats.shape[1]), jnp.float32)
 
 
-def last_kernel(codes, early, middle, before, part_strip, late, keep, send, strip, wide, square):
+def last_kernel(codes, early, middle, before, part_strip, late, keep, mail, strip, wide, square, send):
     _, x, core = position()
     block = late.shape[0]
     half = block // 4
@@ -254,11 +256,17 @@
     left, right = swapped(send, block)
     send[:, -3 * block : -2 * block] = left
     send[:, -block:] = right
+    mail[0:half, :] = send[0:half, -3 * block :]
+    mail[half:, :] = jnp.zeros((24, 3 * block), jnp.float32)
+    for band, (low, high) in enumerate(((0, 3), (3, 6), (6, 8))):
+        mail[half + 8 * band : half + 8 * band + 8, 0 : (high - low) * block] = send[
+            half:, low * block : high * block
+        ]
 
 
 def counted(*levels):
     row = lax.broadcasted_iota(jnp.int32, (8, 1), 0).astype(jnp.float32) - 1.0
-    found = [ref[i : i + 1, 0:1] for ref in levels for i in (0, 1)]
+    found = [ref[ref.shape[0] - 8 + i : ref.shape[0] - 7 + i, 0:1] for ref in levels for i in (0, 1)]
     return sum(jnp.where(row == level, 1.0, 0.0) for level in found)
 
 
@@ -318,9 +326,16 @@
 
 
 def mix_kernel(
-    codes, keep, recv, level, their_level, by_row, both, lse, early, middle, late, sooner, later,
-    out, loss, turned, mix
+    codes, keep, mail, level, their_level, by_row, both, lse, early, middle, late, sooner, later,
+    out, loss, turned, mix, recv
 ):
+    share, block = out.shape[0], 4 * out.shape[0]
+    recv[0:share, 0 : 5 * block] = their_level[0:share, :]
+    recv[0:share, 5 * block :] = mail[0:share, :]
+    for band, (low, high) in enumerate(((0, 3), (3, 6), (6, 8))):
+        recv[share:, low * block : high * block] = mail[
+            share + 8 * band : share + 8 * band + 8, 0 : (high - low) * block
+        ]
     half = Half(0, out.shape[1], codes, recv, counted(level, their_level), turned)
     student = position()[2] == 1
     sign = jnp.where(student, 1.0, -1.0)
@@ -493,7 +508,7 @@
             shape(8, head),
             shape(rows, head),
             shape(head, width, dtype=jnp.bfloat16),
-            shape(8, 128),
+            shape(half + 8, 5 * block),
         ],
         room(head - some, head),
         16,
@@ -524,8 +539,10 @@
     )
     keep, mail = call(
         last_kernel,
-        [shape(half + 8, total), shape(half + 8, total)],
-        [pltpu.VMEM((rows, total), jnp.float32)] + room(block, total),
+        [shape(half + 8, total), shape(half + 24, 3 * block)],
+        [pltpu.VMEM((rows, total), jnp.float32)]
+        + room(block, total)
+        + [pltpu.VMEM((half + 8, total), jnp.float32)],
         16,
         codes,
         b_rows,
@@ -548,7 +565,7 @@
     out, loss = call(
         mix_kernel,
         out_shapes,
-        [pltpu.VMEM((2, block, 8), jnp.float32), pltpu.VMEM((half, total), jnp.bfloat16)],
+        [pltpu.VMEM((2, block, 8), jnp.float32), pltpu.VMEM((half, total), jnp.bfloat16), pltpu.VMEM((half + 8, total), jnp.float32)],
         16,
         codes,
         keep,

time: 38.4 us -> 38.3 us (level)
  no operation moved by 1% of the time
where the time goes in v9:
time: 38.3 us; the launch traced here: 38.1 us
  starting transfers between devices  17.1 us (45%)
  waiting for transfers between devices  9.9 us (26%)
  Pallas kernels  8.37 us (22%)
  between operations  1.48 us (4%)
  local copies, waits for them, and re-layouts  1.18 us (3%)
    ppermute x13, starting transfers between devices, send(): return lax.ppermute(a, ALL, pairs)  17.1 us
    ppermute x13, waiting for transfers between devices, send(): return lax.ppermute(a, ALL, pairs)  9.9 us
    pallas_call x13, Pallas kernels, call(): pl.pallas_call(kernel, out_shape=shapes, in_specs=[SMEM if a.shape == (1,...  8.37 us
    unnamed x4, local copies, waits for them, and re-layouts  1.04 us
  transfers between devices with their start and end apart: 13, of which 6 were waited for; matrix products, arithmetic and copies ran while one was open for 0% of the time, Pallas kernels for 17%

profile of v9, /device:TPU:0, one launch (start us, length us, event | category | flops | bytes accessed | tf_op | source)
XLA Modules:
  0.0 38.1 jit_solution(15783198251049159296)
XLA Ops:
  0.6 0.0 copy-start
  0.7 1.0 %copy-done = bf16[2,128,1152]{2,1,0:T(8,128)(2,1)S(1)} copy-done((bf16[2,128,1152]{2,1,0:T(8,128)(2,1)S(1)}, bf16[2,128,1152]{2,1,0:T(8,128)(2,1)}, u32[]{:S(2)}) %copy-start) | copy-done | bytes 589848
  1.7 4.1 %collective-permute-start.2 = (bf16[64,1152]{1,0:T(8,128)(2,1)S(1)}, bf16[64,1152]{1,0:T(8,128)(2,1)S(1)}, u32[]{:S(2)}, u32[]{:S(2)}) collective-permute-start(bf16[64,1152]{1,0:T(8,128)(2,1)S(1)} %dynamic-slice_bitcast_fusion.1), channel_id=1, source_target_pairs={{0,16},{1,17},{2,18},{3,19},{4,20},{5,21},{6,22},{7,23},{8,24},{9,... | collective-permute-start | bytes 442376 | tf_op jit(solution)/shard_map/ppermute | solution.py:432
  5.9 1.6 %collective-permute-start = (bf16[128,1152]{1,0:T(8,128)(2,1)S(1)}, bf16[128,1152]{1,0:T(8,128)(2,1)S(1)}, u32[]{:S(2)}, u32[]{:S(2)}) collective-permute-start(bf16[128,1152]{1,0:T(8,128)(2,1)S(1)} %dynamic-slice_bitcast_fusion.refs_0_), channel_id=1, source_target_pairs={{0,8},{1,9},{2,10},{3,11},{4,12},{5,13},{6,14},{7,15},{8,0},{9,1},... | collective-permute-start | bytes 884744 | tf_op jit(solution)/shard_map/ppermute | solution.py:432
  7.5 1.5 %collective-permute-start.1 = (bf16[128,1152]{1,0:T(8,128)(2,1)S(1)}, bf16[128,1152]{1,0:T(8,128)(2,1)S(1)}, u32[]{:S(2)}, u32[]{:S(2)}) collective-permute-start(bf16[128,1152]{1,0:T(8,128)(2,1)S(1)} %dynamic-slice_bitcast_fusion.refs_0_), channel_id=1, source_target_pairs={{0,4},{1,5},{2,6},{3,7},{4,0},{5,1},{6,2},{7,3},{8,12},{9,13},{10,... | collective-permute-start | bytes 884744 | tf_op jit(solution)/shard_map/ppermute | solution.py:432
  9.7 3.3 %collective-permute-done.2.refs_3_.refs_0_.refs_2_ = bf16[64,1152]{1,0:T(8,128)(2,1)S(1)} collective-permute-done((bf16[64,1152]{1,0:T(8,128)(2,1)S(1)}, bf16[64,1152]{1,0:T(8,128)(2,1)S(1)}, u32[]{:S(2)}, u32[]{:S(2)}) %collective-permute-start.2) | collective-permute-done | bytes 147488 | tf_op jit(solution)/shard_map/ppermute | solution.py:432
  13.0 1.6 %collective-permute-start.4 = (bf16[80,1152]{1,0:T(8,128)(2,1)S(1)}, bf16[80,1152]{1,0:T(8,128)(2,1)S(1)}, u32[]{:S(2)}, u32[]{:S(2)}) collective-permute-start(bf16[80,1152]{1,0:T(8,128)(2,1)S(1)} %shard_map.51), channel_id=1, source_target_pairs={{0,2},{1,5},{2,0},{3,7},{4,6},{5,1},{6,4},{7,3},{8,10},{9,13},{10,... | collective-permute-start | bytes 552968 | tf_op jit(solution)/shard_map/ppermute | solution.py:432
  14.6 0.6 %collective-permute-start.3 = (bf16[64,1152]{1,0:T(8,128)(2,1)S(1)}, bf16[64,1152]{1,0:T(8,128)(2,1)S(1)}, u32[]{:S(2)}, u32[]{:S(2)}) collective-permute-start(bf16[64,1152]{1,0:T(8,128)(2,1)S(1)} %collective-permute-done.2.refs_3_.refs_0_.refs_2_), channel_id=1, source_target_pairs={{0,8},{1,9},{2,10},{3,11},{4,12},{5,13},{6,14},{7,15},{8,0},{9,1},... | collective-permute-start | bytes 442376 | tf_op jit(solution)/shard_map/ppermute | solution.py:432
  15.2 1.7 %collective-permute-done.refs_1_ = bf16[128,1152]{1,0:T(8,128)(2,1)S(1)} collective-permute-done((bf16[128,1152]{1,0:T(8,128)(2,1)S(1)}, bf16[128,1152]{1,0:T(8,128)(2,1)S(1)}, u32[]{:S(2)}, u32[]{:S(2)}) %collective-permute-start) | collective-permute-done | bytes 294944 | tf_op jit(solution)/shard_map/ppermute | solution.py:432
  17.0 0.0 collective-permute-done.1.refs_2_.refs_0_.refs_1_
  17.0 2.8 %collective-permute-done.3.refs_4_.refs_3_.refs_1_.refs_0_ = bf16[64,1152]{1,0:T(8,128)(2,1)S(1)} collective-permute-done((bf16[64,1152]{1,0:T(8,128)(2,1)S(1)}, bf16[64,1152]{1,0:T(8,128)(2,1)S(1)}, u32[]{:S(2)}, u32[]{:S(2)}) %collective-permute-start.3) | collective-permute-done | bytes 147488 | tf_op jit(solution)/shard_map/ppermute | solution.py:432
  19.7 0.0 collective-permute-done.4.fa.refs_4_
  19.7 0.1 shard_map.57
  19.8 0.0 copy-start.1
  19.8 0.1 collective-permute-start.9
  19.9 1.4 %collective-permute-start.6 = (bf16[64,1152]{1,0:T(8,128)(2,1)S(1)}, bf16[64,1152]{1,0:T(8,128)(2,1)S(1)}, u32[]{:S(2)}, u32[]{:S(2)}) collective-permute-start(bf16[64,1152]{1,0:T(8,128)(2,1)S(1)} %collective-permute-done.3.refs_4_.refs_3_.refs_1_.refs_0_), channel_id=1, source_target_pairs={{0,2},{1,5},{2,0},{3,7},{4,6},{5,1},{6,4},{7,3},{8,10},{9,13},{10,... | collective-permute-start | bytes 442376 | tf_op jit(solution)/shard_map/ppermute | solution.py:432
  21.4 1.6 %collective-permute-start.5 = (bf16[144,1152]{1,0:T(8,128)(2,1)S(1)}, bf16[144,1152]{1,0:T(8,128)(2,1)S(1)}, u32[]{:S(2)}, u32[]{:S(2)}) collective-permute-start(bf16[144,1152]{1,0:T(8,128)(2,1)S(1)} %shard_map.52), channel_id=1, source_target_pairs={{0,4},{1,3},{2,6},{3,1},{4,0},{5,7},{6,2},{7,5},{8,12},{9,11},{10,... | collective-permute-start | bytes 995336 | tf_op jit(solution)/shard_map/ppermute | solution.py:432
  23.0 1.4 %collective-permute-start.7 = (bf16[128,1152]{1,0:T(8,128)(2,1)S(1)}, bf16[128,1152]{1,0:T(8,128)(2,1)S(1)}, u32[]{:S(2)}, u32[]{:S(2)}) collective-permute-start(bf16[128,1152]{1,0:T(8,128)(2,1)S(1)} %shard_map.54), channel_id=1, source_target_pairs={{0,8},{1,9},{2,10},{3,11},{4,12},{5,13},{6,14},{7,15},{8,0},{9,1},... | collective-permute-start | bytes 884744 | tf_op jit(solution)/shard_map/ppermute | solution.py:432
  24.4 0.0 copy-done.1
  24.4 1.5 %shard_map.50 = (s32[1,1024]{1,0:T(1,128)S(1)}, f32[8,512]{1,0:T(8,128)S(1)}, f32[64,512]{1,0:T(8,128)S(1)}, bf16[512,1152]{1,0:T(8,128)(2,1)S(1)}) custom-call(s32[1,1024]{1,0:T(1,128)S(1)} %bitcast.7, bf16[128,1152]{1,0:T(8,128)(2,1)S(1)} %dynamic-slice_bitcast_fusion.refs_0_, bf16[128,1152]{1,0:T(8,128)(2,1)S(1)} %collective-permute-done.refs_1_, ...), custom_call_target="tpu_custom_call" | custom-call | tf_op jit(solution)/shard_map/pallas_call | solution.py:389
  25.9 0.0 collective-permute-done.6.ga.refs_1_.refs_3_
  26.0 0.0 collective-permute-done.9.refs_2_.sooner
  26.0 2.3 %collective-permute-start.10 = (bf16[128,1152]{1,0:T(8,128)(2,1)S(1)}, bf16[128,1152]{1,0:T(8,128)(2,1)S(1)}, u32[]{:S(2)}, u32[]{:S(2)}) collective-permute-start(bf16[128,1152]{1,0:T(8,128)(2,1)S(1)} %shard_map.58), channel_id=1, source_target_pairs={{0,4},{1,3},{2,6},{3,1},{4,0},{5,7},{6,2},{7,5},{8,12},{9,11},{10,... | collective-permute-start | bytes 884744 | tf_op jit(solution)/shard_map/ppermute | solution.py:432
  28.3 0.3 collective-permute-done.5.fb
  28.6 1.6 %shard_map.53 = (f32[8,768]{1,0:T(8,128)S(1)}, f32[64,768]{1,0:T(8,128)S(1)}, bf16[768,1152]{1,0:T(8,128)(2,1)S(1)}, f32[40,640]{1,0:T(8,128)S(1)}) custom-call(s32[1,1024]{1,0:T(1,128)S(1)} %get-tuple-element.19.codes, bf16[512,1152]{1,0:T(8,128)(2,1)S(1)} %get-tuple-element.20.early, f32[8,512]{1,0:T(8,128)S(1)} %get-tuple-element.21.before.refs_3_, ...), custom_call_target="tpu_custom_call" | custom-call | tf_op jit(solution)/shard_map/pallas_call | solution.py:389
  30.2 0.3 collective-permute-start.8
  30.5 1.3 %collective-permute-done.7.late.middle.refs_2_ = bf16[128,1152]{1,0:T(8,128)(2,1)S(1)} collective-permute-done((bf16[128,1152]{1,0:T(8,128)(2,1)S(1)}, bf16[128,1152]{1,0:T(8,128)(2,1)S(1)}, u32[]{:S(2)}, u32[]{:S(2)}) %collective-permute-start.7) | collective-permute-done | bytes 294944 | tf_op jit(solution)/shard_map/ppermute | solution.py:432
  31.9 0.0 collective-permute-done.8._.their_level
  31.9 1.2 %shard_map.55 = (f32[8,896]{1,0:T(8,128)S(1)}, f32[64,896]{1,0:T(8,128)S(1)}) custom-call(s32[1,1024]{1,0:T(1,128)S(1)} %get-tuple-element.19.codes, bf16[768,1152]{1,0:T(8,128)(2,1)S(1)} %get-tuple-element.23.early, f32[8,768]{1,0:T(8,128)S(1)} %get-tuple-element.24.before, f32[64,768]{1,0:T(8,128)S(1)} %get-tuple-element.25.part_strip, ...), custom_call_target="tpu_custom_call" | custom-call | tf_op jit(solution)/shard_map/pallas_call | solution.py:389
  33.1 0.0 collective-permute-done.10.late
  33.1 0.1 shard_map.61
  33.2 0.1 collective-permute-start.12
  33.3 1.6 %shard_map.59 = (f32[40,1024]{1,0:T(8,128)S(1)}, f32[56,384]{1,0:T(8,128)S(1)}) custom-call(s32[1,1024]{1,0:T(1,128)S(1)} %get-tuple-element.19.codes, bf16[768,1152]{1,0:T(8,128)(2,1)S(1)} %get-tuple-element.23.early, bf16[128,1152]{1,0:T(8,128)(2,1)S(1)} %collective-permute-done.7.late.middle.refs_2_, f32[8,896]{1,0:T(8,128)S(1)} %get-tuple-element.27.before.refs_5_, ...), custom_call_target="tpu_custom_call" | custom-call | tf_op jit(solution)/shard_map/pallas_call | solution.py:389
  34.8 0.5 %collective-permute-start.11 = (f32[56,384]{1,0:T(8,128)S(1)}, f32[56,384]{1,0:T(8,128)S(1)}, u32[]{:S(2)}, u32[]{:S(2)}) collective-permute-start(f32[56,384]{1,0:T(8,128)S(1)} %get-tuple-element.30), channel_id=1, source_target_pairs={{0,1},{1,0},{2,3},{3,2},{4,5},{5,4},{6,7},{7,6},{8,9},{9,8},{10,11... | collective-permute-start | bytes 258056 | tf_op jit(solution)/shard_map/ppermute | solution.py:432
  35.3 0.4 %shard_map.60 = (f32[32,1024]{1,0:T(8,128)S(1)}, f32[32,1024]{1,0:T(8,128)S(1)}, f32[32,8]{1,0:T(8,128)S(1)}) custom-call(s32[1,1024]{1,0:T(1,128)S(1)} %get-tuple-element.19.codes, f32[40,1024]{1,0:T(8,128)S(1)} %get-tuple-element.29.keep, f32[40,640]{1,0:T(8,128)S(1)} %get-tuple-element.26.level, f32[40,640]{1,0:T(8,128)S(1)} %collective-permute-done.8._.their_level), custom_call_target="tpu_custom_call" | custom-call | tf_op jit(solution)/shard_map/pallas_call | solution.py:389
  35.8 0.5 %collective-permute-done.11.mail = f32[56,384]{1,0:T(8,128)S(1)} collective-permute-done((f32[56,384]{1,0:T(8,128)S(1)}, f32[56,384]{1,0:T(8,128)S(1)}, u32[]{:S(2)}, u32[]{:S(2)}) %collective-permute-start.11) | collective-permute-done | bytes 86048 | tf_op jit(solution)/shard_map/ppermute | solution.py:432
  36.3 0.0 collective-permute-done.12.later
  36.3 1.8 %shard_map.62 = (f32[32,1152]{1,0:T(8,128)}, f32[1,32]{1,0:T(1,128)}) custom-call(s32[1,1024]{1,0:T(1,128)S(1)} %get-tuple-element.19.codes, f32[40,1024]{1,0:T(8,128)S(1)} %get-tuple-element.29.keep, f32[56,384]{1,0:T(8,128)S(1)} %collective-permute-done.11.mail, f32[40,640]{1,0:T(8,128)S(1)} %get-tuple-element.26.level, ...), custom_call_target="tpu_custom_call" | custom-call | tf_op jit(solution)/shard_map/pallas_call | solution.py:389
  (11 shorter events, 0.3 us)
Async XLA Ops:
  0.6 1.1 %copy-start = (bf16[2,128,1152]{2,1,0:T(8,128)(2,1)S(1)}, bf16[2,128,1152]{2,1,0:T(8,128)(2,1)}, u32[]{:S(2)}) copy-start(bf16[2,128,1152]{2,1,0:T(8,128)(2,1)} %param.3) | copy-start | bytes 1769476
  1.7 11.2 %collective-permute-start.2 = (bf16[64,1152]{1,0:T(8,128)(2,1)S(1)}, bf16[64,1152]{1,0:T(8,128)(2,1)S(1)}, u32[]{:S(2)}, u32[]{:S(2)}) collective-permute-start(bf16[64,1152]{1,0:T(8,128)(2,1)S(1)} %dynamic-slice_bitcast_fusion.1), channel_id=1, source_target_pairs={{0,16},{1,17},{2,18},{3,19},{4,20},{5,21},{6,22},{7,23},{8,24},{9,... | collective-permute-start | bytes 442376 | tf_op jit(solution)/shard_map/ppermute | solution.py:432
  5.9 11.0 %collective-permute-start = (bf16[128,1152]{1,0:T(8,128)(2,1)S(1)}, bf16[128,1152]{1,0:T(8,128)(2,1)S(1)}, u32[]{:S(2)}, u32[]{:S(2)}) collective-permute-start(bf16[128,1152]{1,0:T(8,128)(2,1)S(1)} %dynamic-slice_bitcast_fusion.refs_0_), channel_id=1, source_target_pairs={{0,8},{1,9},{2,10},{3,11},{4,12},{5,13},{6,14},{7,15},{8,0},{9,1},... | collective-permute-start | bytes 884744 | tf_op jit(solution)/shard_map/ppermute | solution.py:432
  7.5 9.5 %collective-permute-start.1 = (bf16[128,1152]{1,0:T(8,128)(2,1)S(1)}, bf16[128,1152]{1,0:T(8,128)(2,1)S(1)}, u32[]{:S(2)}, u32[]{:S(2)}) collective-permute-start(bf16[128,1152]{1,0:T(8,128)(2,1)S(1)} %dynamic-slice_bitcast_fusion.refs_0_), channel_id=1, source_target_pairs={{0,4},{1,5},{2,6},{3,7},{4,0},{5,1},{6,2},{7,3},{8,12},{9,13},{10,... | collective-permute-start | bytes 884744 | tf_op jit(solution)/shard_map/ppermute | solution.py:432
  13.0 6.8 %collective-permute-start.4 = (bf16[80,1152]{1,0:T(8,128)(2,1)S(1)}, bf16[80,1152]{1,0:T(8,128)(2,1)S(1)}, u32[]{:S(2)}, u32[]{:S(2)}) collective-permute-start(bf16[80,1152]{1,0:T(8,128)(2,1)S(1)} %shard_map.51), channel_id=1, source_target_pairs={{0,2},{1,5},{2,0},{3,7},{4,6},{5,1},{6,4},{7,3},{8,10},{9,13},{10,... | collective-permute-start | bytes 552968 | tf_op jit(solution)/shard_map/ppermute | solution.py:432
  14.6 5.1 %collective-permute-start.3 = (bf16[64,1152]{1,0:T(8,128)(2,1)S(1)}, bf16[64,1152]{1,0:T(8,128)(2,1)S(1)}, u32[]{:S(2)}, u32[]{:S(2)}) collective-permute-start(bf16[64,1152]{1,0:T(8,128)(2,1)S(1)} %collective-permute-done.2.refs_3_.refs_0_.refs_2_), channel_id=1, source_target_pairs={{0,8},{1,9},{2,10},{3,11},{4,12},{5,13},{6,14},{7,15},{8,0},{9,1},... | collective-permute-start | bytes 442376 | tf_op jit(solution)/shard_map/ppermute | solution.py:432
  19.8 4.6 %copy-start.1 = (s32[1024]{0:T(1024)S(1)}, s32[1024]{0:T(1024)}, u32[]{:S(2)}) copy-start(s32[1024]{0:T(1024)} %param.4) | copy-start | bytes 12292
  19.8 6.1 %collective-permute-start.9 = (bf16[512,1152]{1,0:T(8,128)(2,1)S(1)}, bf16[512,1152]{1,0:T(8,128)(2,1)S(1)}, u32[]{:S(2)}, u32[]{:S(2)}) collective-permute-start(bf16[512,1152]{1,0:T(8,128)(2,1)S(1)} %shard_map.57), channel_id=1, source_target_pairs={{0,1},{1,0},{2,3},{3,2},{4,5},{5,4},{6,7},{7,6},{8,9},{9,8},{10,11... | collective-permute-start | bytes 3538952 | tf_op jit(solution)/shard_map/ppermute | solution.py:432
  19.9 6.0 %collective-permute-start.6 = (bf16[64,1152]{1,0:T(8,128)(2,1)S(1)}, bf16[64,1152]{1,0:T(8,128)(2,1)S(1)}, u32[]{:S(2)}, u32[]{:S(2)}) collective-permute-start(bf16[64,1152]{1,0:T(8,128)(2,1)S(1)} %collective-permute-done.3.refs_4_.refs_3_.refs_1_.refs_0_), channel_id=1, source_target_pairs={{0,2},{1,5},{2,0},{3,7},{4,6},{5,1},{6,4},{7,3},{8,10},{9,13},{10,... | collective-permute-start | bytes 442376 | tf_op jit(solution)/shard_map/ppermute | solution.py:432
  21.4 7.2 %collective-permute-start.5 = (bf16[144,1152]{1,0:T(8,128)(2,1)S(1)}, bf16[144,1152]{1,0:T(8,128)(2,1)S(1)}, u32[]{:S(2)}, u32[]{:S(2)}) collective-permute-start(bf16[144,1152]{1,0:T(8,128)(2,1)S(1)} %shard_map.52), channel_id=1, source_target_pairs={{0,4},{1,3},{2,6},{3,1},{4,0},{5,7},{6,2},{7,5},{8,12},{9,11},{10,... | collective-permute-start | bytes 995336 | tf_op jit(solution)/shard_map/ppermute | solution.py:432
  23.0 8.8 %collective-permute-start.7 = (bf16[128,1152]{1,0:T(8,128)(2,1)S(1)}, bf16[128,1152]{1,0:T(8,128)(2,1)S(1)}, u32[]{:S(2)}, u32[]{:S(2)}) collective-permute-start(bf16[128,1152]{1,0:T(8,128)(2,1)S(1)} %shard_map.54), channel_id=1, source_target_pairs={{0,8},{1,9},{2,10},{3,11},{4,12},{5,13},{6,14},{7,15},{8,0},{9,1},... | collective-permute-start | bytes 884744 | tf_op jit(solution)/shard_map/ppermute | solution.py:432
  26.0 7.1 %collective-permute-start.10 = (bf16[128,1152]{1,0:T(8,128)(2,1)S(1)}, bf16[128,1152]{1,0:T(8,128)(2,1)S(1)}, u32[]{:S(2)}, u32[]{:S(2)}) collective-permute-start(bf16[128,1152]{1,0:T(8,128)(2,1)S(1)} %shard_map.58), channel_id=1, source_target_pairs={{0,4},{1,3},{2,6},{3,1},{4,0},{5,7},{6,2},{7,5},{8,12},{9,11},{10,... | collective-permute-start | bytes 884744 | tf_op jit(solution)/shard_map/ppermute | solution.py:432
  30.2 1.7 %collective-permute-start.8 = (f32[40,640]{1,0:T(8,128)S(1)}, f32[40,640]{1,0:T(8,128)S(1)}, u32[]{:S(2)}, u32[]{:S(2)}) collective-permute-start(f32[40,640]{1,0:T(8,128)S(1)} %get-tuple-element.26.level), channel_id=1, source_target_pairs={{0,1},{1,0},{2,3},{3,2},{4,5},{5,4},{6,7},{7,6},{8,9},{9,8},{10,11... | collective-permute-start | bytes 307208 | tf_op jit(solution)/shard_map/ppermute | solution.py:432
  33.2 3.1 %collective-permute-start.12 = (bf16[512,1152]{1,0:T(8,128)(2,1)S(1)}, bf16[512,1152]{1,0:T(8,128)(2,1)S(1)}, u32[]{:S(2)}, u32[]{:S(2)}) collective-permute-start(bf16[512,1152]{1,0:T(8,128)(2,1)S(1)} %shard_map.61), channel_id=1, source_target_pairs={{0,1},{1,0},{2,3},{3,2},{4,5},{5,4},{6,7},{7,6},{8,9},{9,8},{10,11... | collective-permute-start | bytes 3538952 | tf_op jit(solution)/shard_map/ppermute | solution.py:432
  34.8 1.4 %collective-permute-start.11 = (f32[56,384]{1,0:T(8,128)S(1)}, f32[56,384]{1,0:T(8,128)S(1)}, u32[]{:S(2)}, u32[]{:S(2)}) collective-permute-start(f32[56,384]{1,0:T(8,128)S(1)} %get-tuple-element.30), channel_id=1, source_target_pairs={{0,1},{1,0},{2,3},{3,2},{4,5},{5,4},{6,7},{7,6},{8,9},{9,8},{10,11... | collective-permute-start | bytes 258056 | tf_op jit(solution)/shard_map/ppermute | solution.py:432
